TPU v7x, 32 devices: a whole 2x2x4 slice. The times are simulated.
32 devices in a mesh: fsdp: 2 (over y), context: 4 (over x, core), tensor: 4 (over z).
Axes of the slice: x: 2, y: 2, z: 4, core: 2. Of those that a mesh axis runs over, the one named last changes fastest.
Arguments:
- tokens: bfloat16 [4, 2048, 2048], P('fsdp', 'context'), may hold values from -6 to 6
- ln_gain: bfloat16 [2048], P('fsdp'), may hold values from 0.5 to 1.5
- ln_bias: bfloat16 [2048], P('fsdp'), may hold values from -1.796875 to 1.796875
- w_qkv: bfloat16 [3, 2048, 2048], P(None, 'fsdp', 'tensor'), may hold values from -0.1875 to 0.1875
- b_qkv: bfloat16 [3, 2048], P(None, ('tensor', 'fsdp')), may hold values from -3 to 3
- w_out: bfloat16 [2048, 2048], P('tensor', 'fsdp'), may hold values from -0.5 to 0.5
- b_out: bfloat16 [2048], P('fsdp'), may hold values from -1.796875 to 1.796875
- w_fc1: bfloat16 [2048, 8192], P('fsdp', 'tensor'), may hold values from -0.125 to 0.125
- b_fc1: bfloat16 [8192], P(('tensor', 'fsdp')), may hold values from -3 to 3
- w_fc2: bfloat16 [8192, 2048], P('tensor', 'fsdp'), may hold values from -0.09375 to 0.09375
- b_fc2: bfloat16 [2048], P('fsdp'), may hold values from -1.796875 to 1.796875
- cotangent: bfloat16 [4, 2048, 2048], P('fsdp', 'context'), may hold values from -6 to 6
Outputs:
- block_out: bfloat16 [4, 2048, 2048], P('fsdp', 'context')
- tokens_grad: bfloat16 [4, 2048, 2048], P('fsdp', 'context')
- ln_gain_grad: float32 [2048], P('fsdp')
- ln_bias_grad: float32 [2048], P('fsdp')
- w_qkv_grad: float32 [3, 2048, 2048], P(None, 'fsdp', 'tensor')
- b_qkv_grad: float32 [3, 2048], P(None, ('tensor', 'fsdp'))
- w_out_grad: float32 [2048, 2048], P('tensor', 'fsdp')
- b_out_grad: float32 [2048], P('fsdp')
- w_fc1_grad: float32 [2048, 8192], P('fsdp', 'tensor')
- b_fc1_grad: float32 [8192], P(('tensor', 'fsdp'))
- w_fc2_grad: float32 [8192, 2048], P('tensor', 'fsdp')
- b_fc2_grad: float32 [2048], P('fsdp')
All inputs are finite; a program needn't handle non-finite values.
Results may differ from a plain program's by a relative error of at most 0.012.
The roundings to bfloat16 on the way count: a program that leaves them out, or rounds other values in their place, can miss the bound.
Values may be sent and summed in bfloat16 or wider, within the bound.
No kernel may reach another device: no remote copies, remote signals or barrier semaphores. Data moves between devices by JAX's collectives and lax.ppermute only.
A program may use at most 256 MiB of HBM per device.

v0:
```python
from functools import partial

import jax
import jax.numpy as jnp
from jax import lax
from jax.sharding import PartitionSpec as P

HD = 64
ROT = 32


EPSILON = 1e-05


def layer_norm(values, norm_gain, norm_bias):
    centered = values - jnp.mean(values, -1, keepdims=True)
    variance = jnp.mean(centered * centered, -1, keepdims=True)
    return centered * lax.rsqrt(variance + EPSILON) * norm_gain + norm_bias


def outer_sum(left, right):
    return lax.dot_general(
        left, right, (((0,), (0,)), ((), ())), preferred_element_type=jnp.float32
    )


def inner_sum(left, right):
    return lax.dot_general(
        left, right, (((1,), (1,)), ((), ())), preferred_element_type=jnp.float32
    )


def causal_scores(query_block, key, start):
    block_rows = query_block.shape[0]
    length = key.shape[0]
    scores = jnp.einsum("qh,kh->qk", query_block, key, preferred_element_type=jnp.float32) * HD ** (
        -0.5
    )
    rows_at = start + lax.iota(jnp.int32, block_rows)
    allowed = lax.iota(jnp.int32, length)[None, :] <= rows_at[:, None]
    return jnp.where(allowed, scores, -1e30)


def attend_pair(stacked):
    query, key, value = stacked
    length = query.shape[0]
    block_rows = min(512, length)
    block_count = length // block_rows

    def attend_one_block(items):
        block_index, query_block = items
        scores = causal_scores(query_block, key, block_index * block_rows)
        highest = jnp.max(scores, -1, keepdims=True)
        weights = jnp.exp(scores - highest)
        total = jnp.sum(weights, -1, keepdims=True)
        probs_low = (weights / total).astype(jnp.bfloat16)
        output = jnp.einsum("qk,kh->qh", probs_low, value, preferred_element_type=jnp.float32)
        return (output, (highest + jnp.log(total))[:, 0])

    outputs, log_totals = lax.map(
        attend_one_block,
        (jnp.arange(block_count, dtype=jnp.int32), query.reshape(block_count, block_rows, HD)),
    )
    return (outputs.reshape(length, HD), log_totals.reshape(length))


def pair_back(stacked):
    query, key, value, out_grad, log_total = stacked
    length = query.shape[0]
    block_rows = min(512, length)
    block_count = length // block_rows
    scale = HD ** (-0.5)

    def pair_one_block(carry, items):
        key_sum, value_sum = carry
        block_index, query_block, grad_block, lse_block = items
        scores = causal_scores(query_block, key, block_index * block_rows)
        probs = jnp.exp(scores - lse_block[:, None])
        prob_grad = jnp.einsum("qh,kh->qk", grad_block, value, preferred_element_type=jnp.float32)
        inner = jnp.sum(probs * prob_grad, -1, keepdims=True)
        score_grad = (probs * (prob_grad - inner)).astype(jnp.bfloat16)
        query_grad = (
            jnp.einsum("qk,kh->qh", score_grad, key, preferred_element_type=jnp.float32) * scale
        )
        key_sum = (
            key_sum
            + jnp.einsum("qk,qh->kh", score_grad, query_block, preferred_element_type=jnp.float32)
            * scale
        )
        value_sum = value_sum + jnp.einsum(
            "qk,qh->kh", probs.astype(jnp.bfloat16), grad_block, preferred_element_type=jnp.float32
        )
        return ((key_sum, value_sum), query_grad)

    zeros = jnp.zeros((length, HD), jnp.float32)
    sums, query_grads = lax.scan(
        pair_one_block,
        (zeros, zeros),
        (
            jnp.arange(block_count, dtype=jnp.int32),
            query.reshape(block_count, block_rows, HD),
            out_grad.reshape(block_count, block_rows, HD),
            log_total.reshape(block_count, block_rows),
        ),
    )
    return jnp.stack([query_grads.reshape(length, HD), sums[0], sums[1]]).astype(jnp.bfloat16)


def rotate(field, cosine, sine):
    half_rot = ROT // 2
    first = field[..., :half_rot]
    second = field[..., half_rot:ROT]
    return jnp.concatenate(
        [first * cosine - second * sine, second * cosine + first * sine, field[..., ROT:]], -1
    )


def per_device(
    tokens, ln_gain, ln_bias, w_qkv, b_qkv, w_out, b_out, w_fc1, b_fc1, w_fc2, b_fc2, cotangent
):
    (
        norm_gain,
        norm_bias,
        qkv_weight,
        qkv_bias,
        out_weight,
        out_bias,
        fc1_weight,
        fc1_bias,
        fc2_weight,
        fc2_bias,
    ) = (
        lax.all_gather(ln_gain, "fsdp", axis=0, tiled=True),
        lax.all_gather(ln_bias, "fsdp", axis=0, tiled=True),
        lax.all_gather(w_qkv, "fsdp", axis=1, tiled=True),
        lax.all_gather(b_qkv, "fsdp", axis=1, tiled=True),
        lax.all_gather(w_out, "fsdp", axis=1, tiled=True),
        lax.all_gather(b_out, "fsdp", axis=0, tiled=True),
        lax.all_gather(w_fc1, "fsdp", axis=0, tiled=True),
        lax.all_gather(b_fc1, "fsdp", axis=0, tiled=True),
        lax.all_gather(w_fc2, "fsdp", axis=1, tiled=True),
        lax.all_gather(b_fc2, "fsdp", axis=0, tiled=True),
    )
    seq_count, row_count, width = tokens.shape
    context_size = lax.axis_size("context")
    local_width = qkv_weight.shape[2]
    heads_local = local_width // HD
    length = row_count * context_size
    pair_count = seq_count * heads_local
    pairs_local = pair_count // context_size
    flat_rows = seq_count * row_count
    inputs = tokens.reshape(flat_rows, width).astype(jnp.float32)
    normed, norm_pull = jax.vjp(
        layer_norm, inputs, norm_gain.astype(jnp.float32), norm_bias.astype(jnp.float32)
    )
    normed_low = normed.astype(jnp.bfloat16)
    raw = jnp.einsum("rd,cde->rce", normed_low, qkv_weight, preferred_element_type=jnp.float32)
    raw = raw + qkv_bias.astype(jnp.float32)[None, :, :]
    heads = raw.reshape(seq_count, row_count, 3, heads_local, HD)
    half_rot = ROT // 2
    positions = (lax.axis_index("context") * row_count + lax.iota(jnp.int32, row_count)).astype(
        jnp.float32
    )
    exponents = lax.iota(jnp.int32, half_rot).astype(jnp.float32) * (2.0 / ROT)
    angles = positions[:, None] * jnp.power(10000.0, -exponents)[None, :]
    cosine = jnp.cos(angles)[None, :, None, None, :]
    sine = jnp.sin(angles)[None, :, None, None, :]
    turned = jnp.concatenate([rotate(heads[:, :, :2], cosine, sine), heads[:, :, 2:]], 2).astype(
        jnp.bfloat16
    )
    outgoing = jnp.transpose(turned, (2, 0, 3, 1, 4)).reshape(3, pair_count, row_count // 2, 2 * HD)
    received = lax.all_to_all(outgoing, "context", split_axis=1, concat_axis=2, tiled=True).reshape(
        3, pairs_local, length, HD
    )
    context, log_totals = lax.map(attend_pair, (received[0], received[1], received[2]))
    context_low = context.astype(jnp.bfloat16).reshape(pairs_local, length // 2, 2 * HD)
    returned = lax.all_to_all(context_low, "context", split_axis=1, concat_axis=0, tiled=True)
    merged = jnp.transpose(returned.reshape(seq_count, heads_local, row_count, HD), (0, 2, 1, 3))
    merged = merged.reshape(flat_rows, local_width)
    attended = jnp.dot(merged, out_weight, preferred_element_type=jnp.float32)
    pre = jnp.dot(normed_low, fc1_weight, preferred_element_type=jnp.float32) + fc1_bias.astype(
        jnp.float32
    )
    hidden_values, gelu_pull = jax.vjp(partial(jax.nn.gelu, approximate=True), pre)
    hidden = hidden_values.astype(jnp.bfloat16)
    fed = jnp.dot(hidden, fc2_weight, preferred_element_type=jnp.float32)
    branch_terms = attended + fed
    both_biases = out_bias.astype(jnp.float32) + fc2_bias.astype(jnp.float32)
    combined = lax.psum(branch_terms, "tensor")
    block_out = (inputs + combined + both_biases).astype(jnp.bfloat16)
    block_out = block_out.reshape(seq_count, row_count, width)
    grad_low = cotangent.reshape(flat_rows, width)
    grad_full = grad_low.astype(jnp.float32)
    bias_grad = jnp.sum(grad_full, 0)
    out_weight_grad = outer_sum(merged, grad_low)
    fc2_weight_grad = outer_sum(hidden, grad_low)
    context_grad = inner_sum(grad_low, out_weight).astype(jnp.bfloat16)
    hidden_grad = inner_sum(grad_low, fc2_weight)
    pre_grad = gelu_pull(hidden_grad)[0].astype(jnp.bfloat16)
    fc1_bias_grad = jnp.sum(pre_grad.astype(jnp.float32), 0)
    fc1_weight_grad = outer_sum(normed_low, pre_grad)
    mlp_norm_grad = inner_sum(pre_grad, fc1_weight)
    context_send = jnp.transpose(
        context_grad.reshape(seq_count, row_count, heads_local, HD), (0, 2, 1, 3)
    )
    context_send = context_send.reshape(pair_count, row_count // 2, 2 * HD)
    context_in = lax.all_to_all(
        context_send, "context", split_axis=0, concat_axis=1, tiled=True
    ).reshape(pairs_local, length, HD)
    pair_grads = lax.map(pair_back, (received[0], received[1], received[2], context_in, log_totals))
    grads_send = jnp.swapaxes(pair_grads, 0, 1).reshape(3, pairs_local, length // 2, 2 * HD)
    grads_back = lax.all_to_all(grads_send, "context", split_axis=2, concat_axis=1, tiled=True)
    grads_back = grads_back.reshape(3, seq_count, heads_local, row_count, HD)
    turned_grad = jnp.transpose(grads_back, (1, 3, 0, 2, 4)).astype(jnp.float32)
    rotated_part = turned_grad[:, :, :2]
    first = rotated_part[..., :half_rot]
    second = rotated_part[..., half_rot:ROT]
    reverted = jnp.concatenate(
        [first * cosine + second * sine, second * cosine - first * sine, rotated_part[..., ROT:]],
        -1,
    )
    raw_grad = jnp.concatenate([reverted, turned_grad[:, :, 2:]], 2).astype(jnp.bfloat16)
    raw_grad = raw_grad.reshape(flat_rows, 3, local_width)
    qkv_bias_grad = jnp.sum(raw_grad.astype(jnp.float32), 0)
    qkv_weight_grad = jnp.einsum(
        "rd,rce->cde", normed_low, raw_grad, preferred_element_type=jnp.float32
    )
    attn_norm_grad = jnp.einsum(
        "rce,cde->rd", raw_grad, qkv_weight, preferred_element_type=jnp.float32
    )
    norm_terms = attn_norm_grad + mlp_norm_grad
    normed_grad = lax.psum(norm_terms, "tensor")
    input_part, gain_grad, shift_grad = norm_pull(normed_grad)
    tokens_grad = (grad_full + input_part).astype(jnp.bfloat16)
    tokens_grad = tokens_grad.reshape(seq_count, row_count, width)
    (
        gain_share_sum,
        shift_share,
        qkv_w_share,
        qkv_b_share,
        out_w_share,
        out_b_share,
        fc1_w_share,
        fc1_b_share,
        fc2_w_share,
        fc2_b_share,
    ) = (
        lax.psum_scatter(gain_grad, ("fsdp", "context"), scatter_dimension=0, tiled=True),
        lax.psum_scatter(shift_grad, ("fsdp", "context"), scatter_dimension=0, tiled=True),
        lax.psum_scatter(qkv_weight_grad, ("fsdp", "context"), scatter_dimension=1, tiled=True),
        lax.psum_scatter(qkv_bias_grad, ("fsdp", "context"), scatter_dimension=1, tiled=True),
        lax.psum_scatter(out_weight_grad, ("fsdp", "context"), scatter_dimension=1, tiled=True),
        lax.psum_scatter(bias_grad, ("fsdp", "context"), scatter_dimension=0, tiled=True),
        lax.psum_scatter(fc1_weight_grad, ("fsdp", "context"), scatter_dimension=0, tiled=True),
        lax.psum_scatter(fc1_bias_grad, ("fsdp", "context"), scatter_dimension=0, tiled=True),
        lax.psum_scatter(fc2_weight_grad, ("fsdp", "context"), scatter_dimension=1, tiled=True),
        lax.psum_scatter(bias_grad, ("fsdp", "context"), scatter_dimension=0, tiled=True),
    )
    finals = (
        lax.all_gather(gain_share_sum, "context", axis=0, tiled=True),
        lax.all_gather(shift_share, "context", axis=0, tiled=True),
        lax.all_gather(qkv_w_share, "context", axis=1, tiled=True),
        lax.all_gather(qkv_b_share, "context", axis=1, tiled=True),
        lax.all_gather(out_w_share, "context", axis=1, tiled=True),
        lax.all_gather(out_b_share, "context", axis=0, tiled=True),
        lax.all_gather(fc1_w_share, "context", axis=0, tiled=True),
        lax.all_gather(fc1_b_share, "context", axis=0, tiled=True),
        lax.all_gather(fc2_w_share, "context", axis=1, tiled=True),
        lax.all_gather(fc2_b_share, "context", axis=0, tiled=True),
    )
    return (
        block_out,
        tokens_grad,
        finals[0],
        finals[1],
        finals[2],
        finals[3],
        finals[4],
        finals[5],
        finals[6],
        finals[7],
        finals[8],
        finals[9],
    )


def solution(mesh):
    return jax.shard_map(
        per_device,
        mesh=mesh,
        in_specs=(
            P("fsdp", "context", None),
            P("fsdp"),
            P("fsdp"),
            P(None, "fsdp", "tensor"),
            P(None, ("tensor", "fsdp")),
            P("tensor", "fsdp"),
            P("fsdp"),
            P("fsdp", "tensor"),
            P(("tensor", "fsdp")),
            P("tensor", "fsdp"),
            P("fsdp"),
            P("fsdp", "context", None),
        ),
        out_specs=(
            P("fsdp", "context", None),
            P("fsdp", "context", None),
            P("fsdp"),
            P("fsdp"),
            P(None, "fsdp", "tensor"),
            P(None, ("tensor", "fsdp")),
            P("tensor", "fsdp"),
            P("fsdp"),
            P("fsdp", "tensor"),
            P(("tensor", "fsdp")),
            P("tensor", "fsdp"),
            P("fsdp"),
        ),
        check_vma=False,
    )
```

profile of v0, /device:TPU:0, one launch (start us, length us, event | category | flops | bytes accessed | tf_op | source)
XLA Modules:
  0.0 1689.6 jit_solution(265413236568293456)
XLA Ops:
  9.5 5.4 all_gather.58
  14.9 4.3 all_gather.59
  19.2 4.3 all_gather.61
  28.8 4.8 fusion.37
  33.6 59.1 %all-gather.14.cloned.1.call-done = bf16[3,2048,512]{2,1,0:T(8,128)(2,1)} async-done(((bf16[3,1024,512]{2,1,0:T(8,128)(2,1)}), bf16[3,2048,512]{2,1,0:T(8,128)(2,1)}) %all-gather.14.cloned.1.call-update) | async-done | bytes 6291472 | tf_op jit(solution)/shard_map/all_gather | solution.py:135
  92.7 11.6 broadcast_add_fusion
  104.3 6.6 copy.72
  110.9 9.1 reshape.310
  120.0 5.3 convert.45
  129.6 11.8 maximum_bitcast_fusion
  141.4 6.8 copy.95
  148.1 9.0 reshape.335
  161.4 6.2 convolution_convert_fusion
  172.5 4.0 copy.83
  176.5 3.9 reshape.318
  180.4 17.3 %all-to-all-done = bf16[3,16,256,128]{3,2,0,1:T(8,128)(2,1)S(1)} async-done(((bf16[3,16,256,128]{3,2,0,1:T(8,128)(2,1)}), bf16[3,16,256,128]{3,2,0,1:T(8,128)(2,1)S(1)}, u32[]{:S(2)}, u32[]{:S(2)}) %all-to-all-start) | async-done | bytes 3145760 | tf_op jit(solution)/shard_map/all_to_all | solution.py:172
  197.7 4.3 all-to-all-start.2
  208.2 80.1 %while.50 = (s32[]{:T(128)}, bf16[4,2048,64]{2,1,0:T(8,128)(2,1)}, f32[4,2048]{1,0:T(4,128)S(1)}, bf16[4,2048,64]{2,1,0:T(8,128)(2,1)}, bf16[4,2048,64]{2,1,0:T(...) while((s32[]{:T(128)}, bf16[4,2048,64]{2,1,0:T(8,128)(2,1)}, ...), condition=%wide.region_7.8_spmd, body=%wide.region_2.7_spmd.sunk | while | flops 277872640 | bytes 16834944 | solution.py:175
  210.6 16.3 while.53
  230.6 16.4 while.53
  250.7 16.3 while.53
  270.7 16.3 while.53
  300.2 10.8 all-to-all-done.1
  314.5 6.6 fusion.61
  321.2 116.1 %while.52 = (s32[]{:T(128)}, bf16[4,3,2048,64]{2,3,1,0:T(8,128)(2,1)}, bf16[4,2048,64]{2,1,0:T(8,128)(2,1)}, bf16[4,2048,64]{2,1,0:T(8,128)(2,1)}, f32[4,2048]{1...) while((s32[]{:T(128)}, ...), condition=%wide.region_13.14_spmd, body=%wide.region_9.13_spmd.sunk | while | flops 684883968 | bytes 42121676 | solution.py:210
  323.8 24.9 %while.54 = (s32[]{:T(128)}, f32[2048,64]{0,1:T(8,128)S(1)}, f32[2048,64]{0,1:T(8,128)S(1)}, bf16[4,512,64]{1,2,0:T(8,128)(2,1)S(1)}, s32[4]{0:T(128)S(1)}, /*in...) while((s32[]{:T(128)}, f32[2048,64]{0,1:T(8,128)S(1)}, ...), condition=%wide.region_12.12_spmd.clone, body=%wide.region_10.11_spmd.clone.sunk | while | flops 682262528 | bytes 35797184 | solution.py:96
  353.0 24.9 %while.54 = (s32[]{:T(128)}, f32[2048,64]{0,1:T(8,128)S(1)}, f32[2048,64]{0,1:T(8,128)S(1)}, bf16[4,512,64]{1,2,0:T(8,128)(2,1)S(1)}, s32[4]{0:T(128)S(1)}, /*in...) while((s32[]{:T(128)}, f32[2048,64]{0,1:T(8,128)S(1)}, ...), condition=%wide.region_12.12_spmd.clone, body=%wide.region_10.11_spmd.clone.sunk | while | flops 682262528 | bytes 35797184 | solution.py:96
  382.0 24.9 %while.54 = (s32[]{:T(128)}, f32[2048,64]{0,1:T(8,128)S(1)}, f32[2048,64]{0,1:T(8,128)S(1)}, bf16[4,512,64]{1,2,0:T(8,128)(2,1)S(1)}, s32[4]{0:T(128)S(1)}, /*in...) while((s32[]{:T(128)}, f32[2048,64]{0,1:T(8,128)S(1)}, ...), condition=%wide.region_12.12_spmd.clone, body=%wide.region_10.11_spmd.clone.sunk | while | flops 682262528 | bytes 35797184 | solution.py:96
  411.0 24.9 %while.54 = (s32[]{:T(128)}, f32[2048,64]{0,1:T(8,128)S(1)}, f32[2048,64]{0,1:T(8,128)S(1)}, bf16[4,512,64]{1,2,0:T(8,128)(2,1)S(1)}, s32[4]{0:T(128)S(1)}, /*in...) while((s32[]{:T(128)}, f32[2048,64]{0,1:T(8,128)S(1)}, ...), condition=%wide.region_12.12_spmd.clone, body=%wide.region_10.11_spmd.clone.sunk | while | flops 682262528 | bytes 35797184 | solution.py:96
  437.3 6.5 copy.85
  443.9 7.6 reshape.320
  453.9 39.6 %all_to_all.54 = bf16[3,4,1024,128]{3,1,0,2:T(4,128)(2,1)S(1)} all-to-all(bf16[3,4,1024,128]{3,1,0,2:T(4,128)(2,1)S(1)} %copy.86), channel_id=1, replica_groups=mesh['fsdp'=2,'context'=4,'tensor'=4] {'context'}, dimensions={2} | all-to-all | bytes 6291456 | tf_op jit(solution)/shard_map/all_to_all | solution.py:212
  494.3 5.3 convert_element_type.129
  499.6 8.2 copy.88
  528.5 11.6 convolution_bitcast_fusion
  540.8 4.3 all_gather.64
  545.1 14.5 fusion.59
  563.1 12.8 fusion.53
  576.0 19.0 %convert_reduce_fusion.1 = (f32[2048]{0:T(1024)S(1)}, bf16[1024,2048]{1,0:T(8,128)(2,1)S(1)}) fusion(f32[1024,2048]{1,0:T(8,128)} %copy-done.32, f32[2048]{0:T(1024)S(1)} %convert_element_type.120, bf16[1024,2048]{1,0:T(8,128)(2,1)} %bitcast.263, bf16[2048,2048]{1,0:T(8,128)(2,1)} %all-gather.20.cloned.1.call-done), kind=kOutput, calls=%fused_computation.79 | convolution fusion | flops 8638167040 | bytes 25182208 | tf_op jit(solution)/shard_map/dot_general | solution.py:28
  597.1 11.7 fusion.62
  610.3 18.5 %fusion.54 = f32[1024,2048]{1,0:T(8,128)} fusion(bf16[2048,2048]{1,0:T(8,128)(2,1)} %all-gather.20.cloned.1.call-done, f32[1024,2048]{1,0:T(8,128)} %copy-done.32, f32[2048]{0:T(1024)S(1)} %convert_element_type.120), kind=kOutput, calls=%fused_computation.115 | convolution fusion | flops 8610906112 | bytes 25174016 | tf_op jit(solution)/shard_map/dot_general | solution.py:186
  628.9 12.8 fusion.60
  641.8 7.0 convolution_add_fusion.1
  648.8 11.6 bitcast_add_fusion
  661.1 90.9 %reduce-scatter.14.cloned.1.call-done = f32[2048,256]{1,0:T(8,128)} async-done(((f32[2048,2048]{1,0:T(8,128)}), f32[2048,256]{1,0:T(8,128)}) %reduce-scatter.14.cloned.1.call-update) | async-done | bytes 2097168 | tf_op jit(solution)/shard_map/reduce_scatter | solution.py:256
  752.0 119.9 %reduce-scatter.12.cloned.1.call-done = f32[256,2048]{1,0:T(8,128)} async-done(((f32[2048,2048]{1,0:T(8,128)}), f32[256,2048]{1,0:T(8,128)}) %reduce-scatter.12.cloned.1.call-update) | async-done | bytes 2097168 | tf_op jit(solution)/shard_map/reduce_scatter | solution.py:254
  873.2 4.3 all_gather.66
  877.5 4.3 all_gather.67
  884.8 24.7 %reduce-scatter.16.cloned.1.call-done = f32[64,3]{1,0:T(8,128)} async-done(((f32[512,3]{1,0:T(8,128)}), f32[64,3]{1,0:T(8,128)}) %reduce-scatter.16.cloned.1.call-update) | async-done | bytes 784
  910.3 5.2 all-gather.2
  916.1 17.4 %all-gather.24.cloned.1.call-done = f32[512,1024]{1,0:T(8,128)} async-done(((f32[512,256]{1,0:T(8,128)}), f32[512,1024]{1,0:T(8,128)}) %all-gather.24.cloned.1.call-update) | async-done | bytes 2097168 | tf_op jit(solution)/shard_map/all_gather | solution.py:264
  933.5 566.5 %all-reduce.8.cloned.1.call-done = (f32[1024,2048]{1,0:T(8,128)}, f32[1024,2048]{1,0:T(8,128)}) async-done(((f32[1024,2048]{1,0:T(8,128)}, f32[1024,2048]{1,0:T(8,128)}), (f32[1024,2048]{1,0:T(8,128)}, f32[1024,2048]{1,0:T(8,128)})) %all-reduce.8.cloned.1.call-update) | async-done | bytes 16777232 | tf_op jit(solution)/shard_map/psum | solution.py:189
  1500.0 6.5 fusion.55
  1509.2 3.8 fusion.38
  1513.0 24.1 %all-reduce.4 = (f32[2048]{0:T(1024)S(1)}, f32[2048]{0:T(1024)S(1)}, f32[2048]{0:T(1024)S(1)}, f32[2048]{0:T(1024)S(1)}) all-reduce(f32[2048]{0:T(1024)S(1)} %get-tuple-element.258, f32[2048]{0:T(1024)S(1)} %get-tuple-element.260, ...), channel_id=2, replica_groups=mesh['fsdp'=2,'context'=4,'tensor'=4] {'fsdp','context'}, use_global_device_ids=true, to_apply=%region_18.19.clone | all-reduce | flops 8192 | bytes 65536
  1537.2 5.1 all-gather.3
  1542.5 5.1 all-gather.4
  1547.5 5.1 all-gather.1
  1552.6 5.1 all-gather
  1557.6 15.0 add_convert_fusion
  1572.7 6.7 copy.93
  1579.4 28.0 %all-gather.28.cloned.1.call-done = f32[2048,1024]{1,0:T(8,128)} async-done(((f32[2048,256]{1,0:T(8,128)}), f32[2048,1024]{1,0:T(8,128)}) %all-gather.28.cloned.1.call-update) | async-done | bytes 8388624 | tf_op jit(solution)/shard_map/all_gather | solution.py:268
  1607.3 59.7 %all-gather.26.cloned.1.call-done = f32[1024,2048]{1,0:T(8,128)} async-done(((f32[256,2048]{1,0:T(8,128)}), f32[1024,2048]{1,0:T(8,128)}) %all-gather.26.cloned.1.call-update) | async-done | bytes 8388624 | tf_op jit(solution)/shard_map/all_gather | solution.py:266
  1670.8 8.0 copy.172
  (524 shorter events, 263.3 us)
Async XLA Ops:
  7.2 2.3 copy-start.25
  7.2 7.7 copy-start.26
  7.2 12.0 copy-start.27
  7.2 85.5 %all-gather.14.cloned.1.call-start = ((), (), s32[]{:S(2)}) async-start(), calls=%async_computation.9 | async-start | bytes 9437184 | tf_op jit(solution)/shard_map/all_gather | solution.py:135
  7.9 153.5 %all-gather.16.cloned.1.call-start = ((), (), s32[]{:S(2)}) async-start(), calls=%async_computation.10 | async-start | bytes 3145728 | tf_op jit(solution)/shard_map/all_gather | solution.py:137
  8.7 536.4 %all-gather.18.cloned.1.call-start = ((), (), s32[]{:S(2)}) async-start(), calls=%async_computation.11 | async-start | bytes 12582912 | tf_op jit(solution)/shard_map/all_gather | solution.py:139
  9.4 17.3 %copy-start = (bf16[2,512,2048]{2,1,0:T(8,128)(2,1)S(1)}, bf16[2,512,2048]{2,1,0:T(8,128)(2,1)}, u32[]{:S(2)}) copy-start(bf16[2,512,2048]{2,1,0:T(8,128)(2,1)} %param.20) | copy-start | bytes 12582916
  14.8 14.0 copy-start.17
  26.7 6.9 copy-start.19
  28.0 0.6 copy-start.23
  28.6 5.0 copy-start.21
  28.8 98.1 %copy-start.13 = (f32[512,16]{0,1:T(8,128)}, f32[512,16]{0,1:T(8,128)S(1)}, u32[]{:S(2)}) copy-start(f32[512,16]{0,1:T(8,128)S(1)} %get-tuple-element.351) | copy-start | bytes 98308
  28.8 98.1 %copy-start.15 = (f32[512,16]{0,1:T(8,128)}, f32[512,16]{0,1:T(8,128)S(1)}, u32[]{:S(2)}) copy-start(f32[512,16]{0,1:T(8,128)S(1)} %get-tuple-element.352) | copy-start | bytes 98308
  157.1 40.6 %all-to-all-start = ((bf16[3,16,256,128]{3,2,0,1:T(8,128)(2,1)}), bf16[3,16,256,128]{3,2,0,1:T(8,128)(2,1)S(1)}, u32[]{:S(2)}, u32[]{:S(2)}) async-start(bf16[3,16,256,128]{3,2,0,1:T(8,128)(2,1)} %reshape.335), calls=%async_computation | async-start | bytes 6291456 | tf_op jit(solution)/shard_map/all_to_all | solution.py:172
  160.8 415.2 %all-gather.20.cloned.1.call-start = ((), (), s32[]{:S(2)}) async-start(), calls=%async_computation.12 | async-start | bytes 12582912 | tf_op jit(solution)/shard_map/all_gather | solution.py:141
  197.7 95.4 %all-to-all-start.2 = ((bf16[16,256,128]{2,1,0:T(8,128)(2,1)}), bf16[16,256,128]{2,1,0:T(8,128)(2,1)}, u32[]{:S(2)}, u32[]{:S(2)}) async-start(bf16[16,256,128]{2,1,0:T(8,128)(2,1)} %reshape.318), calls=%async_computation.2 | async-start | bytes 2097152 | tf_op jit(solution)/shard_map/all_to_all | solution.py:207
  293.1 18.0 %all-to-all-start.1 = ((bf16[4,1024,128]{2,0,1:T(4,128)(2,1)}), bf16[4,1024,128]{2,0,1:T(4,128)(2,1)S(1)}, u32[]{:S(2)}, u32[]{:S(2)}) async-start(bf16[4,1024,128]{2,0,1:T(4,128)(2,1)} %copy.79), calls=%async_computation.1 | async-start | bytes 2097152 | tf_op jit(solution)/shard_map/all_to_all | solution.py:177
  296.6 332.2 %reduce-scatter.10.cloned.1.call-start = ((), (), s32[]{:S(2)}) async-start(), calls=%async_computation.15 | async-start | bytes 4718592 | tf_op jit(solution)/shard_map/reduce_scatter | solution.py:252
  313.5 1.0 copy-start.5
  321.1 339.4 %reduce-scatter.8.cloned.1.call-start = ((), (), s32[]{:S(2)}) async-start(), calls=%async_computation.13 | async-start | bytes 14155776 | tf_op jit(solution)/shard_map/reduce_scatter | solution.py:250
  516.1 2.7 copy-start.14
  516.1 2.7 copy-start.16
  516.1 3.8 copy-start.10
  522.9 5.6 copy-start.8
  540.1 0.7 copy-start.28
  540.1 211.8 %reduce-scatter.14.cloned.1.call-start = ((), (), s32[]{:S(2)}) async-start(), calls=%async_computation.19 | async-start | bytes 18874368 | tf_op jit(solution)/shard_map/reduce_scatter | solution.py:256
  545.1 18.0 %copy-start.4 = (bf16[2,512,2048]{2,1,0:T(8,128)(2,1)S(1)}, bf16[2,512,2048]{2,1,0:T(8,128)(2,1)}, u32[]{:S(2)}) copy-start(bf16[2,512,2048]{2,1,0:T(8,128)(2,1)} %param.31) | copy-start | bytes 12582916
  559.7 3.4 copy-start.32
  575.9 296.0 %reduce-scatter.12.cloned.1.call-start = ((), (), s32[]{:S(2)}) async-start(), calls=%async_computation.17 | async-start | bytes 18874368 | tf_op jit(solution)/shard_map/reduce_scatter | solution.py:254
  576.0 21.1 %copy-start.7 = (bf16[1024,2048]{1,0:T(8,128)(2,1)S(1)}, bf16[1024,2048]{1,0:T(8,128)(2,1)}, u32[]{:S(2)}) copy-start(bf16[1024,2048]{1,0:T(8,128)(2,1)} %fusion.37) | copy-start | bytes 12582916
  595.1 2.0 copy-start.33
  608.8 300.6 %reduce-scatter.16.cloned.1.call-start = ((), (), s32[]{:S(2)}) async-start(), calls=%async_computation.21 | async-start | bytes 294912
  610.2 323.3 %all-gather.24.cloned.1.call-start = ((), (), s32[]{:S(2)}) async-start(), calls=%async_computation.16 | async-start | bytes 2621440 | tf_op jit(solution)/shard_map/all_gather | solution.py:264
  628.8 12.9 copy-start.6
  628.9 871.1 %all-reduce.8.cloned.1.call-start = ((), (), s32[]{:S(2)}) async-start(), calls=%async_computation.22 | async-start | bytes 33554432 | tf_op jit(solution)/shard_map/psum | solution.py:189
  628.9 12.9 copy-start.3
  628.9 12.9 copy-start.11
  641.8 7.0 copy-start.9
  660.4 211.5 %copy-start.31 = (u32[32]{0:T(128)S(1)}, u32[32]{0:T(128)}, u32[]{:S(2)}) copy-start(u32[32]{0:T(128)} %constant.120) | copy-start | bytes 388
  660.4 212.8 %copy-start.29 = (bf16[1024]{0:T(1024)(128)(2,1)S(1)}, bf16[1024]{0:T(1024)(128)(2,1)}, u32[]{:S(2)}) copy-start(bf16[1024]{0:T(1024)(128)(2,1)} %param.26) | copy-start | bytes 6148
  660.5 217.1 %copy-start.30 = (bf16[1024]{0:T(1024)(128)(2,1)S(1)}, bf16[1024]{0:T(1024)(128)(2,1)}, u32[]{:S(2)}) copy-start(bf16[1024]{0:T(1024)(128)(2,1)} %param.30) | copy-start | bytes 6148
  660.5 912.2 %all-gather.22.cloned.1.call-start = ((), (), s32[]{:S(2)}) async-start(), calls=%async_computation.14 | async-start | bytes 7864320 | tf_op jit(solution)/shard_map/all_gather | solution.py:262
  661.0 946.3 %all-gather.28.cloned.1.call-start = ((), (), s32[]{:S(2)}) async-start(), calls=%async_computation.20 | async-start | bytes 10485760 | tf_op jit(solution)/shard_map/all_gather | solution.py:268
  751.9 748.0 %copy-start.18 = (f32[2048]{0:T(1024)S(1)}, f32[2048]{0:T(1024)}, u32[]{:S(2)}) copy-start(f32[2048]{0:T(1024)} %copy-done.17) | copy-start | bytes 24580
  752.0 748.0 %copy-start.20 = (f32[1,4,2,128]{3,1,2,0:T(4,128)S(1)}, f32[1,4,2,128]{3,1,2,0:T(4,128)}, u32[]{:S(2)}) copy-start(f32[1,4,2,128]{3,1,2,0:T(4,128)} %copy-done.19) | copy-start | bytes 12292
  752.0 915.1 %all-gather.26.cloned.1.call-start = ((), (), s32[]{:S(2)}) async-start(), calls=%async_computation.18 | async-start | bytes 10485760 | tf_op jit(solution)/shard_map/all_gather | solution.py:266
  1500.0 6.5 copy-start.24
  1500.0 6.5 copy-start.1
  1500.0 9.2 copy-start.2
  1500.0 9.2 copy-start.22
  1572.6 96.2 %copy-start.12 = (f32[512,1024]{1,0:T(8,128)S(1)}, f32[512,1024]{1,0:T(8,128)}, u32[]{:S(2)}) copy-start(f32[512,1024]{1,0:T(8,128)} %all-gather.24.cloned.1.call-done) | copy-start | bytes 6291460
  1668.9 10.6 slice-start
  1670.8 8.6 slice-start.1
Sparse Core Ops, SparseCore 0:
  9.6 83.0 all-gather.13
  94.2 33.1 all-gather.15
  129.0 103.9 all-gather.17
  234.4 103.9 all-gather.19
  341.6 51.3 reduce-scatter.9
  540.2 91.7 reduce-scatter.7
  636.0 115.9 reduce-scatter.13
  755.9 115.9 reduce-scatter.11
  875.8 33.5 reduce-scatter.15
  910.9 22.5 all-gather.23
  936.7 563.2 all-reduce.7
  1501.4 45.9 all-gather.21
  1549.0 58.2 all-gather.27
  1608.7 58.2 all-gather.25
where the time goes:
time: 1690 us
  waiting for transfers between devices  998 us (59%)
  matrix products  248 us (15%)
  local copies, waits for them, and re-layouts  190 us (11%)
  blocking collectives  116 us (7%)
  other arithmetic  86.9 us (5%)
  loops' own time  23.1 us (1%)
    psum x1, waiting for transfers between devices, per_device(): combined = lax.psum(branch_terms, 'tensor')  567 us
    reduce_scatter x1, waiting for transfers between devices, per_device(): lax.psum_scatter(fc1_weight_grad, ('fsdp', 'context'), scatter_dimension=...  120 us
    reduce_scatter x1, waiting for transfers between devices, per_device(): lax.psum_scatter(fc2_weight_grad, ('fsdp', 'context'), scatter_dimension=...  90.9 us
    all_gather x1, waiting for transfers between devices, per_device(): lax.all_gather(fc1_w_share, 'context', axis=0, tiled=True)  59.7 us
    all_gather x1, waiting for transfers between devices, per_device(): lax.all_gather(w_qkv, 'fsdp', axis=1, tiled=True)  59.1 us
    dot_general x32, matrix products, causal_scores(): jnp.einsum('qh,kh->qk', query_block, key, preferred_element_type=jnp.floa...  45.1 us
    all_to_all x1, blocking collectives, per_device(): lax.all_to_all(grads_send, 'context', split_axis=2, concat_axis=1, tiled=...  39.6 us
    dot_general x3, matrix products, inner_sum(): lax.dot_general(left, right, (((1,), (1,)), ((), ())), preferred_element_...  38.1 us
  transfers between devices with their start and end apart: 17, of which 10 were waited for; matrix products, arithmetic and copies ran while one was open for 30% of the time, Pallas kernels for 0%

commit v1 on v0

v1 whole, which is shorter than its diff:
```python
import functools

import jax
import jax.numpy as jnp
from jax import lax
import jax.experimental.pallas as pl
import jax.experimental.pallas.tpu as pltpu
from jax.sharding import PartitionSpec as P

HD = 64
ROT = 32
EPSILON = 1e-05
LANES = 128
F32 = jnp.float32
BF16 = jnp.bfloat16
ROOT = 0.7978845608028654
CUBE = 0.044715
VMEM_BYTES = 60 << 20


def lasting(micros):
    return pl.CostEstimate(flops=0, bytes_accessed=int(micros * 3.4e6), transcendentals=0)


def nn(a, b):
    return lax.dot_general(a, b, (((1,), (0,)), ((), ())), preferred_element_type=F32)


def nt(a, b):
    return lax.dot_general(a, b, (((1,), (1,)), ((), ())), preferred_element_type=F32)


def tn(a, b):
    return lax.dot_general(a, b, (((0,), (0,)), ((), ())), preferred_element_type=F32)


def add_low(*terms):
    total = terms[0].astype(F32)
    for term in terms[1:]:
        total = total + term.astype(F32)
    return total.astype(BF16)


def to_fsdp(value):
    return lax.ppermute(value, "fsdp", [(0, 1), (1, 0)])


def to_context(value, mask):
    size = lax.axis_size("context")
    return lax.ppermute(value, "context", [(i, i ^ mask) for i in range(size)])


def to_tensor(value, mask):
    size = lax.axis_size("tensor")
    return lax.ppermute(value, "tensor", [(i, i ^ mask) for i in range(size)])


def after(value, *others):
    return lax.optimization_barrier((value,) + others)[0]


def masks_of(size):
    mask = 1
    while mask < size:
        yield mask
        mask *= 2


def sum_everywhere(value, over_tensor):
    for mask in masks_of(lax.axis_size("context")):
        value = value + to_context(value, mask)
    value = value + to_fsdp(value)
    if over_tensor:
        for mask in masks_of(lax.axis_size("tensor")):
            value = value + to_tensor(value, mask)
    return value


def own_blocks(own, axis, place, block):
    count = own.shape[axis] // block
    return [
        lax.dynamic_slice_in_dim(own, (p ^ place) * block, block, axis) for p in range(count)
    ]


class Order:
    def __init__(self):
        self.last = None

    def __call__(self, value):
        return value if self.last is None else after(value, self.last)

    def mark(self, value):
        self.last = value
        return value

    def wait(self, *values):
        if self.last is not None:
            values = lax.optimization_barrier(values + (self.last,))[:-1]
        else:
            values = lax.optimization_barrier(values)
        self.last = values[0]
        return values


class Reduction:
    def __init__(self, order, pairs, block):
        self.order, self.pairs, self.block = order, pairs, block

    def send(self):
        (self.sent,) = outer(self.order, self.pairs, 1, None)
        self.sent = to_context(self.sent, 1)

    def keep(self):
        results = outer(self.order, self.pairs, 0, self.sent)
        self.near, self.far = results[: len(self.pairs)], results[len(self.pairs) :]
        self.near, self.far = list(self.near), list(self.far)
        self.pieces = [None] * len(self.pairs)

    def over_fsdp(self, i, *earlier):
        self.far[i] = to_fsdp(after(self.far[i], *earlier) if earlier else self.far[i])
        return self.far[i]

    def over_chips(self, i):
        self.near[i] = self.order.mark(add_low(self.order(self.near[i]), self.far[i]))
        self.masks = list(masks_of(lax.axis_size("context") // 2))
        if self.masks:
            self.far[i] = to_context(self.near[i], 2 * self.masks[0])
        return self.far[i]

    def over_cores(self, i):
        total = self.near[i]
        for n, mask in enumerate(self.masks):
            other = self.far[i] if n == 0 else to_context(total, 2 * mask)
            total = self.order.mark(add_turned(self.order(total), other, mask, self.block))
        self.pieces[i] = (total, to_context(total, 1))


def prepare_kernel(count, me_ref, tokens, grad, gain, bias, normed_out, grad_out, sum_out, kept):
    values = tokens[...].astype(F32)
    centered = values - jnp.mean(values, -1, keepdims=True)
    variance = jnp.mean(centered * centered, -1, keepdims=True)
    kept[...] = (centered * lax.rsqrt(variance + EPSILON) * gain[...] + bias[...]).astype(BF16)
    me = me_ref[0]
    block = tokens.shape[1] // count
    for p in range(count):
        source = pl.ds(pl.multiple_of((p ^ me) * block, block), block)
        normed_out[:, p * block : (p + 1) * block] = kept[:, source]
        grad_out[:, p * block : (p + 1) * block] = grad[:, source]
    part = jnp.sum(grad[...].astype(F32), 0, keepdims=True)

    @pl.when(pl.program_id(0) == 0)
    def _():
        sum_out[...] = part

    @pl.when(pl.program_id(0) > 0)
    def _():
        sum_out[...] += part


def prepare(me, count, tokens, grad, gain, bias):
    rows, width = tokens.shape
    tile = min(128, rows)
    row_spec = pl.BlockSpec((tile, width), lambda r, me: (r, 0))
    one_spec = pl.BlockSpec((1, width), lambda r, me: (0, 0))
    return pl.pallas_call(
        functools.partial(prepare_kernel, count),
        out_shape=[
            jax.ShapeDtypeStruct((rows, width), BF16),
            jax.ShapeDtypeStruct((rows, width), BF16),
            jax.ShapeDtypeStruct((1, width), F32),
        ],
        grid_spec=pltpu.PrefetchScalarGridSpec(
            num_scalar_prefetch=1,
            grid=(rows // tile,),
            in_specs=[row_spec, row_spec, one_spec, one_spec],
            out_specs=[row_spec, row_spec, one_spec],
            scratch_shapes=[pltpu.VMEM((tile, width), BF16)],
        ),
        compiler_params=pltpu.CompilerParams(vmem_limit_bytes=VMEM_BYTES),
        cost_estimate=lasting(10),
        name="prepare",
    )(me, tokens, grad, gain, bias)


def turn(part, cosine, below, above):
    return (
        part * cosine
        + pltpu.roll(part, LANES - ROT // 2, 1) * below
        + pltpu.roll(part, ROT // 2, 1) * above
    )


def project_kernel(seqs, qkv_count, out_count, parts, k_ref, c_ref, *refs):
    normed, grad, bias, cosine, below, above = refs[:6]
    ends = (6 + qkv_count, 6 + qkv_count + out_count)
    outs, kept = refs[ends[1] : -1], refs[-1]
    which = pl.program_id(0)
    rows, width = kept.shape
    length = rows // seqs

    @pl.when(which < 3)
    def _():
        weight = jnp.concatenate([w[0] for w in refs[6 : ends[0]]], 0)
        raw = nn(normed[...], weight) + bias[0]

        @pl.when(which < 2)
        def _():
            for s in range(seqs):
                for lane in range(0, width, LANES):
                    part = raw[s * length : (s + 1) * length, lane : lane + LANES]
                    kept[s * length : (s + 1) * length, lane : lane + LANES] = turn(
                        part, cosine[...], below[...], above[...]
                    ).astype(BF16)

        @pl.when(which == 2)
        def _():
            kept[...] = raw.astype(BF16)

    @pl.when(which == 3)
    def _():
        weight = jnp.concatenate([w[...] for w in refs[ends[0] : ends[1]]], 1)
        kept[...] = nt(grad[...], weight).astype(BF16)

    span = width // parts
    for m in range(parts):
        at = pl.ds(pl.multiple_of((m ^ c_ref[0]) * span, span), span) if parts > 1 else slice(None)
        for s in range(seqs):
            part = kept[s * length : (s + 1) * length, at]
            if parts == 1:
                outs[s][0, 0] = part
            else:
                outs[3 * s + min(m, 2)][max(m - 2, 0), 0] = part


def project(place, context, normed, grad, qkv, qkv_rest, out, out_rest, bias, tables, seqs, parts):
    rows, depth = normed.shape
    width = qkv.shape[2]
    block = qkv_rest[0].shape[1]
    count = qkv.shape[1] // block
    length = rows // seqs
    span = width // parts
    table = pl.BlockSpec((length, LANES), lambda c, k, x: (0, 0))
    whole = pl.BlockSpec((rows, depth), lambda c, k, x: (0, 0), pipeline_mode=pl.Buffered(1))

    def qkv_spec(p):
        return pl.BlockSpec((1, block, width), lambda c, k, x: (jnp.minimum(c, 2), p ^ k[0], 0))

    def out_spec(p):
        return pl.BlockSpec((width, block), lambda c, k, x: (0, p ^ k[0]))

    qkv_specs = [qkv_spec(p) for p in range(count)] + [
        pl.BlockSpec((1, block, width), lambda c, k, x: (jnp.minimum(c, 2), 0, 0))
    ] * len(qkv_rest)
    out_specs = [out_spec(p) for p in range(count)] + [
        pl.BlockSpec((width, block), lambda c, k, x: (0, 0))
    ] * len(out_rest)
    counts = [1] if parts == 1 else [1, 1, 2]
    results = pl.pallas_call(
        functools.partial(project_kernel, seqs, len(qkv_specs), len(out_specs), parts),
        out_shape=[jax.ShapeDtypeStruct((n, 4, length, span), BF16) for n in counts] * seqs,
        grid_spec=pltpu.PrefetchScalarGridSpec(
            num_scalar_prefetch=2,
            grid=(4,),
            in_specs=[
                whole,
                whole,
                pl.BlockSpec((1, 1, width), lambda c, k, x: (jnp.minimum(c, 2), 0, 0)),
                table,
                table,
                table,
            ]
            + qkv_specs
            + out_specs,
            out_specs=[
                pl.BlockSpec((n, 1, length, span), lambda c, k, x: (0, c, 0, 0)) for n in counts
            ]
            * seqs,
            scratch_shapes=[pltpu.VMEM((rows, width), BF16)],
        ),
        compiler_params=pltpu.CompilerParams(vmem_limit_bytes=VMEM_BYTES),
        cost_estimate=lasting(19),
        name="project",
    )(
        place,
        context,
        normed,
        grad,
        bias,
        *tables,
        *([qkv] * count),
        *qkv_rest,
        *([out] * count),
        *out_rest,
    )
    return [results[s * len(counts) : (s + 1) * len(counts)] for s in range(seqs)]


def attend_kernel(parts, queries_at_once, keys_at_once, me_ref, *refs):
    pieces = refs[:parts]
    outs = refs[parts:-11]
    q_all, k_all, v_all, g_all, v_turned, k_turned, o_all, dq_all, dk_all, dv_all, held = refs[-11:]
    rows, width = pieces[0].shape[2:]
    length = rows * parts
    me = me_ref[0]
    bq, bk = queries_at_once, keys_at_once
    scale = HD**-0.5
    for m in range(parts):
        at = pl.ds(pl.multiple_of((me ^ m) * rows, rows), rows)
        q_all[at, :] = (pieces[m][0, 0].astype(F32) * scale).astype(BF16)
        k_all[at, :] = pieces[m][0, 1]
        v_all[at, :] = pieces[m][0, 2]
        g_all[at, :] = pieces[m][0, 3]
    v_turned[...] = v_all[...].T
    k_turned[...] = k_all[...].T
    dk_all[...] = jnp.zeros_like(dk_all)
    dv_all[...] = jnp.zeros_like(dv_all)
    heads = width // HD
    lane_head = lax.broadcasted_iota(jnp.int32, (1, width), 1) // HD
    row_head = lax.broadcasted_iota(jnp.int32, (width, 1), 0) // HD

    def one_block(i, _):
        at_q = pl.ds(pl.multiple_of(i * bq, bq), bq)
        query = q_all[at_q, :]
        grad = g_all[at_q, :]
        blocks = (i + 1) * (bq // bk)
        outs_now = jnp.zeros((width, bq), F32)
        grads_now = jnp.zeros((width, bq), F32)
        for h in range(heads):
            q_head = jnp.where(lane_head == h, query, jnp.zeros_like(query))
            g_head = jnp.where(lane_head == h, grad, jnp.zeros_like(grad))

            def score(j, top, masked=False):
                at_k = pl.ds(pl.multiple_of(j * bk, bk), bk)
                scores = nt(k_all[at_k, :], q_head)
                if masked:
                    key = j * bk + lax.broadcasted_iota(jnp.int32, (bk, bq), 0)
                    place = i * bq + lax.broadcasted_iota(jnp.int32, (bk, bq), 1)
                    scores = jnp.where(key <= place, scores, -1e30)
                held[at_k, :] = scores
                return jnp.maximum(top, jnp.max(scores.reshape(bk // 8, 8, bq), 0))

            top = jnp.full((8, bq), -1e30, F32)
            top = lax.fori_loop(0, i * (bq // bk), score, top)
            for d in range(bq // bk):
                top = score(i * (bq // bk) + d, top, True)
            top = jnp.max(top, 0, keepdims=True)

            def weigh(j, carry):
                total, output = carry
                at_k = pl.ds(pl.multiple_of(j * bk, bk), bk)
                weights = jnp.exp(held[at_k, :] - top)
                held[at_k, :] = weights
                total = total + jnp.sum(weights.reshape(bk // 8, 8, bq), 0)
                return total, output + nn(v_turned[:, at_k], weights.astype(BF16))

            total, output = lax.fori_loop(
                0, blocks, weigh, (jnp.zeros((8, bq), F32), jnp.zeros((width, bq), F32))
            )
            inverse = 1.0 / jnp.sum(total, 0, keepdims=True)
            output = output * inverse
            g_turned = g_head.T.astype(F32)
            inner = jnp.sum(output * g_turned, 0, keepdims=True) * inverse
            g_scaled = (g_turned * inverse).astype(BF16)
            g_rows = g_scaled.T

            def back(j, total):
                at_k = pl.ds(pl.multiple_of(j * bk, bk), bk)
                weights = held[at_k, :]
                prob_grad = nn(v_all[at_k, :], g_scaled)
                score_grad = (weights * (prob_grad - inner)).astype(BF16)
                dv_all[at_k, :] += nn(weights.astype(BF16), g_rows)
                dk_all[at_k, :] += nn(score_grad, q_head)
                return total + nn(k_turned[:, at_k], score_grad)

            q_grad = lax.fori_loop(0, blocks, back, jnp.zeros((width, bq), F32)) * scale
            outs_now = jnp.where(row_head == h, output, outs_now)
            grads_now = jnp.where(row_head == h, q_grad, grads_now)
        o_all[at_q, :] = outs_now.T.astype(BF16)
        dq_all[at_q, :] = grads_now.T.astype(BF16)
        return 0

    lax.fori_loop(0, length // bq, one_block, 0)
    for m in range(parts):
        at = pl.ds(pl.multiple_of((me ^ m) * rows, rows), rows)
        out, i = (outs[m], 0) if len(outs) == parts else (outs[min(m, 2)], max(m - 2, 0))
        out[i, 0] = o_all[at, :]
        out[i, 1] = dq_all[at, :]
        out[i, 2] = dk_all[at, :].astype(BF16)
        out[i, 3] = dv_all[at, :].astype(BF16)


def attend(context, pieces, paired):
    parts = len(pieces)
    seqs, _, rows, width = pieces[0].shape
    length = rows * parts
    bq = min(1024, length)
    bk = bq
    vmem = pltpu.VMEM
    counts = [1, 1, 2] if paired else [seqs] * parts
    return pl.pallas_call(
        functools.partial(attend_kernel, parts, bq, bk),
        out_shape=[jax.ShapeDtypeStruct((n, 4, rows, width), BF16) for n in counts],
        grid_spec=pltpu.PrefetchScalarGridSpec(
            num_scalar_prefetch=1,
            grid=(seqs,),
            in_specs=[pl.BlockSpec((1, 4, rows, width), lambda s, me: (s, 0, 0, 0))] * parts,
            out_specs=[
                pl.BlockSpec((n if paired else 1, 4, rows, width), lambda s, me: (s, 0, 0, 0))
                for n in counts
            ],
            scratch_shapes=[vmem((length, width), BF16)] * 4
            + [vmem((width, length), BF16)] * 2
            + [vmem((length, width), BF16)] * 2
            + [vmem((length, width), F32)] * 2
            + [vmem((length, bq), F32)],
        ),
        compiler_params=pltpu.CompilerParams(vmem_limit_bytes=VMEM_BYTES),
        cost_estimate=lasting(28),
        name="attend",
    )(context, *pieces)


def unturn_kernel(parts, c_ref, *refs):
    pieces = refs[:parts]
    cosine, below, above = refs[parts : parts + 3]
    merged, raw, sums = refs[-3:]
    width = merged.shape[1]
    span = width // parts
    for m in range(parts):
        at = pl.ds(pl.multiple_of((m ^ c_ref[0]) * span, span), span) if parts > 1 else slice(None)
        merged[:, at] = pieces[m][0, 0]
    for c in range(3):
        for m in range(parts):
            for lane in range(0, span, LANES):
                start = (m ^ c_ref[0]) * span + c * width + lane if parts > 1 else c * width + lane
                at = pl.ds(pl.multiple_of(start, LANES), LANES)
                part = pieces[m][0, c + 1, :, lane : lane + LANES]
                if c < 2:
                    part = turn(part.astype(F32), cosine[...], -below[...], -above[...])
                    part = part.astype(BF16)
                raw[:, at] = part
                sums[:, at] = jnp.sum(part.astype(F32), 0, keepdims=True)


def unturn(context, pieces, tables, s, rows, earlier):
    parts = len(pieces)
    length, span = pieces[0].shape[2:]
    width = span * parts
    vmem = pl.BlockSpec(memory_space=pltpu.VMEM)
    return pl.pallas_call(
        functools.partial(unturn_kernel, parts),
        out_shape=[
            jax.ShapeDtypeStruct((rows, width), BF16),
            jax.ShapeDtypeStruct((rows, 3 * width), BF16),
            jax.ShapeDtypeStruct((1, 3 * width), F32),
        ],
        grid=(1,),
        in_specs=[pl.BlockSpec(memory_space=pltpu.SMEM)]
        + [vmem] * (parts + 3)
        + [pl.BlockSpec(memory_space=pl.ANY)] * len(earlier),
        out_specs=[
            pl.BlockSpec((length, width), lambda i: (s, 0)),
            pl.BlockSpec((length, 3 * width), lambda i: (s, 0)),
            vmem,
        ],
        input_output_aliases={parts + 4 + i: i for i in range(len(earlier))},
        compiler_params=pltpu.CompilerParams(vmem_limit_bytes=VMEM_BYTES),
        cost_estimate=lasting(4),
        name="unturn",
    )(context, *pieces, *tables, *earlier)


def norm_back_kernel(count, k_ref, raw, back, *refs):
    width = refs[0].shape[2]
    total = back[...].astype(F32)
    for c in range(3):
        weight = jnp.concatenate([w[c] for w in refs[:count]], 0)
        total = total + nt(raw[:, c * width : (c + 1) * width], weight)
    refs[-1][...] = total.astype(BF16)


def norm_back(place, raw, back, own, rest, s, seqs, earlier):
    rows, depth = back.shape
    width = own.shape[2]
    block = rest[0].shape[1]
    count = own.shape[1] // block
    length = rows // seqs
    tile = min(256, length)
    skip = s * (length // tile)

    def own_spec(p):
        return pl.BlockSpec((3, block, width), lambda r, k: (0, p ^ k[0], 0))

    specs = [own_spec(p) for p in range(count)] + [
        pl.BlockSpec((3, block, width), lambda r, k: (0, 0, 0))
    ] * len(rest)
    some = pl.BlockSpec((tile, depth), lambda r, k: (r + skip, 0))
    return pl.pallas_call(
        functools.partial(norm_back_kernel, len(specs)),
        out_shape=jax.ShapeDtypeStruct((rows, depth), BF16),
        grid_spec=pltpu.PrefetchScalarGridSpec(
            num_scalar_prefetch=1,
            grid=(length // tile,),
            in_specs=[pl.BlockSpec((tile, 3 * width), lambda r, k: (r + skip, 0)), some]
            + specs
            + [pl.BlockSpec(memory_space=pl.ANY)] * len(earlier),
            out_specs=some,
        ),
        input_output_aliases={3 + len(specs) + i: i for i in range(len(earlier))},
        compiler_params=pltpu.CompilerParams(vmem_limit_bytes=VMEM_BYTES),
        cost_estimate=lasting(8),
        name="norm_back",
    )(place, raw, back, *([own] * count), *rest, *earlier)


def gelu_pair(value):
    square = value * value
    bent = jnp.tanh(ROOT * value * (1.0 + CUBE * square))
    half = 0.5 * (1.0 + bent)
    slope = half + 0.5 * value * (1.0 - bent * bent) * (ROOT * (1.0 + 3.0 * CUBE * square))
    return value * half, slope


def feed_kernel(first_count, second_count, onto, k_ref, *refs):
    normed, grad, bias = refs[:3]
    ends = (3 + first_count, 3 + first_count + second_count)
    first = jnp.concatenate([r[...] for r in refs[3 : ends[0]]], 0)
    second = jnp.concatenate([r[...] for r in refs[ends[0] : ends[1]]], 1)
    hidden_out, pre_grad_out, sum_out, fed_out, back_out, fed, back = refs[ends[1] + onto :]
    tile = pl.program_id(0)

    @pl.when(tile == 0)
    def _():
        if onto:
            fed[...] = refs[ends[1]][...].astype(F32)
            back[...] = refs[ends[1] + 1][...].astype(F32)
        else:
            fed[...] = jnp.zeros_like(fed)
            back[...] = jnp.zeros_like(back)

    hidden, slope = gelu_pair(nn(normed[...], first) + bias[...])
    hidden_low = hidden.astype(BF16)
    pre_grad = (nt(grad[...], second) * slope).astype(BF16)
    hidden_out[...] = hidden_low
    pre_grad_out[...] = pre_grad
    fed[...] += nn(hidden_low, second)
    back[...] += nt(pre_grad, first)
    sum_out[...] = jnp.sum(pre_grad.astype(F32), 0, keepdims=True)

    @pl.when(tile == pl.num_programs(0) - 1)
    def _():
        fed_out[...] = fed[...].astype(BF16)
        back_out[...] = back[...].astype(BF16)


def feed(
    place, block, normed, grad, bias, own_first, rest_first, own_second, rest_second, part, sums
):
    rows, width = normed.shape
    inside = rest_first[0].shape[0] // block
    units = rest_first[0].shape[1]
    count = own_first.shape[0] // block
    tile = min(512, units)
    skip = part * (units // tile)
    whole = pl.BlockSpec((rows, width), lambda t, k: (0, 0), pipeline_mode=pl.Buffered(1))

    def first_spec(p):
        return pl.BlockSpec((block, tile), lambda t, k: (p ^ k[0], t + skip))

    def second_spec(p):
        return pl.BlockSpec((tile, block), lambda t, k: (t + skip, p ^ k[0]))

    def first_rest(p):
        return pl.BlockSpec((block, tile), lambda t, k: (p ^ (k[0] % inside), t))

    def second_rest(p):
        return pl.BlockSpec((tile, block), lambda t, k: (t, p ^ (k[0] % inside)))

    first = [first_spec(p) for p in range(count)]
    first += [first_rest(p) for p in range(inside)] * len(rest_first)
    second = [second_spec(p) for p in range(count)]
    second += [second_rest(p) for p in range(inside)] * len(rest_second)
    unit_rows = pl.BlockSpec((rows, tile), lambda t, k: (0, t))
    return pl.pallas_call(
        functools.partial(feed_kernel, len(first), len(second), len(sums)),
        out_shape=[
            jax.ShapeDtypeStruct((rows, units), BF16),
            jax.ShapeDtypeStruct((rows, units), BF16),
            jax.ShapeDtypeStruct((1, units), F32),
            jax.ShapeDtypeStruct((rows, width), BF16),
            jax.ShapeDtypeStruct((rows, width), BF16),
        ],
        grid_spec=pltpu.PrefetchScalarGridSpec(
            num_scalar_prefetch=1,
            grid=(units // tile,),
            in_specs=[whole, whole, pl.BlockSpec((1, tile), lambda t, k: (0, t + skip))]
            + first
            + second
            + [whole] * len(sums),
            out_specs=[
                unit_rows,
                unit_rows,
                pl.BlockSpec((1, tile), lambda t, k: (0, t)),
                whole,
                whole,
            ],
            scratch_shapes=[pltpu.VMEM((rows, width), F32)] * 2,
        ),
        compiler_params=pltpu.CompilerParams(vmem_limit_bytes=VMEM_BYTES),
        cost_estimate=lasting(31),
        name="feed",
    )(
        place,
        normed,
        grad,
        bias,
        *([own_first] * count),
        *[piece for piece in rest_first for _ in range(inside)],
        *([own_second] * count),
        *[piece for piece in rest_second for _ in range(inside)],
        *sums,
    )


def outer_kernel(steps, adds, *refs):
    count = len(steps)
    lefts, rights = refs[: 2 * count], refs[2 * count : 3 * count]
    outs = refs[3 * count + adds : -1]
    turned = refs[-1]
    quarter = lefts[0].shape[1]
    step = pl.program_id(0)
    start = 0
    for i in range(count):

        @pl.when(step == start)
        def _():
            turned[:quarter, :] = lefts[2 * i][...].T
            turned[quarter:, :] = lefts[2 * i + 1][...].T

        @pl.when((step >= start) & (step < start + steps[i]))
        def _():
            value = nn(turned[...], rights[i][...])
            for high in range(2):
                part = value[high * quarter : (high + 1) * quarter]
                if adds:
                    part = part + refs[3 * count][high].astype(F32)
                    outs[high * count + i][...] = part.astype(BF16)
                else:
                    outs[0][high] = part.astype(BF16)

        start += steps[i]


def outer(order, pairs, low, received):
    rows, width = pairs[0][0].shape
    quarter = width // 4
    tile = min([512] + [right.shape[1] for _, right in pairs])
    steps = [right.shape[1] // tile for _, right in pairs]
    total = sum(steps) * tile
    adds = received is not None

    def left_spec(high):
        return pl.BlockSpec((rows, quarter), lambda t: (0, 2 * high + low))

    def column_spec(height, i):
        start = sum(steps[:i])
        return pl.BlockSpec((height, tile), lambda t: (0, jnp.clip(t - start, 0, steps[i] - 1)))

    both = pl.BlockSpec((2, quarter, tile), lambda t: (0, 0, t))
    if adds:
        out_shape = [
            jax.ShapeDtypeStruct((quarter, right.shape[1]), BF16) for _, right in pairs
        ] * 2
        out_specs = [column_spec(quarter, i) for i in range(len(pairs))] * 2
    else:
        out_shape = [jax.ShapeDtypeStruct((2, quarter, total), BF16)]
        out_specs = [both]
    results = pl.pallas_call(
        functools.partial(outer_kernel, steps, int(adds)),
        out_shape=out_shape,
        grid=(sum(steps),),
        in_specs=[left_spec(high) for _ in pairs for high in range(2)]
        + [column_spec(rows, i) for i in range(len(pairs))]
        + [both] * adds,
        out_specs=out_specs,
        scratch_shapes=[pltpu.VMEM((2 * quarter, rows), BF16)],
        compiler_params=pltpu.CompilerParams(vmem_limit_bytes=VMEM_BYTES),
        cost_estimate=lasting(11),
        name="outer",
    )(
        *[left for left, _ in pairs for _ in range(2)],
        *[order(right) if i == 0 else right for i, (_, right) in enumerate(pairs)],
        *([received] if adds else []),
    )
    order.mark(results[0])
    return results


def add_turned_kernel(left, right, out):
    out[...] = add_low(left[...], right[...])


def add_turned(left, right, mask, block):
    rows, width = left.shape
    tile = width
    spec = pl.BlockSpec((block, tile), lambda p, t: (p, t))
    return pl.pallas_call(
        add_turned_kernel,
        out_shape=jax.ShapeDtypeStruct((rows, width), BF16),
        grid=(rows // block, width // tile),
        in_specs=[spec, pl.BlockSpec((block, tile), lambda p, t: (p ^ mask, t))],
        out_specs=spec,
        cost_estimate=lasting(2.5),
        name="add_turned",
    )(left, right)


def finish_kernel(half, tiles, turned, k_ref, *refs):
    out = refs[-1]
    for i, piece in enumerate(refs[:-1]):
        here = pl.program_id(0) // half == i % 2
        if tiles is not None:
            here = here & (pl.program_id(1) // tiles == i // 2)

        @pl.when(here)
        def _():
            value = piece[...].astype(F32)
            value = value.T if turned else value
            out[...] = value.reshape(out.shape)


def finish(place, parts, block, turned=False, groups=1):
    rows, some = parts[0][0].shape
    width = some * len(parts)
    half = rows // block
    if groups > 1:
        tile = width // groups
        shape = (groups, 2 * rows, tile)
        out_spec = pl.BlockSpec((1, block, tile), lambda p, t, k: (t, p ^ k[0], 0))
    elif turned:
        tile = min(1024, some)
        shape = (width, 2 * rows)
        out_spec = pl.BlockSpec((tile, block), lambda p, t, k: (t, p ^ k[0]))
    else:
        tile = min(1024, some)
        shape = (2 * rows, width)
        out_spec = pl.BlockSpec((block, tile), lambda p, t, k: (p ^ k[0], t))
    tiles = some // tile

    def piece_spec(part, side):
        def index(p, t, k):
            return (
                jnp.clip(p - side * half, 0, half - 1),
                jnp.clip(t - part * tiles, 0, tiles - 1),
            )

        return pl.BlockSpec((block, tile), index)

    return pl.pallas_call(
        functools.partial(finish_kernel, half, tiles if len(parts) > 1 else None, turned),
        out_shape=jax.ShapeDtypeStruct(shape, F32),
        grid_spec=pltpu.PrefetchScalarGridSpec(
            num_scalar_prefetch=1,
            grid=(2 * half, width // tile),
            in_specs=[piece_spec(part, side) for part in range(len(parts)) for side in (0, 1)],
            out_specs=out_spec,
        ),
        compiler_params=pltpu.CompilerParams(vmem_limit_bytes=VMEM_BYTES),
        cost_estimate=lasting(8),
        name="finish",
    )(place, *[piece for part in parts for piece in part])


def rotation_tables(positions):
    half = ROT // 2
    exponents = lax.iota(jnp.int32, half).astype(F32) * (2.0 / ROT)
    angles = positions[:, None] * jnp.power(10000.0, -exponents)[None, :]
    cosine, sine = jnp.cos(angles), jnp.sin(angles)
    ones = jnp.ones((positions.shape[0], HD - ROT), F32)
    none = jnp.zeros_like(ones)
    nought = jnp.zeros_like(sine)
    copies = LANES // HD
    return (
        jnp.concatenate([cosine, cosine, ones] * copies, 1),
        jnp.concatenate([-sine, nought, none] * copies, 1),
        jnp.concatenate([nought, sine, none] * copies, 1),
    )


def per_device(
    tokens, ln_gain, ln_bias, w_qkv, b_qkv, w_out, b_out, w_fc1, b_fc1, w_fc2, b_fc2, cotangent
):
    seqs, length, width = tokens.shape
    size = lax.axis_size("context")
    context = lax.axis_index("context")
    shard = lax.axis_index("fsdp")
    tensor_size = lax.axis_size("tensor")
    tensor = lax.axis_index("tensor")
    across = size // 2
    place = (context & 1) * across + context // 2
    me = shard * size + place
    block = width // (2 * size)
    rows = seqs * length
    heads_width = w_out.shape[0]
    heads_local = heads_width // HD
    head_groups = min(heads_local, size)
    seq_groups = size // head_groups
    span = heads_width // head_groups
    direct = seq_groups == 1 and span % LANES == 0 and size == 4
    me_s, place_s, context_s = (jnp.reshape(v, (1,)).astype(jnp.int32) for v in (me, place, context))

    small = (ln_gain, ln_bias, b_out, b_fc2, b_fc1, b_qkv.reshape(-1))
    packed = jnp.concatenate(small)
    other = to_fsdp(packed)
    halves = 2
    units = w_fc1.shape[1] // halves

    def qkv_at(p):
        return lax.dynamic_slice_in_dim(w_qkv, (place ^ p) * block, block, 1)

    def out_at(p):
        return lax.dynamic_slice_in_dim(w_out, (place ^ p) * block, block, 1)

    flat = tokens.reshape(rows, width)
    grad_flat = cotangent.reshape(rows, width)
    both = jnp.where(shard == 0, jnp.stack([packed, other]), jnp.stack([other, packed]))
    both = both.astype(F32)
    vectors = []
    at = 0
    for value in small:
        vectors.append(both[:, at : at + value.size])
        at += value.size
    gain, bias, out_bias, fc2_bias, fc1_bias = (v.reshape(1, -1) for v in vectors[:5])
    qkv_bias = jnp.swapaxes(vectors[5].reshape(2, 3, -1), 0, 1).reshape(3, 1, heads_width)
    normed, grad, bias_sum = prepare(me_s, 2 * size, flat, grad_flat, gain, bias)
    positions = (context * length + lax.iota(jnp.int32, length)).astype(F32)
    tables = rotation_tables(positions)
    bias_sum, *tables = lax.optimization_barrier((bias_sum, *tables))

    order = Order()
    half = across * block
    core = context & 1

    def fc_from(i, *done):
        first = lax.dynamic_slice(w_fc1, (core * half, i * units), (half, units))
        second = lax.dynamic_slice(w_fc2, (i * units, core * half), (units, half))
        return to_fsdp(after(first, *done)), to_fsdp(after(second, *done))

    rest_qkv = [to_fsdp(qkv_at(0))]
    ready = rest_qkv[0]
    rest_out = [to_fsdp(after(out_at(0), ready))]

    def first_from(i, *done):
        part = lax.dynamic_slice(w_fc1, (core * half, i * units), (half, units))
        return to_fsdp(after(part, *done))

    def second_from(i, *done):
        part = lax.dynamic_slice(w_fc2, (i * units, core * half), (units, half))
        return to_fsdp(after(part, *done))

    first_near = [first_from(0, ready)]
    order.mark(bias_sum)
    for mask in masks_of(across):
        rest_qkv = rest_qkv + [to_context(piece, 2 * mask) for piece in rest_qkv]
    waited = order.wait(*rest_qkv, *rest_out)
    rest_qkv, rest_out = list(waited[: len(rest_qkv)]), list(waited[len(rest_qkv) :])
    for mask in masks_of(across):
        rest_out = rest_out + [to_context(piece, 2 * mask) for piece in rest_out]
    rest_qkv = rest_qkv + [to_context(piece, 1) for piece in rest_qkv]
    waited = order.wait(first_near[0], *rest_out)
    first_near[0], rest_out = waited[0], list(waited[1:])
    second_near = [second_from(0, first_near[0])]
    rest_out = rest_out + [to_context(piece, 1) for piece in rest_out]

    near = jnp.concatenate([out_at(p) for p in range(across)] + rest_out[:across], 1)
    near = lax.all_gather(near, "tensor", axis=0, tiled=True)

    pieces = project(
        place_s,
        context_s,
        order(normed),
        grad,
        w_qkv,
        rest_qkv,
        w_out,
        rest_out,
        qkv_bias,
        tables,
        seqs,
        size if direct else 1,
    )
    def send_across(own, beside, across_pair):
        return own, beside, to_context(across_pair, 2)

    def pass_on(own, beside, far_pair):
        (far_pair,) = order.wait(far_pair)
        return [own, to_context(order(beside), 1), far_pair[:1], to_context(far_pair[1:], 1)]

    if direct:
        here = [send_across(*pieces[0])]
    else:
        field = jnp.concatenate([row[0] for row in pieces], 0)

        def part_for(mask):
            target = context ^ mask
            starts = [0] * 4
            sizes = list(field.shape)
            starts[0] = (target // head_groups) * (seqs // seq_groups)
            sizes[0] = seqs // seq_groups
            starts[3] = (target % head_groups) * span
            sizes[3] = span
            return lax.dynamic_slice(field, starts, sizes)

        here = [[part_for(0)] + [to_context(part_for(m), m) for m in range(1, size)]]

    order.mark(pieces[0][0])

    sums = ()
    fed_parts = []
    back = []

    def feed_part(i, sums):
        first, second = first_near[i], second_near[i]
        hidden, pre_grad, pre_sum, *sums = feed(
            place_s,
            block,
            order(normed),
            grad,
            fc1_bias,
            w_fc1,
            [first, to_context(first, 1)],
            w_fc2,
            [second, to_context(second, 1)],
            i,
            tuple(sums),
        )
        fed_parts.append((hidden, pre_grad, order.mark(pre_sum)))
        return sums

    rows_here = list(here)
    for i in range(max(halves, len(pieces) if direct else 1)):
        if i < halves:
            (second_near[i],) = order.wait(second_near[i])
            if i + 1 < halves:
                first_near.append(first_from(i + 1, second_near[i]))
            sums = feed_part(i, sums)
            if i + 1 < halves:
                (first_near[i + 1],) = order.wait(first_near[i + 1])
                second_near.append(second_from(i + 1, first_near[i + 1]))
        if i == halves - 1:
            fed, fed_back = sums
            fed_share = lax.psum_scatter(fed, "tensor", scatter_dimension=0, tiled=True)
            fc_sums = [
                Reduction(order, ((normed, part[1]), (grad, part[0])), block)
                for part in fed_parts
            ]
            fc_sums[0].send()
        if i < len(here):
            if direct and i == 0:
                rows_here = [pass_on(*here[0])]
                for own, beside, across_pair in pieces[1:]:
                    across_pair = after(order(across_pair), here[-1][2])
                    here.append(send_across(own, beside, across_pair))
            row = rows_here[i]
            result = attend(context_s, [order(row[0])] + row[1:], direct)
            order.mark(result[0])
            if direct:
                back.append(send_across(*result))
                if i + 1 < len(here):
                    rows_here.append(pass_on(*here[i + 1]))
            else:
                back.append(
                    [result[0]] + [to_context(result[m], m) for m in range(1, size)]
                )
    if not direct:
        stacked = jnp.stack(back[0])
        sources = lax.iota(jnp.int32, size) ^ context
        ordered = jnp.take(stacked, sources, axis=0)
        ordered = ordered.reshape(seq_groups, head_groups, seqs // seq_groups, 4, length, span)
        ordered = jnp.transpose(ordered, (0, 2, 3, 4, 1, 5))
        ordered = ordered.reshape(seqs, 4, length, heads_width)
        back = [[ordered[s : s + 1]] for s in range(seqs)]

    def through(s, unturned, norm_terms):
        row = [order(back[s][0])] + back[s][1:]
        *unturned, part_sum = unturn(context_s, row, tables, s, rows, tuple(unturned))
        norm_terms = norm_back(
            place_s, unturned[1], fed_back, w_qkv, rest_qkv, s, seqs, tuple(norm_terms)
        )
        order.mark(norm_terms)
        return unturned, [norm_terms], part_sum

    first_sum, second_sum = fc_sums
    if direct:
        back[0] = pass_on(*back[0])
    first_sum.keep()
    first_sum.over_fsdp(0)
    unturned = []
    norm_terms = ()
    qkv_bias_sum = 0.0
    for s in range(seqs):
        if direct and s:
            back[s] = pass_on(*back[s])
        unturned, norm_terms, part_sum = through(s, unturned, norm_terms)
        qkv_bias_sum = qkv_bias_sum + part_sum
    merged, raw_grad = unturned
    norm_share = lax.psum_scatter(norm_terms[0], "tensor", scatter_dimension=0, tiled=True)
    share = rows // tensor_size

    def rows_for(mask):
        return lax.dynamic_slice_in_dim(merged, (tensor ^ mask) * share, share, 0)

    def arrived(*values):
        return order.wait(*values)

    heads_from = [rows_for(0)] + [to_tensor(rows_for(m), m) for m in range(1, tensor_size)]
    last_sum = Reduction(order, ((grad, merged), (normed, raw_grad)), block)
    (first_sum.far[0],) = arrived(first_sum.far[0])
    first_sum.over_fsdp(1, first_sum.far[0])
    first_sum.over_chips(0)
    second_sum.send()
    far = to_context(order(near), 1)
    heads_from[1:] = arrived(*heads_from[1:])

    def in_order(blocks):
        return jnp.concatenate(own_blocks(blocks, 1, me, block), 1).astype(F32)

    inputs = lax.dynamic_slice_in_dim(flat, tensor * share, share, 0).astype(F32)
    all_heads = jnp.zeros((share, tensor_size * heads_width), BF16)
    for m in range(tensor_size):
        all_heads = lax.dynamic_update_slice_in_dim(
            all_heads, order(heads_from[m]), (tensor ^ m) * heads_width, 1
        )
    near_part, far_part = nn(all_heads, near), nn(all_heads, far)
    attended = [near_part[:, :half], far_part[:, :half], near_part[:, half:], far_part[:, half:]]
    branch_sum = in_order(jnp.concatenate(attended, 1) + fed_share.astype(F32))
    block_out = (inputs + branch_sum + out_bias + fc2_bias).astype(BF16)
    order.mark(block_out)
    block_out = lax.all_gather(block_out, "tensor", axis=0, tiled=True).reshape(tokens.shape)
    second_sum.keep()
    first_sum.far[1], first_sum.far[0] = arrived(first_sum.far[1], first_sum.far[0])
    second_sum.over_fsdp(0, first_sum.far[1])
    first_sum.over_chips(1)
    first_sum.over_cores(0)

    normed_grad = in_order(order(norm_share))
    centered = inputs - jnp.mean(inputs, -1, keepdims=True)
    root = lax.rsqrt(jnp.mean(centered * centered, -1, keepdims=True) + EPSILON)
    unit = centered * root
    scaled = normed_grad * gain
    inner = jnp.mean(scaled * unit, -1, keepdims=True)
    input_part = root * (scaled - jnp.mean(scaled, -1, keepdims=True) - unit * inner)
    grad_share = lax.dynamic_slice_in_dim(grad_flat, tensor * share, share, 0).astype(F32)
    tokens_grad = (grad_share + input_part).astype(BF16)
    norm_sums = jnp.stack([jnp.sum(normed_grad * unit, 0), jnp.sum(normed_grad, 0)])
    order.mark(norm_sums)
    order.mark(tokens_grad)
    tokens_grad = lax.all_gather(tokens_grad, "tensor", axis=0, tiled=True).reshape(tokens.shape)

    second_sum.far[0], first_sum.far[1] = arrived(second_sum.far[0], first_sum.far[1])
    second_sum.over_fsdp(1, second_sum.far[0])
    second_sum.over_chips(0)
    last_sum.send()
    first_sum.over_cores(1)
    last_sum.keep()
    second_sum.far[1], second_sum.far[0] = arrived(second_sum.far[1], second_sum.far[0])
    last_sum.over_fsdp(1, second_sum.far[1])
    second_sum.over_chips(1)
    second_sum.over_cores(0)
    fc1_grad = order.mark(
        finish(place_s, [first_sum.pieces[0], second_sum.pieces[0]], block)
    )
    last_sum.far[1], second_sum.far[1] = arrived(last_sum.far[1], second_sum.far[1])
    last_sum.over_fsdp(0, last_sum.far[1])
    last_sum.over_chips(1)
    second_sum.over_cores(1)
    fc2_grad = order.mark(
        finish(place_s, [first_sum.pieces[1], second_sum.pieces[1]], block, turned=True)
    )
    (last_sum.far[0],) = arrived(last_sum.far[0])
    last_sum.over_chips(0)
    last_sum.over_cores(1)
    qkv_grad = order.mark(finish(place_s, [last_sum.pieces[1]], block, groups=3))
    last_sum.over_cores(0)
    out_grad = order.mark(finish(place_s, [last_sum.pieces[0]], block, turned=True))

    units_here = b_fc1.shape[0] * 2
    small_sums = [norm_sums.reshape(1, -1), bias_sum] + [part[2] for part in fed_parts]
    small_sums = jnp.concatenate(small_sums + [qkv_bias_sum], 1)
    small_sums = sum_everywhere(after(small_sums, fc1_grad), False)[0]
    norm_sums = small_sums[: 2 * width].reshape(2, width)
    for mask in masks_of(tensor_size):
        norm_sums = norm_sums + to_tensor(norm_sums, mask)
    other_sums = small_sums[2 * width :]

    def shard_of(value):
        part = value.shape[-1] // 2
        return lax.dynamic_slice_in_dim(value, shard * part, part, value.ndim - 1)

    out_bias_grad = shard_of(other_sums[:width])
    fc1_bias_grad = shard_of(other_sums[width : width + units_here])
    qkv_bias_grad = shard_of(other_sums[width + units_here :].reshape(3, heads_width))
    return (
        block_out,
        tokens_grad,
        shard_of(norm_sums[0]),
        shard_of(norm_sums[1]),
        qkv_grad,
        qkv_bias_grad,
        out_grad,
        out_bias_grad,
        fc1_grad,
        fc1_bias_grad,
        fc2_grad,
        out_bias_grad,
    )


def solution(mesh):
    return jax.shard_map(
        per_device,
        mesh=mesh,
        in_specs=(
            P("fsdp", "context", None),
            P("fsdp"),
            P("fsdp"),
            P(None, "fsdp", "tensor"),
            P(None, ("tensor", "fsdp")),
            P("tensor", "fsdp"),
            P("fsdp"),
            P("fsdp", "tensor"),
            P(("tensor", "fsdp")),
            P("tensor", "fsdp"),
            P("fsdp"),
            P("fsdp", "context", None),
        ),
        out_specs=(
            P("fsdp", "context", None),
            P("fsdp", "context", None),
            P("fsdp"),
            P("fsdp"),
            P(None, "fsdp", "tensor"),
            P(None, ("tensor", "fsdp")),
            P("tensor", "fsdp"),
            P("fsdp"),
            P("fsdp", "tensor"),
            P(("tensor", "fsdp")),
            P("tensor", "fsdp"),
            P("fsdp"),
        ),
        check_vma=False,
    )
```

time: 1690 us -> 601 us (0.36)
  waiting for transfers between devices: 998 us -> 148 us
  Pallas kernels: 0 us -> 285 us
  matrix products: 248 us -> 6.97 us
  local copies, waits for them, and re-layouts: 190 us -> 50.7 us
  blocking collectives: 116 us -> 0 us
  other arithmetic: 86.9 us -> 22.8 us
  starting transfers between devices: 12 us -> 63.9 us
  loops' own time: 23.1 us -> 0 us
    psum x1 -> x0, waiting for transfers between devices: 567 us -> none  [per_device(): combined = lax.psum(branch_terms, 'tensor')]
    pallas_call x0 -> x26, Pallas kernels: none -> 285 us  [the longest x6 67.1 us: outer(): pl.pallas_call(functools.partial(outer_kernel, steps, int(adds)), out_sha...]
    dot_general x124 -> x2, matrix products: 248 us -> 6.97 us  [nn(): lax.dot_general(a, b, (((1,), (0,)), ((), ())), preferred_element_type=F32)]
    reduce_scatter x4 -> x2, waiting for transfers between devices: 211 us -> 0.31 us  [the longest x1 0.29 us: per_device(): lax.psum_scatter(norm_terms[0], 'tensor', scatter_dimension=0, tiled=True)]
    all_gather x8 -> x3, waiting for transfers between devices: 164 us -> 0.01 us  [the longest x1 0.01 us: per_device(): near = lax.all_gather(near, 'tensor', axis=0, tiled=True)]
    ppermute x0 -> x59, waiting for transfers between devices: none -> 147 us  [the longest x40 66.2 us: to_context(): return lax.ppermute(value, 'context', [(i, i ^ mask) for i in range(size)])]
    ppermute x0 -> x59, starting transfers between devices: none -> 63.7 us  [the longest x5 28 us: to_tensor(): return lax.ppermute(value, 'tensor', [(i, i ^ mask) for i in range(size)])]
    all_gather x11 -> x0, blocking collectives: 52.4 us -> none  [the longest x1 5.39 us: per_device(): lax.all_gather(ln_gain, 'fsdp', axis=0, tiled=True)]
  transfers between devices with their start and end apart: 17 -> 64, of which waited for: 10 -> 36; matrix products, arithmetic and copies ran while one was open for 30% -> 10% of each run, Pallas kernels for 0% -> 47%
where the time goes in v1:
time: 601 us; the launch traced here: 593 us
  Pallas kernels  285 us (47%)
  waiting for transfers between devices  148 us (25%)
  starting transfers between devices  63.9 us (11%)
  local copies, waits for them, and re-layouts  50.7 us (8%)
  other arithmetic  22.8 us (4%)
  between operations  15.1 us (3%)
  matrix products  6.97 us (1%)
    pallas_call x6, Pallas kernels, outer(): pl.pallas_call(functools.partial(outer_kernel, steps, int(adds)), out_sha...  67.1 us
    ppermute x40, waiting for transfers between devices, to_context(): return lax.ppermute(value, 'context', [(i, i ^ mask) for i in range(size)])  66.2 us
    pallas_call x2, Pallas kernels, feed(): pl.pallas_call(functools.partial(feed_kernel, len(first), len(second), le...  61.8 us
    pallas_call x2, Pallas kernels, attend(): pl.pallas_call(functools.partial(attend_kernel, parts, bq, bk), out_shape...  56.5 us
    ppermute x14, waiting for transfers between devices, to_fsdp(): return lax.ppermute(value, 'fsdp', [(0, 1), (1, 0)])  43.7 us
    ppermute x5, waiting for transfers between devices, to_tensor(): return lax.ppermute(value, 'tensor', [(i, i ^ mask) for i in range(size)])  37.5 us
    pallas_call x4, Pallas kernels, finish(): pl.pallas_call(functools.partial(finish_kernel, half, tiles if len(parts)...  29.9 us
    unnamed x136, local copies, waits for them, and re-layouts  29 us
  transfers between devices with their start and end apart: 64, of which 36 were waited for; matrix products, arithmetic and copies ran while one was open for 10% of the time, Pallas kernels for 47%

profile of v1, /device:TPU:0, one launch (start us, length us, event | category | flops | bytes accessed | tf_op | source)
XLA Modules:
  0.0 592.5 jit_solution(11964750333817556537)
XLA Ops:
  7.2 2.1 constant_dynamic-slice_fusion.12
  9.3 3.0 collective-permute-start.1
  16.5 3.1 constant_dynamic-slice_fusion.14
  24.2 6.1 %collective-permute-done = bf16[5888]{0:T(1024)(128)(2,1)S(1)} collective-permute-done((bf16[5888]{0:T(1024)(128)(2,1)S(1)}, bf16[5888]{0:T(1024)(128)(2,1)S(1)}, u32[]{:S(2)}, u32[]{:S(2)}) %collective-permute-start) | collective-permute-done | bytes 11808 | tf_op jit(solution)/shard_map/ppermute | solution.py:45
  35.5 10.5 %prepare.1 = (bf16[1024,2048]{1,0:T(8,128)(2,1)}, bf16[1024,2048]{1,0:T(8,128)(2,1)}, f32[1,2048]{1,0:T(1,128)}) custom-call(s32[1]{0:T(128)} %bitcast.3.me_ref, bf16[1024,2048]{1,0:T(8,128)(2,1)} %bitcast.47, bf16[1024,2048]{1,0:T(8,128)(2,1)} %bitcast.52, f32[1,2048]{1,0:T(1,128)} %bitcast.64, f32[1,2048]{1,0:T(1,128)} %bitcast.65), custom_call_target="tpu_custom_call" | custom-call | bytes 34000000 | tf_op jit(solution)/shard_map/prepare/pallas_call | solution.py:166
  46.0 4.6 collective-permute-done.3.refs_11_.refs_5_
  52.0 5.0 collective-permute-done.5.refs_19_
  57.0 3.4 collective-permute-done.2.refs_7_.refs_8_
  61.8 3.0 constant_dynamic-slice_fusion.15
  71.2 19.5 %project.1 = (bf16[1,4,512,128]{3,2,1,0:T(8,128)(2,1)}, bf16[1,4,512,128]{3,2,1,0:T(8,128)(2,1)}, bf16[2,4,512,128]{3,2,1,0:T(8,128)(2,1)}, bf16[1,4,512,128]{3,...) custom-call(s32[1]{0:T(128)} %bitcast.2.k_ref, s32[1]{0:T(128)} %bitcast.1.c_ref.me_ref, ...), custom_call_target="tpu_custom_call" | custom-call | bytes 64600000 | tf_op jit(solution)/shard_map/project/pallas_call | solution.py:259
  94.9 29.9 %feed.2 = (bf16[1024,1024]{1,0:T(8,128)(2,1)}, bf16[1024,1024]{1,0:T(8,128)(2,1)}, f32[1,1024]{1,0:T(1,128)}, bf16[1024,2048]{1,0:T(8,128)(2,1)}, bf16[1024,2048]{1,0:T(8,128)(2,1)}) custom-call(s32[1]{0:T(128)} %bitcast.2.k_ref, bf16[1024,2048]{1,0:T(8,128)(2,1)} %get-tuple-element.170.refs_0_.refs_1_.refs_2_.refs_3_, ...), custom_call_target="tpu_custom_call" | custom-call | bytes 105400000 | tf_op jit(solution)/shard_map/feed/pallas_call | solution.py:585
  130.8 28.1 %attend.2 = (bf16[1,4,512,128]{3,2,1,0:T(8,128)(2,1)}, bf16[1,4,512,128]{3,2,1,0:T(8,128)(2,1)}, bf16[2,4,512,128]{3,2,1,0:T(8,128)(2,1)}) custom-call(s32[1]{0:T(128)} %bitcast.1.c_ref.me_ref, bf16[1,4,512,128]{3,2,1,0:T(8,128)(2,1)} %get-tuple-element.164.refs_0_, bf16[1,4,512,128]{3,2,1,0:T(8,128)(2,1)} %copy-done.36, ...), custom_call_target="tpu_custom_call" | custom-call | bytes 95200000 | tf_op jit(solution)/shard_map/attend/pallas_call | solution.py:401
  159.4 2.3 collective-permute-done.20.refs_17_.refs_18_
  162.7 31.9 %feed.3 = (bf16[1024,1024]{1,0:T(8,128)(2,1)}, bf16[1024,1024]{1,0:T(8,128)(2,1)}, f32[1,1024]{1,0:T(1,128)}, bf16[1024,2048]{1,0:T(8,128)(2,1)}, bf16[1024,2048]{1,0:T(8,128)(2,1)}) custom-call(s32[1]{0:T(128)} %bitcast.2.k_ref, bf16[1024,2048]{1,0:T(8,128)(2,1)} %get-tuple-element.170.refs_0_.refs_1_.refs_2_.refs_3_, ...), custom_call_target="tpu_custom_call" | custom-call | bytes 105400000 | tf_op jit(solution)/shard_map/feed/pallas_call | solution.py:585
  194.7 10.4 %outer.6 = bf16[2,512,2048]{2,1,0:T(8,128)(2,1)} custom-call(bf16[1024,2048]{1,0:T(8,128)(2,1)} %get-tuple-element.170.refs_0_.refs_1_.refs_2_.refs_3_, bf16[1024,2048]{1,0:T(8,128)(2,1)} %get-tuple-element.170.refs_0_.refs_1_.refs_2_.refs_3_, bf16[1024,2048]{1,0:T(8,128)(2,1)} %get-tuple-element.142.refs_1_.refs_2_.refs_3_.refs_0_, ...), custom_call_target="tpu_custom_call" | custom-call | bytes 37400000 | tf_op jit(solution)/shard_map/outer/pallas_call | solution.py:679
  206.6 2.1 fusion.22
  209.2 3.8 collective-permute-done.21.refs_1_
  214.5 28.4 %attend.3 = (bf16[1,4,512,128]{3,2,1,0:T(8,128)(2,1)}, bf16[1,4,512,128]{3,2,1,0:T(8,128)(2,1)}, bf16[2,4,512,128]{3,2,1,0:T(8,128)(2,1)}) custom-call(s32[1]{0:T(128)} %bitcast.1.c_ref.me_ref, bf16[1,4,512,128]{3,2,1,0:T(8,128)(2,1)} %get-tuple-element.176.refs_0_, bf16[1,4,512,128]{3,2,1,0:T(8,128)(2,1)} %copy-done.37, ...), custom_call_target="tpu_custom_call" | custom-call | bytes 95200000 | tf_op jit(solution)/shard_map/attend/pallas_call | solution.py:401
  245.4 11.5 %outer.7 = (bf16[512,1024]{1,0:T(8,128)(2,1)}, bf16[512,1024]{1,0:T(8,128)(2,1)}, bf16[512,1024]{1,0:T(8,128)(2,1)}, bf16[512,1024]{1,0:T(8,128)(2,1)}) custom-call(bf16[1024,2048]{1,0:T(8,128)(2,1)} %get-tuple-element.170.refs_0_.refs_1_.refs_2_.refs_3_, bf16[1024,2048]{1,0:T(8,128)(2,1)} %get-tuple-element.170.refs_0_.refs_1_.refs_2_.refs_3_, ...), custom_call_target="tpu_custom_call" | custom-call | bytes 37400000 | tf_op jit(solution)/shard_map/outer/pallas_call | solution.py:679
  258.0 4.2 unturn.2
  262.2 8.1 %norm_back.2.refs_8_ = bf16[1024,2048]{1,0:T(8,128)(2,1)} custom-call(s32[1]{0:T(128)} %bitcast.2.k_ref, bf16[1024,1536]{1,0:T(8,128)(2,1)} %get-tuple-element.188.raw.refs_8_, bf16[1024,2048]{1,0:T(8,128)(2,1)} %get-tuple-element.189.back, bf16[3,1024,512]{2,1,0:T(8,128)(2,1)} %refs_3_.7, bf16[3,1024,512]{2,1,0:T(8,128)(2,1)} %refs_3_.7, ...), custom_call_target="tpu_custom_call" | custom-call | bytes 27200000 | tf_op jit(solution)/shard_map/norm_back/pallas_call | solution.py:499
  274.6 4.2 unturn.3
  278.8 8.1 %norm_back.3 = bf16[1024,2048]{1,0:T(8,128)(2,1)} custom-call(s32[1]{0:T(128)} %bitcast.2.k_ref, bf16[1024,1536]{1,0:T(8,128)(2,1)} %get-tuple-element.198.raw.refs_5_, bf16[1024,2048]{1,0:T(8,128)(2,1)} %get-tuple-element.189.back, bf16[3,1024,512]{2,1,0:T(8,128)(2,1)} %refs_3_.7, bf16[3,1024,512]{2,1,0:T(8,128)(2,1)} %refs_3_.7, ...), custom_call_target="tpu_custom_call", output_to_operand_aliasing={{}: (11, {})} | custom-call | bytes 27200000 | tf_op jit(solution)/shard_map/norm_back/pallas_call | solution.py:499
  286.9 10.2 %collective-permute-done.33 = bf16[512,1024]{1,0:T(8,128)(2,1)S(1)} collective-permute-done((bf16[512,1024]{1,0:T(8,128)(2,1)S(1)}, bf16[512,1024]{1,0:T(8,128)(2,1)S(1)}, u32[]{:S(2)}, u32[]{:S(2)}) %collective-permute-start.33) | collective-permute-done | bytes 1048608 | tf_op jit(solution)/shard_map/ppermute | solution.py:45
  297.5 10.9 %outer.8 = bf16[2,512,2048]{2,1,0:T(8,128)(2,1)} custom-call(bf16[1024,2048]{1,0:T(8,128)(2,1)} %get-tuple-element.170.refs_0_.refs_1_.refs_2_.refs_3_, bf16[1024,2048]{1,0:T(8,128)(2,1)} %get-tuple-element.170.refs_0_.refs_1_.refs_2_.refs_3_, bf16[1024,2048]{1,0:T(8,128)(2,1)} %get-tuple-element.142.refs_1_.refs_2_.refs_3_.refs_0_, ...), custom_call_target="tpu_custom_call" | custom-call | bytes 37400000 | tf_op jit(solution)/shard_map/outer/pallas_call | solution.py:679
  312.1 2.7 collective-permute-start.31
  315.0 21.8 %collective-permute-done.30 = bf16[256,512]{1,0:T(8,128)(2,1)S(1)} collective-permute-done((bf16[256,512]{1,0:T(8,128)(2,1)S(1)}, bf16[256,512]{1,0:T(8,128)(2,1)S(1)}, u32[]{:S(2)}, u32[]{:S(2)}) %collective-permute-start.30) | collective-permute-done | bytes 262176 | tf_op jit(solution)/shard_map/ppermute | solution.py:55
  336.8 5.2 collective-permute-done.31
  342.0 7.6 %collective-permute-done.32 = bf16[256,512]{1,0:T(8,128)(2,1)S(1)} collective-permute-done((bf16[256,512]{1,0:T(8,128)(2,1)S(1)}, bf16[256,512]{1,0:T(8,128)(2,1)S(1)}, u32[]{:S(2)}, u32[]{:S(2)}) %collective-permute-start.32) | collective-permute-done | bytes 262176 | tf_op jit(solution)/shard_map/ppermute | solution.py:55
  350.6 3.5 fusion.26
  354.2 3.5 fusion.27
  359.6 2.8 fusion.10
  362.4 11.4 %outer.9 = (bf16[512,1024]{1,0:T(8,128)(2,1)}, bf16[512,1024]{1,0:T(8,128)(2,1)}, bf16[512,1024]{1,0:T(8,128)(2,1)}, bf16[512,1024]{1,0:T(8,128)(2,1)}) custom-call(bf16[1024,2048]{1,0:T(8,128)(2,1)} %get-tuple-element.170.refs_0_.refs_1_.refs_2_.refs_3_, bf16[1024,2048]{1,0:T(8,128)(2,1)} %get-tuple-element.170.refs_0_.refs_1_.refs_2_.refs_3_, ...), custom_call_target="tpu_custom_call" | custom-call | bytes 37400000 | tf_op jit(solution)/shard_map/outer/pallas_call | solution.py:679
  378.0 2.7 add_turned.6.refs_0_
  388.4 2.3 fusion.15
  390.7 3.5 fusion.9
  394.2 6.5 %collective-permute-done.39 = bf16[512,1024]{1,0:T(8,128)(2,1)S(1)} collective-permute-done((bf16[512,1024]{1,0:T(8,128)(2,1)}, bf16[512,1024]{1,0:T(8,128)(2,1)S(1)}, u32[]{:S(2)}, u32[]{:S(2)}) %collective-permute-start.39) | collective-permute-done | bytes 1048608 | tf_op jit(solution)/shard_map/ppermute | solution.py:45
  401.7 2.5 add_convert_fusion.2.left
  404.2 11.3 %outer.10 = bf16[2,512,2048]{2,1,0:T(8,128)(2,1)} custom-call(bf16[1024,2048]{1,0:T(8,128)(2,1)} %get-tuple-element.142.refs_1_.refs_2_.refs_3_.refs_0_, bf16[1024,2048]{1,0:T(8,128)(2,1)} %get-tuple-element.142.refs_1_.refs_2_.refs_3_.refs_0_, bf16[1024,2048]{1,0:T(8,128)(2,1)} %get-tuple-element.170.refs_0_.refs_1_.refs_2_.refs_3_, ...), custom_call_target="tpu_custom_call" | custom-call | bytes 37400000 | tf_op jit(solution)/shard_map/outer/pallas_call | solution.py:679
  417.6 2.5 add_turned.7.refs_0_
  420.1 3.0 collective-permute-done.43.refs_6_
  423.0 11.6 %outer.11 = (bf16[512,512]{1,0:T(8,128)(2,1)}, bf16[512,1536]{1,0:T(8,128)(2,1)}, bf16[512,512]{1,0:T(8,128)(2,1)}, bf16[512,1536]{1,0:T(8,128)(2,1)}) custom-call(bf16[1024,2048]{1,0:T(8,128)(2,1)} %get-tuple-element.142.refs_1_.refs_2_.refs_3_.refs_0_, bf16[1024,2048]{1,0:T(8,128)(2,1)} %get-tuple-element.142.refs_1_.refs_2_.refs_3_.refs_0_, ...), custom_call_target="tpu_custom_call" | custom-call | bytes 37400000 | tf_op jit(solution)/shard_map/outer/pallas_call | solution.py:679
  434.6 6.8 %collective-permute-done.41 = bf16[512,1024]{1,0:T(8,128)(2,1)} collective-permute-done((bf16[512,1024]{1,0:T(8,128)(2,1)}, bf16[512,1024]{1,0:T(8,128)(2,1)}, u32[]{:S(2)}, u32[]{:S(2)}) %collective-permute-start.41) | collective-permute-done | bytes 1048608 | tf_op jit(solution)/shard_map/ppermute | solution.py:45
  444.6 2.8 add_turned.8.refs_2_
  448.7 1.9 collective-permute-done.44.refs_3_
  450.6 8.1 %finish.4 = f32[1024,2048]{1,0:T(8,128)} custom-call(s32[1]{0:T(128)} %bitcast.2.k_ref, bf16[512,1024]{1,0:T(8,128)(2,1)} %add_turned.6.refs_0_, bf16[512,1024]{1,0:T(8,128)(2,1)} %collective-permute-done.38.refs_1_, bf16[512,1024]{1,0:T(8,128)(2,1)} %add_turned.8.refs_2_, bf16[512,1024]{1,0:T(8,128)(2,1)} %collective-permute-done.44.refs_3_), custom_call_target="tpu_custom_call" | custom-call | bytes 27200000 | tf_op jit(solution)/shard_map/finish/pallas_call | solution.py:760
  458.7 14.3 %collective-permute-done.51.right = bf16[512,1024]{1,0:T(8,128)(2,1)S(1)} collective-permute-done((bf16[512,1024]{1,0:T(8,128)(2,1)S(1)}, bf16[512,1024]{1,0:T(8,128)(2,1)S(1)}, u32[]{:S(2)}, u32[]{:S(2)}) %collective-permute-start.51) | collective-permute-done | bytes 1048608 | tf_op jit(solution)/shard_map/ppermute | solution.py:50
  473.0 4.7 collective-permute-done.50
  477.7 2.4 add_convert_fusion.left
  481.3 2.4 add_turned.9.refs_2_
  486.9 8.8 %finish.5 = f32[2048,1024]{1,0:T(8,128)} custom-call(s32[1]{0:T(128)} %bitcast.2.k_ref, bf16[512,1024]{1,0:T(8,128)(2,1)} %add_turned.7.refs_0_, bf16[512,1024]{1,0:T(8,128)(2,1)} %collective-permute-done.53.refs_1_, bf16[512,1024]{1,0:T(8,128)(2,1)} %add_turned.9.refs_2_, bf16[512,1024]{1,0:T(8,128)(2,1)} %collective-permute-done.54.refs_3_), custom_call_target="tpu_custom_call" | custom-call | bytes 27200000 | tf_op jit(solution)/shard_map/finish/pallas_call | solution.py:760
  495.6 2.8 collective-permute-done.52
  498.6 16.5 %collective-permute-done.55.right = bf16[512,1536]{1,0:T(8,128)(2,1)} collective-permute-done((bf16[512,1536]{1,0:T(8,128)(2,1)S(1)}, bf16[512,1536]{1,0:T(8,128)(2,1)}, u32[]{:S(2)}, u32[]{:S(2)}) %collective-permute-start.55) | collective-permute-done | bytes 1572896 | tf_op jit(solution)/shard_map/ppermute | solution.py:50
  515.1 2.9 add_turned.10.refs_0_
  518.6 2.5 collective-permute-done.45
  522.3 2.9 collective-permute-done.46
  526.4 2.9 collective-permute-done.47
  530.5 16.7 %collective-permute-start.48 = (f32[2,2048]{1,0:T(2,128)S(1)}, f32[2,2048]{1,0:T(2,128)S(1)}, u32[]{:S(2)}, u32[]{:S(2)}) collective-permute-start(f32[2,2048]{1,0:T(2,128)S(1)} %reshape.134), channel_id=1, source_target_pairs={{0,1},{1,0},{2,3},{3,2},{4,5},{5,4},{6,7},{7,6},{8,9},{9,8},{10,11... | collective-permute-start | bytes 49160 | tf_op jit(solution)/shard_map/ppermute | solution.py:55
  549.3 6.8 %collective-permute-start.49 = (f32[2,2048]{1,0:T(2,128)S(1)}, f32[2,2048]{1,0:T(2,128)S(1)}, u32[]{:S(2)}, u32[]{:S(2)}) collective-permute-start(f32[2,2048]{1,0:T(2,128)S(1)} %add.220), channel_id=1, source_target_pairs={{0,2},{1,3},{2,0},{3,1},{4,6},{5,7},{6,4},{7,5},{8,10},{9,11},{10,... | collective-permute-start | bytes 49160 | tf_op jit(solution)/shard_map/ppermute | solution.py:55
  559.3 9.2 %finish.6 = f32[3,1024,512]{2,1,0:T(8,128)} custom-call(s32[1]{0:T(128)} %bitcast.2.k_ref, bf16[512,1536]{1,0:T(8,128)(2,1)} %add_turned.10.refs_0_, bf16[512,1536]{1,0:T(8,128)(2,1)} %copy-done.21), custom_call_target="tpu_custom_call" | custom-call | bytes 27200000 | tf_op jit(solution)/shard_map/finish/pallas_call | solution.py:760
  569.3 2.0 add_turned.11.refs_0_
  574.2 3.8 finish.7
  578.6 4.9 copy.76
  583.6 2.0 copy.77
  (304 shorter events, 90.6 us)
Async XLA Ops:
  7.2 301.2 %all-gather.4.cloned.1.call-start = ((), (), s32[]{:S(2)}) async-start(), calls=%async_computation.2 | async-start | bytes 5242880 | tf_op jit(solution)/shard_map/all_gather | solution.py:877
  9.3 21.0 %collective-permute-start.1 = (bf16[3,256,512]{2,1,0:T(8,128)(2,1)}, bf16[3,256,512]{2,1,0:T(8,128)(2,1)S(1)}, u32[]{:S(2)}, u32[]{:S(2)}) collective-permute-start(bf16[3,256,512]{2,1,0:T(8,128)(2,1)} %constant_dynamic-slice_fusion.12), channel_id=1, source_target_pairs={{0,16},{16,0},{1,17},{17,1},{2,18},{18,2},{3,19},{19,3},{4,20},{20... | collective-permute-start | bytes 2359304 | tf_op jit(solution)/shard_map/ppermute | solution.py:45
  16.4 13.9 %collective-permute-start = (bf16[5888]{0:T(1024)(128)(2,1)S(1)}, bf16[5888]{0:T(1024)(128)(2,1)S(1)}, u32[]{:S(2)}, u32[]{:S(2)}) collective-permute-start(bf16[5888]{0:T(1024)(128)(2,1)S(1)} %constant_dynamic-update-slice_fusion.12), channel_id=1, source_target_pairs={{0,16},{16,0},{1,17},{17,1},{2,18},{18,2},{3,19},{19,3},{4,20},{20... | collective-permute-start | bytes 35336 | tf_op jit(solution)/shard_map/ppermute | solution.py:45
  30.3 15.7 %collective-permute-start.4 = (bf16[512,256]{1,0:T(8,128)(2,1)S(1)}, bf16[512,256]{1,0:T(8,128)(2,1)S(1)}, u32[]{:S(2)}, u32[]{:S(2)}) collective-permute-start(bf16[512,256]{1,0:T(8,128)(2,1)S(1)} %get-tuple-element.135), channel_id=1, source_target_pairs={{0,16},{16,0},{1,17},{17,1},{2,18},{18,2},{3,19},{19,3},{4,20},{20... | collective-permute-start | bytes 786440 | tf_op jit(solution)/shard_map/ppermute | solution.py:45
  32.2 28.2 %collective-permute-start.2 = (bf16[512,1024]{1,0:T(8,128)(2,1)}, bf16[512,1024]{1,0:T(8,128)(2,1)S(1)}, u32[]{:S(2)}, u32[]{:S(2)}) collective-permute-start(bf16[512,1024]{1,0:T(8,128)(2,1)} %get-tuple-element.134), channel_id=1, source_target_pairs={{0,16},{16,0},{1,17},{17,1},{2,18},{18,2},{3,19},{19,3},{4,20},{20... | collective-permute-start | bytes 3145736 | tf_op jit(solution)/shard_map/ppermute | solution.py:45
  32.4 18.2 %collective-permute-start.3 = (bf16[3,256,512]{2,1,0:T(8,128)(2,1)S(1)}, bf16[3,256,512]{2,1,0:T(8,128)(2,1)S(1)}, u32[]{:S(2)}, u32[]{:S(2)}) collective-permute-start(bf16[3,256,512]{2,1,0:T(8,128)(2,1)S(1)} %collective-permute-done.1.refs_10_.refs_4_), channel_id=1, source_target_pairs={{0,8},{4,12},{8,0},{12,4},{1,9},{5,13},{9,1},{13,5},{2,10},{6,14},... | collective-permute-start | bytes 2359304 | tf_op jit(solution)/shard_map/ppermute | solution.py:50
  50.6 6.4 %collective-permute-start.5 = (bf16[512,256]{1,0:T(8,128)(2,1)S(1)}, bf16[512,256]{1,0:T(8,128)(2,1)S(1)}, u32[]{:S(2)}, u32[]{:S(2)}) collective-permute-start(bf16[512,256]{1,0:T(8,128)(2,1)S(1)} %collective-permute-done.4.refs_18_), channel_id=1, source_target_pairs={{0,8},{4,12},{8,0},{12,4},{1,9},{5,13},{9,1},{13,5},{2,10},{6,14},... | collective-permute-start | bytes 786440 | tf_op jit(solution)/shard_map/ppermute | solution.py:50
  61.7 296.1 %reduce-scatter.3.cloned.1.call-start = ((), (), s32[]{:S(2)}) async-start(), calls=%async_computation.3 | async-start | bytes 5242880 | tf_op jit(solution)/shard_map/reduce_scatter | solution.py:953
  64.8 26.0 %collective-permute-start.10 = (bf16[1024,512]{1,0:T(8,128)(2,1)}, bf16[1024,512]{1,0:T(8,128)(2,1)}, u32[]{:S(2)}, u32[]{:S(2)}) collective-permute-start(bf16[1024,512]{1,0:T(8,128)(2,1)} %get-tuple-element.150), channel_id=1, source_target_pairs={{0,16},{16,0},{1,17},{17,1},{2,18},{18,2},{3,19},{19,3},{4,20},{20... | collective-permute-start | bytes 3145736 | tf_op jit(solution)/shard_map/ppermute | solution.py:45
  66.2 3.8 collective-permute-start.6
  66.2 4.2 collective-permute-start.7
  66.7 3.0 collective-permute-start.8
  66.8 3.2 collective-permute-start.9
  69.7 24.2 %collective-permute-start.11 = (bf16[512,1024]{1,0:T(8,128)(2,1)}, bf16[512,1024]{1,0:T(8,128)(2,1)}, u32[]{:S(2)}, u32[]{:S(2)}) collective-permute-start(bf16[512,1024]{1,0:T(8,128)(2,1)} %copy-done.12), channel_id=1, source_target_pairs={{0,4},{4,0},{8,12},{12,8},{1,5},{5,1},{9,13},{13,9},{2,6},{6,2},{1... | collective-permute-start | bytes 3145736 | tf_op jit(solution)/shard_map/ppermute | solution.py:50
  90.8 3.2 collective-permute-start.12
  91.0 33.8 %collective-permute-start.13 = (bf16[512,1024]{1,0:T(8,128)(2,1)}, bf16[512,1024]{1,0:T(8,128)(2,1)S(1)}, u32[]{:S(2)}, u32[]{:S(2)}) collective-permute-start(bf16[512,1024]{1,0:T(8,128)(2,1)} %get-tuple-element.155), channel_id=1, source_target_pairs={{0,16},{16,0},{1,17},{17,1},{2,18},{18,2},{3,19},{19,3},{4,20},{20... | collective-permute-start | bytes 3145736 | tf_op jit(solution)/shard_map/ppermute | solution.py:45
  91.9 33.0 %collective-permute-start.15 = (bf16[2,4,512,128]{3,2,1,0:T(8,128)(2,1)}, bf16[2,4,512,128]{3,2,1,0:T(8,128)(2,1)S(1)}, u32[]{:S(2)}, u32[]{:S(2)}) collective-permute-start(bf16[2,4,512,128]{3,2,1,0:T(8,128)(2,1)} %get-tuple-element.160), channel_id=1, source_target_pairs={{0,8},{4,12},{8,0},{12,4},{1,9},{5,13},{9,1},{13,5},{2,10},{6,14},... | collective-permute-start | bytes 3145736 | tf_op jit(solution)/shard_map/ppermute | solution.py:50
  124.9 34.1 %collective-permute-start.16 = (bf16[2,4,512,128]{3,2,1,0:T(8,128)(2,1)}, bf16[2,4,512,128]{3,2,1,0:T(8,128)(2,1)}, u32[]{:S(2)}, u32[]{:S(2)}) collective-permute-start(bf16[2,4,512,128]{3,2,1,0:T(8,128)(2,1)} %get-tuple-element.163), channel_id=1, source_target_pairs={{0,8},{4,12},{8,0},{12,4},{1,9},{5,13},{9,1},{13,5},{2,10},{6,14},... | collective-permute-start | bytes 3145736 | tf_op jit(solution)/shard_map/ppermute | solution.py:50
  126.3 32.7 %collective-permute-start.14 = (bf16[1024,512]{1,0:T(8,128)(2,1)}, bf16[1024,512]{1,0:T(8,128)(2,1)S(1)}, u32[]{:S(2)}, u32[]{:S(2)}) collective-permute-start(bf16[1024,512]{1,0:T(8,128)(2,1)} %get-tuple-element.158), channel_id=1, source_target_pairs={{0,16},{16,0},{1,17},{17,1},{2,18},{18,2},{3,19},{19,3},{4,20},{20... | collective-permute-start | bytes 3145736 | tf_op jit(solution)/shard_map/ppermute | solution.py:45
  127.1 2.1 collective-permute-start.17
  127.9 2.9 collective-permute-start.18
  128.4 30.9 %collective-permute-start.19 = (bf16[512,1024]{1,0:T(8,128)(2,1)S(1)}, bf16[512,1024]{1,0:T(8,128)(2,1)S(1)}, u32[]{:S(2)}, u32[]{:S(2)}) collective-permute-start(bf16[512,1024]{1,0:T(8,128)(2,1)S(1)} %collective-permute-done.13.refs_7_.refs_8_), channel_id=1, source_target_pairs={{0,4},{4,0},{8,12},{12,8},{1,5},{5,1},{9,13},{13,9},{2,6},{6,2},{1... | collective-permute-start | bytes 3145736 | tf_op jit(solution)/shard_map/ppermute | solution.py:50
  159.0 2.7 collective-permute-start.20
  194.6 186.4 %reduce-scatter.5.cloned.1.call-start = ((), (), s32[]{:S(2)}) async-start(), calls=%async_computation.5 | async-start | bytes 5242880 | tf_op jit(solution)/shard_map/reduce_scatter | solution.py:1008
  205.1 40.4 %collective-permute-start.25 = (bf16[2,512,2048]{2,1,0:T(8,128)(2,1)}, bf16[2,512,2048]{2,1,0:T(8,128)(2,1)}, u32[]{:S(2)}, u32[]{:S(2)}) collective-permute-start(bf16[2,512,2048]{2,1,0:T(8,128)(2,1)} %outer.6), channel_id=1, source_target_pairs={{0,4},{4,0},{8,12},{12,8},{1,5},{5,1},{9,13},{13,9},{2,6},{6,2},{1... | collective-permute-start | bytes 12582920 | tf_op jit(solution)/shard_map/ppermute | solution.py:50
  205.4 38.6 %collective-permute-start.24 = (bf16[2,4,512,128]{3,2,1,0:T(8,128)(2,1)S(1)}, bf16[2,4,512,128]{3,2,1,0:T(8,128)(2,1)S(1)}, u32[]{:S(2)}, u32[]{:S(2)}) collective-permute-start(bf16[2,4,512,128]{3,2,1,0:T(8,128)(2,1)S(1)} %copy-done.48), channel_id=1, source_target_pairs={{0,8},{4,12},{8,0},{12,4},{1,9},{5,13},{9,1},{13,5},{2,10},{6,14},... | collective-permute-start | bytes 3145736 | tf_op jit(solution)/shard_map/ppermute | solution.py:50
  206.6 6.4 %collective-permute-start.21 = (bf16[1,4,512,128]{3,2,1,0:T(8,128)(2,1)S(1)}, bf16[1,4,512,128]{3,2,1,0:T(8,128)(2,1)S(1)}, u32[]{:S(2)}, u32[]{:S(2)}) collective-permute-start(bf16[1,4,512,128]{3,2,1,0:T(8,128)(2,1)S(1)} %copy-done.50), channel_id=1, source_target_pairs={{0,4},{4,0},{8,12},{12,8},{1,5},{5,1},{9,13},{13,9},{2,6},{6,2},{1... | collective-permute-start | bytes 1572872 | tf_op jit(solution)/shard_map/ppermute | solution.py:50
  208.7 5.0 collective-permute-start.22
  242.9 27.3 %collective-permute-start.23 = (bf16[2,4,512,128]{3,2,1,0:T(8,128)(2,1)}, bf16[2,4,512,128]{3,2,1,0:T(8,128)(2,1)S(1)}, u32[]{:S(2)}, u32[]{:S(2)}) collective-permute-start(bf16[2,4,512,128]{3,2,1,0:T(8,128)(2,1)} %get-tuple-element.180), channel_id=1, source_target_pairs={{0,8},{4,12},{8,0},{12,4},{1,9},{5,13},{9,1},{13,5},{2,10},{6,14},... | collective-permute-start | bytes 3145736 | tf_op jit(solution)/shard_map/ppermute | solution.py:50
  244.0 12.9 %collective-permute-start.26 = (bf16[1,4,512,128]{3,2,1,0:T(8,128)(2,1)}, bf16[1,4,512,128]{3,2,1,0:T(8,128)(2,1)S(1)}, u32[]{:S(2)}, u32[]{:S(2)}) collective-permute-start(bf16[1,4,512,128]{3,2,1,0:T(8,128)(2,1)} %get-tuple-element.187), channel_id=1, source_target_pairs={{0,4},{4,0},{8,12},{12,8},{1,5},{5,1},{9,13},{13,9},{2,6},{6,2},{1... | collective-permute-start | bytes 1572872 | tf_op jit(solution)/shard_map/ppermute | solution.py:50
  245.1 11.9 %collective-permute-start.27 = (bf16[1,4,512,128]{3,2,1,0:T(8,128)(2,1)S(1)}, bf16[1,4,512,128]{3,2,1,0:T(8,128)(2,1)S(1)}, u32[]{:S(2)}, u32[]{:S(2)}) collective-permute-start(bf16[1,4,512,128]{3,2,1,0:T(8,128)(2,1)S(1)} %get-tuple-element.276), channel_id=1, source_target_pairs={{0,4},{4,0},{8,12},{12,8},{1,5},{5,1},{9,13},{13,9},{2,6},{6,2},{1... | collective-permute-start | bytes 1572872 | tf_op jit(solution)/shard_map/ppermute | solution.py:50
  271.1 1.9 collective-permute-start.29
  271.4 2.4 collective-permute-start.28
  271.8 25.2 %collective-permute-start.33 = (bf16[512,1024]{1,0:T(8,128)(2,1)S(1)}, bf16[512,1024]{1,0:T(8,128)(2,1)S(1)}, u32[]{:S(2)}, u32[]{:S(2)}) collective-permute-start(bf16[512,1024]{1,0:T(8,128)(2,1)S(1)} %copy-done.49), channel_id=1, source_target_pairs={{0,16},{16,0},{1,17},{17,1},{2,18},{18,2},{3,19},{19,3},{4,20},{20... | collective-permute-start | bytes 3145736 | tf_op jit(solution)/shard_map/ppermute | solution.py:45
  286.8 239.6 %all-gather.6.cloned.1.call-start = ((), (), s32[]{:S(2)}) async-start(), calls=%async_computation.4 | async-start | bytes 5242880 | tf_op jit(solution)/shard_map/all_gather | solution.py:1040
  308.4 45.7 %collective-permute-start.34 = (bf16[2048,1024]{1,0:T(8,128)(2,1)}, bf16[2048,1024]{1,0:T(8,128)(2,1)}, u32[]{:S(2)}, u32[]{:S(2)}) collective-permute-start(bf16[2048,1024]{1,0:T(8,128)(2,1)} %all-gather.4.cloned.1.call-done), channel_id=1, source_target_pairs={{0,4},{4,0},{8,12},{12,8},{1,5},{5,1},{9,13},{13,9},{2,6},{6,2},{1... | collective-permute-start | bytes 12582920 | tf_op jit(solution)/shard_map/ppermute | solution.py:50
  309.9 52.5 %collective-permute-start.37 = (bf16[2,512,2048]{2,1,0:T(8,128)(2,1)}, bf16[2,512,2048]{2,1,0:T(8,128)(2,1)}, u32[]{:S(2)}, u32[]{:S(2)}) collective-permute-start(bf16[2,512,2048]{2,1,0:T(8,128)(2,1)} %outer.8), channel_id=1, source_target_pairs={{0,4},{4,0},{8,12},{12,8},{1,5},{5,1},{9,13},{13,9},{2,6},{6,2},{1... | collective-permute-start | bytes 12582920 | tf_op jit(solution)/shard_map/ppermute | solution.py:50
  310.5 26.3 %collective-permute-start.30 = (bf16[256,512]{1,0:T(8,128)(2,1)S(1)}, bf16[256,512]{1,0:T(8,128)(2,1)S(1)}, u32[]{:S(2)}, u32[]{:S(2)}) collective-permute-start(bf16[256,512]{1,0:T(8,128)(2,1)S(1)} %get-tuple-element.272), channel_id=1, source_target_pairs={{0,1},{1,0},{2,3},{3,2},{4,5},{5,4},{6,7},{7,6},{8,9},{9,8},{10,11... | collective-permute-start | bytes 786440 | tf_op jit(solution)/shard_map/ppermute | solution.py:55
  312.1 29.9 %collective-permute-start.31 = (bf16[256,512]{1,0:T(8,128)(2,1)S(1)}, bf16[256,512]{1,0:T(8,128)(2,1)S(1)}, u32[]{:S(2)}, u32[]{:S(2)}) collective-permute-start(bf16[256,512]{1,0:T(8,128)(2,1)S(1)} %get-tuple-element.271), channel_id=1, source_target_pairs={{0,2},{1,3},{2,0},{3,1},{4,6},{5,7},{6,4},{7,5},{8,10},{9,11},{10,... | collective-permute-start | bytes 786440 | tf_op jit(solution)/shard_map/ppermute | solution.py:55
  314.8 34.8 %collective-permute-start.32 = (bf16[256,512]{1,0:T(8,128)(2,1)S(1)}, bf16[256,512]{1,0:T(8,128)(2,1)S(1)}, u32[]{:S(2)}, u32[]{:S(2)}) collective-permute-start(bf16[256,512]{1,0:T(8,128)(2,1)S(1)} %get-tuple-element.270), channel_id=1, source_target_pairs={{0,3},{1,2},{2,1},{3,0},{4,7},{5,6},{6,5},{7,4},{8,11},{9,10},{10,... | collective-permute-start | bytes 786440 | tf_op jit(solution)/shard_map/ppermute | solution.py:55
  336.8 37.4 %collective-permute-start.36 = (bf16[512,1024]{1,0:T(8,128)(2,1)S(1)}, bf16[512,1024]{1,0:T(8,128)(2,1)}, u32[]{:S(2)}, u32[]{:S(2)}) collective-permute-start(bf16[512,1024]{1,0:T(8,128)(2,1)S(1)} %add_convert_fusion.4.left), channel_id=1, source_target_pairs={{0,8},{4,12},{8,0},{12,4},{1,9},{5,13},{9,1},{13,5},{2,10},{6,14},... | collective-permute-start | bytes 3145736 | tf_op jit(solution)/shard_map/ppermute | solution.py:50
  349.6 24.6 %collective-permute-start.35 = (bf16[512,1024]{1,0:T(8,128)(2,1)}, bf16[512,1024]{1,0:T(8,128)(2,1)}, u32[]{:S(2)}, u32[]{:S(2)}) collective-permute-start(bf16[512,1024]{1,0:T(8,128)(2,1)} %get-tuple-element.214), channel_id=1, source_target_pairs={{0,16},{16,0},{1,17},{17,1},{2,18},{18,2},{3,19},{19,3},{4,20},{20... | collective-permute-start | bytes 3145736 | tf_op jit(solution)/shard_map/ppermute | solution.py:45
  375.8 25.9 %collective-permute-start.40 = (bf16[512,1024]{1,0:T(8,128)(2,1)S(1)}, bf16[512,1024]{1,0:T(8,128)(2,1)S(1)}, u32[]{:S(2)}, u32[]{:S(2)}) collective-permute-start(bf16[512,1024]{1,0:T(8,128)(2,1)S(1)} %add_convert_fusion.3.left), channel_id=1, source_target_pairs={{0,8},{4,12},{8,0},{12,4},{1,9},{5,13},{9,1},{13,5},{2,10},{6,14},... | collective-permute-start | bytes 3145736 | tf_op jit(solution)/shard_map/ppermute | solution.py:50
  376.9 23.9 %collective-permute-start.39 = (bf16[512,1024]{1,0:T(8,128)(2,1)}, bf16[512,1024]{1,0:T(8,128)(2,1)S(1)}, u32[]{:S(2)}, u32[]{:S(2)}) collective-permute-start(bf16[512,1024]{1,0:T(8,128)(2,1)} %get-tuple-element.225), channel_id=1, source_target_pairs={{0,16},{16,0},{1,17},{17,1},{2,18},{18,2},{3,19},{19,3},{4,20},{20... | collective-permute-start | bytes 3145736 | tf_op jit(solution)/shard_map/ppermute | solution.py:45
  378.0 194.5 %all-gather.8.cloned.1.call-start = ((), (), s32[]{:S(2)}) async-start(), calls=%async_computation.6 | async-start | bytes 5242880 | tf_op jit(solution)/shard_map/all_gather | solution.py:1059
  415.5 7.5 %collective-permute-start.43 = (bf16[2,512,2048]{2,1,0:T(8,128)(2,1)}, bf16[2,512,2048]{2,1,0:T(8,128)(2,1)}, u32[]{:S(2)}, u32[]{:S(2)}) collective-permute-start(bf16[2,512,2048]{2,1,0:T(8,128)(2,1)} %outer.10), channel_id=1, source_target_pairs={{0,4},{4,0},{8,12},{12,8},{1,5},{5,1},{9,13},{13,9},{2,6},{6,2},{1... | collective-permute-start | bytes 12582920 | tf_op jit(solution)/shard_map/ppermute | solution.py:50
  415.5 25.9 %collective-permute-start.41 = (bf16[512,1024]{1,0:T(8,128)(2,1)}, bf16[512,1024]{1,0:T(8,128)(2,1)}, u32[]{:S(2)}, u32[]{:S(2)}) collective-permute-start(bf16[512,1024]{1,0:T(8,128)(2,1)} %get-tuple-element.230), channel_id=1, source_target_pairs={{0,16},{16,0},{1,17},{17,1},{2,18},{18,2},{3,19},{19,3},{4,20},{20... | collective-permute-start | bytes 3145736 | tf_op jit(solution)/shard_map/ppermute | solution.py:45
  416.3 25.3 %collective-permute-start.42 = (bf16[512,1024]{1,0:T(8,128)(2,1)S(1)}, bf16[512,1024]{1,0:T(8,128)(2,1)}, u32[]{:S(2)}, u32[]{:S(2)}) collective-permute-start(bf16[512,1024]{1,0:T(8,128)(2,1)S(1)} %add_convert_fusion.2.left), channel_id=1, source_target_pairs={{0,8},{4,12},{8,0},{12,4},{1,9},{5,13},{9,1},{13,5},{2,10},{6,14},... | collective-permute-start | bytes 3145736 | tf_op jit(solution)/shard_map/ppermute | solution.py:50
  441.6 36.0 %collective-permute-start.50 = (bf16[512,1536]{1,0:T(8,128)(2,1)}, bf16[512,1536]{1,0:T(8,128)(2,1)}, u32[]{:S(2)}, u32[]{:S(2)}) collective-permute-start(bf16[512,1536]{1,0:T(8,128)(2,1)} %get-tuple-element.243), channel_id=1, source_target_pairs={{0,16},{16,0},{1,17},{17,1},{2,18},{18,2},{3,19},{19,3},{4,20},{20... | collective-permute-start | bytes 4718600 | tf_op jit(solution)/shard_map/ppermute | solution.py:45
  443.0 5.7 collective-permute-start.38
  447.4 3.1 collective-permute-start.44
  448.0 25.1 %collective-permute-start.51 = (bf16[512,1024]{1,0:T(8,128)(2,1)S(1)}, bf16[512,1024]{1,0:T(8,128)(2,1)S(1)}, u32[]{:S(2)}, u32[]{:S(2)}) collective-permute-start(bf16[512,1024]{1,0:T(8,128)(2,1)S(1)} %add_convert_fusion.1.left), channel_id=1, source_target_pairs={{0,8},{4,12},{8,0},{12,4},{1,9},{5,13},{9,1},{13,5},{2,10},{6,14},... | collective-permute-start | bytes 3145736 | tf_op jit(solution)/shard_map/ppermute | solution.py:50
  480.1 35.0 %collective-permute-start.55 = (bf16[512,1536]{1,0:T(8,128)(2,1)S(1)}, bf16[512,1536]{1,0:T(8,128)(2,1)}, u32[]{:S(2)}, u32[]{:S(2)}) collective-permute-start(bf16[512,1536]{1,0:T(8,128)(2,1)S(1)} %add_convert_fusion.left), channel_id=1, source_target_pairs={{0,8},{4,12},{8,0},{12,4},{1,9},{5,13},{9,1},{13,5},{2,10},{6,14},... | collective-permute-start | bytes 4718600 | tf_op jit(solution)/shard_map/ppermute | solution.py:50
  481.3 3.9 collective-permute-start.53
  483.7 3.1 collective-permute-start.54
  484.3 14.1 %collective-permute-start.52 = (bf16[512,512]{1,0:T(8,128)(2,1)}, bf16[512,512]{1,0:T(8,128)(2,1)S(1)}, u32[]{:S(2)}, u32[]{:S(2)}) collective-permute-start(bf16[512,512]{1,0:T(8,128)(2,1)} %get-tuple-element.247), channel_id=1, source_target_pairs={{0,16},{16,0},{1,17},{17,1},{2,18},{18,2},{3,19},{19,3},{4,20},{20... | collective-permute-start | bytes 1572872 | tf_op jit(solution)/shard_map/ppermute | solution.py:45
  518.0 40.2 %collective-permute-start.56 = (bf16[512,1536]{1,0:T(8,128)(2,1)}, bf16[512,1536]{1,0:T(8,128)(2,1)S(1)}, u32[]{:S(2)}, u32[]{:S(2)}) collective-permute-start(bf16[512,1536]{1,0:T(8,128)(2,1)} %add_turned.10.refs_0_), channel_id=1, source_target_pairs={{0,4},{4,0},{8,12},{12,8},{1,5},{5,1},{9,13},{13,9},{2,6},{6,2},{1... | collective-permute-start | bytes 4718600 | tf_op jit(solution)/shard_map/ppermute | solution.py:50
  518.0 3.1 collective-permute-start.45
  521.1 4.1 collective-permute-start.46
  525.2 4.0 collective-permute-start.47
  529.4 39.2 %collective-permute-start.57 = (bf16[512,512]{1,0:T(8,128)(2,1)S(1)}, bf16[512,512]{1,0:T(8,128)(2,1)S(1)}, u32[]{:S(2)}, u32[]{:S(2)}) collective-permute-start(bf16[512,512]{1,0:T(8,128)(2,1)S(1)} %add_convert_fusion.5.left), channel_id=1, source_target_pairs={{0,8},{4,12},{8,0},{12,4},{1,9},{5,13},{9,1},{13,5},{2,10},{6,14},... | collective-permute-start | bytes 1572872 | tf_op jit(solution)/shard_map/ppermute | solution.py:50
  530.5 18.8 %collective-permute-start.48 = (f32[2,2048]{1,0:T(2,128)S(1)}, f32[2,2048]{1,0:T(2,128)S(1)}, u32[]{:S(2)}, u32[]{:S(2)}) collective-permute-start(f32[2,2048]{1,0:T(2,128)S(1)} %reshape.134), channel_id=1, source_target_pairs={{0,1},{1,0},{2,3},{3,2},{4,5},{5,4},{6,7},{7,6},{8,9},{9,8},{10,11... | collective-permute-start | bytes 49160 | tf_op jit(solution)/shard_map/ppermute | solution.py:55
  549.3 8.8 %collective-permute-start.49 = (f32[2,2048]{1,0:T(2,128)S(1)}, f32[2,2048]{1,0:T(2,128)S(1)}, u32[]{:S(2)}, u32[]{:S(2)}) collective-permute-start(f32[2,2048]{1,0:T(2,128)S(1)} %add.220), channel_id=1, source_target_pairs={{0,2},{1,3},{2,0},{3,1},{4,6},{5,7},{6,4},{7,5},{8,10},{9,11},{10,... | collective-permute-start | bytes 49160 | tf_op jit(solution)/shard_map/ppermute | solution.py:55
  571.3 2.1 collective-permute-start.58
  (52 other events, 526.4 us)
Sparse Core Ops, SparseCore 0:
  61.8 81.9 all-gather.3
  194.7 76.9 reduce-scatter.2
  287.0 93.9 reduce-scatter.4
  382.4 94.7 all-gather.5
  478.7 79.9 all-gather.7

commit v2 on v1

--- a/solution.py
+++ b/solution.py
@@ -64,16 +64,6 @@
     while mask < size:
         yield mask
         mask *= 2
-
-
-def sum_everywhere(value, over_tensor):
-    for mask in masks_of(lax.axis_size("context")):
-        value = value + to_context(value, mask)
-    value = value + to_fsdp(value)
-    if over_tensor:
-        for mask in masks_of(lax.axis_size("tensor")):
-            value = value + to_tensor(value, mask)
-    return value
 
 
 def own_blocks(own, axis, place, block):
@@ -296,14 +286,13 @@
     return [results[s * len(counts) : (s + 1) * len(counts)] for s in range(seqs)]
 
 
-def attend_kernel(parts, queries_at_once, keys_at_once, me_ref, *refs):
+def attend_kernel(parts, bq, bk, me_ref, *refs):
     pieces = refs[:parts]
     outs = refs[parts:-11]
     q_all, k_all, v_all, g_all, v_turned, k_turned, o_all, dq_all, dk_all, dv_all, held = refs[-11:]
     rows, width = pieces[0].shape[2:]
     length = rows * parts
     me = me_ref[0]
-    bq, bk = queries_at_once, keys_at_once
     scale = HD**-0.5
     for m in range(parts):
         at = pl.ds(pl.multiple_of((me ^ m) * rows, rows), rows)
@@ -317,70 +306,57 @@
     dv_all[...] = jnp.zeros_like(dv_all)
     heads = width // HD
     lane_head = lax.broadcasted_iota(jnp.int32, (1, width), 1) // HD
-    row_head = lax.broadcasted_iota(jnp.int32, (width, 1), 0) // HD
-
-    def one_block(i, _):
-        at_q = pl.ds(pl.multiple_of(i * bq, bq), bq)
-        query = q_all[at_q, :]
-        grad = g_all[at_q, :]
-        blocks = (i + 1) * (bq // bk)
-        outs_now = jnp.zeros((width, bq), F32)
-        grads_now = jnp.zeros((width, bq), F32)
+
+    for first in range(0, length, bq):
+        at_q = slice(first, first + bq)
+        query, grad = q_all[at_q, :], g_all[at_q, :]
+        spans = [slice(k, min(k + bk, first + bq)) for k in range(0, first + bq, bk)]
+        outputs, q_grads = [], []
         for h in range(heads):
+            at_h = slice(h * HD, (h + 1) * HD)
             q_head = jnp.where(lane_head == h, query, jnp.zeros_like(query))
             g_head = jnp.where(lane_head == h, grad, jnp.zeros_like(grad))
-
-            def score(j, top, masked=False):
-                at_k = pl.ds(pl.multiple_of(j * bk, bk), bk)
-                scores = nt(k_all[at_k, :], q_head)
-                if masked:
-                    key = j * bk + lax.broadcasted_iota(jnp.int32, (bk, bq), 0)
-                    place = i * bq + lax.broadcasted_iota(jnp.int32, (bk, bq), 1)
-                    scores = jnp.where(key <= place, scores, -1e30)
-                held[at_k, :] = scores
-                return jnp.maximum(top, jnp.max(scores.reshape(bk // 8, 8, bq), 0))
-
             top = jnp.full((8, bq), -1e30, F32)
-            top = lax.fori_loop(0, i * (bq // bk), score, top)
-            for d in range(bq // bk):
-                top = score(i * (bq // bk) + d, top, True)
+            for span in spans:
+                scores = nt(k_all[span, :], q_head)
+                free = min(span.stop, max(first, span.start)) - span.start
+                if free:
+                    part = scores[:free]
+                    held[span.start : span.start + free, :] = part
+                    top = jnp.maximum(top, jnp.max(part.reshape(free // 8, 8, bq), 0))
+                rest = span.stop - span.start - free
+                if rest:
+                    key = span.start + free + lax.broadcasted_iota(jnp.int32, (rest, bq), 0)
+                    place = first + lax.broadcasted_iota(jnp.int32, (rest, bq), 1)
+                    part = jnp.where(key <= place, scores[free:], -1e30)
+                    held[span.start + free : span.stop, :] = part
+                    top = jnp.maximum(top, jnp.max(part.reshape(rest // 8, 8, bq), 0))
             top = jnp.max(top, 0, keepdims=True)
-
-            def weigh(j, carry):
-                total, output = carry
-                at_k = pl.ds(pl.multiple_of(j * bk, bk), bk)
-                weights = jnp.exp(held[at_k, :] - top)
-                held[at_k, :] = weights
-                total = total + jnp.sum(weights.reshape(bk // 8, 8, bq), 0)
-                return total, output + nn(v_turned[:, at_k], weights.astype(BF16))
-
-            total, output = lax.fori_loop(
-                0, blocks, weigh, (jnp.zeros((8, bq), F32), jnp.zeros((width, bq), F32))
-            )
+            total = jnp.zeros((8, bq), F32)
+            output = jnp.zeros((HD, bq), F32)
+            for span in spans:
+                weights = jnp.exp(held[span, :] - top)
+                held[span, :] = weights
+                total = total + jnp.sum(weights.reshape(-1, 8, bq), 0)
+                output = output + nn(v_turned[at_h, span], weights.astype(BF16))
             inverse = 1.0 / jnp.sum(total, 0, keepdims=True)
             output = output * inverse
             g_turned = g_head.T.astype(F32)
-            inner = jnp.sum(output * g_turned, 0, keepdims=True) * inverse
+            inner = jnp.sum(output * g_turned[at_h], 0, keepdims=True) * inverse
             g_scaled = (g_turned * inverse).astype(BF16)
             g_rows = g_scaled.T
-
-            def back(j, total):
-                at_k = pl.ds(pl.multiple_of(j * bk, bk), bk)
-                weights = held[at_k, :]
-                prob_grad = nn(v_all[at_k, :], g_scaled)
+            q_grad = jnp.zeros((HD, bq), F32)
+            for span in spans:
+                weights = held[span, :]
+                prob_grad = nn(v_all[span, :], g_scaled)
                 score_grad = (weights * (prob_grad - inner)).astype(BF16)
-                dv_all[at_k, :] += nn(weights.astype(BF16), g_rows)
-                dk_all[at_k, :] += nn(score_grad, q_head)
-                return total + nn(k_turned[:, at_k], score_grad)
-
-            q_grad = lax.fori_loop(0, blocks, back, jnp.zeros((width, bq), F32)) * scale
-            outs_now = jnp.where(row_head == h, output, outs_now)
-            grads_now = jnp.where(row_head == h, q_grad, grads_now)
-        o_all[at_q, :] = outs_now.T.astype(BF16)
-        dq_all[at_q, :] = grads_now.T.astype(BF16)
-        return 0
-
-    lax.fori_loop(0, length // bq, one_block, 0)
+                dv_all[span, :] += nn(weights.astype(BF16), g_rows)
+                dk_all[span, :] += nn(score_grad, q_head)
+                q_grad = q_grad + nn(k_turned[at_h, span], score_grad)
+            outputs.append(output)
+            q_grads.append(q_grad * scale)
+        o_all[at_q, :] = jnp.concatenate(outputs, 0).T.astype(BF16)
+        dq_all[at_q, :] = jnp.concatenate(q_grads, 0).T.astype(BF16)
     for m in range(parts):
         at = pl.ds(pl.multiple_of((me ^ m) * rows, rows), rows)
         out, i = (outs[m], 0) if len(outs) == parts else (outs[min(m, 2)], max(m - 2, 0))
@@ -394,8 +370,8 @@
     parts = len(pieces)
     seqs, _, rows, width = pieces[0].shape
     length = rows * parts
-    bq = min(1024, length)
-    bk = bq
+    bq = min(512, length)
+    bk = min(2048, length)
     vmem = pltpu.VMEM
     counts = [1, 1, 2] if paired else [seqs] * parts
     return pl.pallas_call(
@@ -472,40 +448,53 @@
 
 
 def norm_back_kernel(count, k_ref, raw, back, *refs):
-    width = refs[0].shape[2]
-    total = back[...].astype(F32)
-    for c in range(3):
-        weight = jnp.concatenate([w[c] for w in refs[:count]], 0)
-        total = total + nt(raw[:, c * width : (c + 1) * width], weight)
-    refs[-1][...] = total.astype(BF16)
-
-
-def norm_back(place, raw, back, own, rest, s, seqs, earlier):
+    out, total = refs[-2:]
+    weight = jnp.concatenate([w[0] for w in refs[:count]], 0)
+    term = nt(raw[...], weight)
+    step = pl.program_id(0)
+
+    @pl.when(step == 0)
+    def _():
+        total[...] = back[...].astype(F32) + term
+
+    @pl.when(step == 1)
+    def _():
+        total[...] += term
+
+    @pl.when(step == 2)
+    def _():
+        out[...] = (total[...] + term).astype(BF16).reshape(out.shape)
+
+
+def norm_back(place, raw, back, own, rest, s, seqs, shares, earlier):
     rows, depth = back.shape
     width = own.shape[2]
     block = rest[0].shape[1]
     count = own.shape[1] // block
     length = rows // seqs
-    tile = min(256, length)
-    skip = s * (length // tile)
 
     def own_spec(p):
-        return pl.BlockSpec((3, block, width), lambda r, k: (0, p ^ k[0], 0))
+        return pl.BlockSpec((1, block, width), lambda c, k: (c, p ^ k[0], 0))
 
     specs = [own_spec(p) for p in range(count)] + [
-        pl.BlockSpec((3, block, width), lambda r, k: (0, 0, 0))
+        pl.BlockSpec((1, block, width), lambda c, k: (c, 0, 0))
     ] * len(rest)
-    some = pl.BlockSpec((tile, depth), lambda r, k: (r + skip, 0))
     return pl.pallas_call(
         functools.partial(norm_back_kernel, len(specs)),
-        out_shape=jax.ShapeDtypeStruct((rows, depth), BF16),
+        out_shape=jax.ShapeDtypeStruct((shares, seqs, length // shares, depth), BF16),
         grid_spec=pltpu.PrefetchScalarGridSpec(
             num_scalar_prefetch=1,
-            grid=(length // tile,),
-            in_specs=[pl.BlockSpec((tile, 3 * width), lambda r, k: (r + skip, 0)), some]
+            grid=(3,),
+            in_specs=[
+                pl.BlockSpec((length, width), lambda c, k: (s, c)),
+                pl.BlockSpec((length, depth), lambda c, k: (s, 0)),
+            ]
             + specs
             + [pl.BlockSpec(memory_space=pl.ANY)] * len(earlier),
-            out_specs=some,
+            out_specs=pl.BlockSpec(
+                (shares, 1, length // shares, depth), lambda c, k: (0, s, 0, 0)
+            ),
+            scratch_shapes=[pltpu.VMEM((length, depth), F32)],
         ),
         input_output_aliases={3 + len(specs) + i: i for i in range(len(earlier))},
         compiler_params=pltpu.CompilerParams(vmem_limit_bytes=VMEM_BYTES),
@@ -522,7 +511,7 @@
     return value * half, slope
 
 
-def feed_kernel(first_count, second_count, onto, k_ref, *refs):
+def feed_kernel(first_count, second_count, onto, seqs, shares, k_ref, *refs):
     normed, grad, bias = refs[:3]
     ends = (3 + first_count, 3 + first_count + second_count)
     first = jnp.concatenate([r[...] for r in refs[3 : ends[0]]], 0)
@@ -550,12 +539,29 @@
 
     @pl.when(tile == pl.num_programs(0) - 1)
     def _():
-        fed_out[...] = fed[...].astype(BF16)
+        tile_rows = fed.shape[0] // (seqs * shares)
+        for to in range(seqs * shares):
+            source = (to % seqs * shares + to // seqs) * tile_rows
+            fed_out[to * tile_rows : (to + 1) * tile_rows, :] = fed[
+                source : source + tile_rows, :
+            ].astype(BF16)
         back_out[...] = back[...].astype(BF16)
 
 
 def feed(
-    place, block, normed, grad, bias, own_first, rest_first, own_second, rest_second, part, sums
+    place,
+    block,
+    normed,
+    grad,
+    bias,
+    own_first,
+    rest_first,
+    own_second,
+    rest_second,
+    part,
+    sums,
+    seqs,
+    shares,
 ):
     rows, width = normed.shape
     inside = rest_first[0].shape[0] // block
@@ -583,7 +589,7 @@
     second += [second_rest(p) for p in range(inside)] * len(rest_second)
     unit_rows = pl.BlockSpec((rows, tile), lambda t, k: (0, t))
     return pl.pallas_call(
-        functools.partial(feed_kernel, len(first), len(second), len(sums)),
+        functools.partial(feed_kernel, len(first), len(second), len(sums), seqs, shares),
         out_shape=[
             jax.ShapeDtypeStruct((rows, units), BF16),
             jax.ShapeDtypeStruct((rows, units), BF16),
@@ -716,18 +722,23 @@
     )(left, right)
 
 
-def finish_kernel(half, tiles, turned, k_ref, *refs):
+def finish_kernel(half, turned, groups, k_ref, *refs):
     out = refs[-1]
-    for i, piece in enumerate(refs[:-1]):
-        here = pl.program_id(0) // half == i % 2
-        if tiles is not None:
-            here = here & (pl.program_id(1) // tiles == i // 2)
-
-        @pl.when(here)
+    pieces = refs[:-1]
+    for i, piece in enumerate(pieces):
+        width = piece.shape[1] // groups
+
+        @pl.when(pl.program_id(0) // half == i % 2)
         def _():
             value = piece[...].astype(F32)
-            value = value.T if turned else value
-            out[...] = value.reshape(out.shape)
+            start = i // 2 * piece.shape[1]
+            if groups > 1:
+                for g in range(groups):
+                    out[g] = value[:, g * width : (g + 1) * width]
+            elif turned:
+                out[start : start + width, :] = value.T
+            else:
+                out[:, start : start + width] = value
 
 
 def finish(place, parts, block, turned=False, groups=1):
@@ -735,39 +746,29 @@
     width = some * len(parts)
     half = rows // block
     if groups > 1:
-        tile = width // groups
-        shape = (groups, 2 * rows, tile)
-        out_spec = pl.BlockSpec((1, block, tile), lambda p, t, k: (t, p ^ k[0], 0))
+        shape = (groups, 2 * rows, width // groups)
+        out_spec = pl.BlockSpec((groups, block, width // groups), lambda p, k: (0, p ^ k[0], 0))
     elif turned:
-        tile = min(1024, some)
         shape = (width, 2 * rows)
-        out_spec = pl.BlockSpec((tile, block), lambda p, t, k: (t, p ^ k[0]))
+        out_spec = pl.BlockSpec((width, block), lambda p, k: (0, p ^ k[0]))
     else:
-        tile = min(1024, some)
         shape = (2 * rows, width)
-        out_spec = pl.BlockSpec((block, tile), lambda p, t, k: (p ^ k[0], t))
-    tiles = some // tile
-
-    def piece_spec(part, side):
-        def index(p, t, k):
-            return (
-                jnp.clip(p - side * half, 0, half - 1),
-                jnp.clip(t - part * tiles, 0, tiles - 1),
-            )
-
-        return pl.BlockSpec((block, tile), index)
+        out_spec = pl.BlockSpec((block, width), lambda p, k: (p ^ k[0], 0))
+
+    def piece_spec(side):
+        return pl.BlockSpec((block, some), lambda p, k: (jnp.clip(p - side * half, 0, half - 1), 0))
 
     return pl.pallas_call(
-        functools.partial(finish_kernel, half, tiles if len(parts) > 1 else None, turned),
+        functools.partial(finish_kernel, half, turned, groups),
         out_shape=jax.ShapeDtypeStruct(shape, F32),
         grid_spec=pltpu.PrefetchScalarGridSpec(
             num_scalar_prefetch=1,
-            grid=(2 * half, width // tile),
-            in_specs=[piece_spec(part, side) for part in range(len(parts)) for side in (0, 1)],
+            grid=(2 * half,),
+            in_specs=[piece_spec(side) for _ in parts for side in (0, 1)],
             out_specs=out_spec,
         ),
         compiler_params=pltpu.CompilerParams(vmem_limit_bytes=VMEM_BYTES),
-        cost_estimate=lasting(8),
+        cost_estimate=lasting(6),
         name="finish",
     )(place, *[piece for part in parts for piece in part])
 
@@ -847,31 +848,36 @@
         second = lax.dynamic_slice(w_fc2, (i * units, core * half), (units, half))
         return to_fsdp(after(first, *done)), to_fsdp(after(second, *done))
 
+    first_mine = [
+        lax.dynamic_slice(w_fc1, (core * half, i * units), (half, units)) for i in range(halves)
+    ]
+    second_mine = [
+        lax.dynamic_slice(w_fc2, (i * units, core * half), (units, half)) for i in range(halves)
+    ]
     rest_qkv = [to_fsdp(qkv_at(0))]
     ready = rest_qkv[0]
     rest_out = [to_fsdp(after(out_at(0), ready))]
-
-    def first_from(i, *done):
-        part = lax.dynamic_slice(w_fc1, (core * half, i * units), (half, units))
-        return to_fsdp(after(part, *done))
-
-    def second_from(i, *done):
-        part = lax.dynamic_slice(w_fc2, (i * units, core * half), (units, half))
-        return to_fsdp(after(part, *done))
-
-    first_near = [first_from(0, ready)]
+    first_near = [to_fsdp(after(first_mine[0], ready))]
     order.mark(bias_sum)
     for mask in masks_of(across):
         rest_qkv = rest_qkv + [to_context(piece, 2 * mask) for piece in rest_qkv]
-    waited = order.wait(*rest_qkv, *rest_out)
-    rest_qkv, rest_out = list(waited[: len(rest_qkv)]), list(waited[len(rest_qkv) :])
+    mine = first_mine[1:] + second_mine
+    waited = order.wait(*rest_qkv, *rest_out, *mine)
+    rest_qkv, rest_out = list(waited[:across]), list(waited[across : -len(mine)])
+    first_mine[1:], second_mine = waited[-len(mine) : -halves], waited[-halves:]
     for mask in masks_of(across):
         rest_out = rest_out + [to_context(piece, 2 * mask) for piece in rest_out]
     rest_qkv = rest_qkv + [to_context(piece, 1) for piece in rest_qkv]
     waited = order.wait(first_near[0], *rest_out)
     first_near[0], rest_out = waited[0], list(waited[1:])
-    second_near = [second_from(0, first_near[0])]
     rest_out = rest_out + [to_context(piece, 1) for piece in rest_out]
+    second_near = [to_fsdp(after(second_mine[0], first_near[0]))]
+
+    def first_from(i, *done):
+        return to_fsdp(after(first_mine[i], *done))
+
+    def second_from(i, *done):
+        return to_fsdp(after(second_mine[i], *done))
 
     near = jnp.concatenate([out_at(p) for p in range(across)] + rest_out[:across], 1)
     near = lax.all_gather(near, "tensor", axis=0, tiled=True)
@@ -934,6 +940,7 @@
             [second, to_context(second, 1)],
             i,
             tuple(sums),
+            *((seqs, tensor_size) if i == halves - 1 else (1, 1)),
         )
         fed_parts.append((hidden, pre_grad, order.mark(pre_sum)))
         return sums
@@ -955,6 +962,8 @@
                 Reduction(order, ((normed, part[1]), (grad, part[0])), block)
                 for part in fed_parts
             ]
+            if direct and 0 < i < len(rows_here):
+                rows_here[i] = list(order.wait(*rows_here[i]))
             fc_sums[0].send()
         if i < len(here):
             if direct and i == 0:
@@ -982,63 +991,96 @@
         ordered = ordered.reshape(seqs, 4, length, heads_width)
         back = [[ordered[s : s + 1]] for s in range(seqs)]
 
-    def through(s, unturned, norm_terms):
+    share = rows // tensor_size
+
+    def turn_back(s, unturned):
         row = [order(back[s][0])] + back[s][1:]
-        *unturned, part_sum = unturn(context_s, row, tables, s, rows, tuple(unturned))
-        norm_terms = norm_back(
-            place_s, unturned[1], fed_back, w_qkv, rest_qkv, s, seqs, tuple(norm_terms)
+        results = unturn(context_s, row, tables, s, rows, tuple(unturned))
+        order.mark(results[0])
+        return results
+
+    def add_heads(s, raw_grad, norm_terms):
+        return order.mark(
+            norm_back(
+                place_s,
+                order(raw_grad),
+                fed_back,
+                w_qkv,
+                rest_qkv,
+                s,
+                seqs,
+                tensor_size,
+                tuple(norm_terms),
+            )
         )
-        order.mark(norm_terms)
-        return unturned, [norm_terms], part_sum
+
+    part_rows = length // tensor_size
+
+    def heads_of(s, merged):
+        def rows_for(mask):
+            start = s * length + (tensor ^ mask) * part_rows
+            return lax.dynamic_slice_in_dim(merged, start, part_rows, 0)
+
+        return [rows_for(0)] + [to_tensor(rows_for(m), m) for m in range(1, tensor_size)]
+
+    def arrived(*values):
+        return order.wait(*values)
 
     first_sum, second_sum = fc_sums
     if direct:
         back[0] = pass_on(*back[0])
-    first_sum.keep()
-    first_sum.over_fsdp(0)
     unturned = []
     norm_terms = ()
+    heads_from = []
     qkv_bias_sum = 0.0
     for s in range(seqs):
-        if direct and s:
-            back[s] = pass_on(*back[s])
-        unturned, norm_terms, part_sum = through(s, unturned, norm_terms)
+        *unturned, part_sum = turn_back(s, unturned)
         qkv_bias_sum = qkv_bias_sum + part_sum
+        heads_from.append(heads_of(s, unturned[0]))
+        norm_terms = [add_heads(s, unturned[1], norm_terms)]
+        if s == 0:
+            first_sum.keep()
+            first_sum.over_fsdp(0)
+        if direct and s + 1 < seqs:
+            back[s + 1] = pass_on(*back[s + 1])
     merged, raw_grad = unturned
-    norm_share = lax.psum_scatter(norm_terms[0], "tensor", scatter_dimension=0, tiled=True)
-    share = rows // tensor_size
-
-    def rows_for(mask):
-        return lax.dynamic_slice_in_dim(merged, (tensor ^ mask) * share, share, 0)
-
-    def arrived(*values):
-        return order.wait(*values)
-
-    heads_from = [rows_for(0)] + [to_tensor(rows_for(m), m) for m in range(1, tensor_size)]
     last_sum = Reduction(order, ((grad, merged), (normed, raw_grad)), block)
+    arrivals = arrived(*[piece for pieces_here in heads_from for piece in pieces_here[1:]])
+    norm_share = order(norm_terms[0]).reshape(rows, width)
+    norm_share = lax.psum_scatter(norm_share, "tensor", scatter_dimension=0, tiled=True)
+    second_sum.send()
     (first_sum.far[0],) = arrived(first_sum.far[0])
     first_sum.over_fsdp(1, first_sum.far[0])
     first_sum.over_chips(0)
-    second_sum.send()
-    far = to_context(order(near), 1)
-    heads_from[1:] = arrived(*heads_from[1:])
 
     def in_order(blocks):
         return jnp.concatenate(own_blocks(blocks, 1, me, block), 1).astype(F32)
 
-    inputs = lax.dynamic_slice_in_dim(flat, tensor * share, share, 0).astype(F32)
+    def shared_rows(value):
+        return lax.dynamic_slice_in_dim(value, tensor * part_rows, part_rows, 1).reshape(share, width)
+
+    def from_shares(value):
+        value = value.reshape(tensor_size, seqs, part_rows, width)
+        return jnp.swapaxes(value, 0, 1).reshape(tokens.shape)
+
+    inputs = shared_rows(tokens).astype(F32)
     all_heads = jnp.zeros((share, tensor_size * heads_width), BF16)
-    for m in range(tensor_size):
-        all_heads = lax.dynamic_update_slice_in_dim(
-            all_heads, order(heads_from[m]), (tensor ^ m) * heads_width, 1
-        )
+    arrivals = list(arrivals)
+    for s in range(seqs):
+        for m in range(tensor_size):
+            piece = arrivals.pop(0) if m else heads_from[s][0]
+            all_heads = lax.dynamic_update_slice(
+                all_heads, order(piece), (s * part_rows, (tensor ^ m) * heads_width)
+            )
+    far = to_context(near, 1)
     near_part, far_part = nn(all_heads, near), nn(all_heads, far)
     attended = [near_part[:, :half], far_part[:, :half], near_part[:, half:], far_part[:, half:]]
     branch_sum = in_order(jnp.concatenate(attended, 1) + fed_share.astype(F32))
     block_out = (inputs + branch_sum + out_bias + fc2_bias).astype(BF16)
     order.mark(block_out)
-    block_out = lax.all_gather(block_out, "tensor", axis=0, tiled=True).reshape(tokens.shape)
+    block_out = from_shares(lax.all_gather(block_out, "tensor", axis=0, tiled=True))
     second_sum.keep()
+    last_sum.send()
     first_sum.far[1], first_sum.far[0] = arrived(first_sum.far[1], first_sum.far[0])
     second_sum.over_fsdp(0, first_sum.far[1])
     first_sum.over_chips(1)
@@ -1051,23 +1093,42 @@
     scaled = normed_grad * gain
     inner = jnp.mean(scaled * unit, -1, keepdims=True)
     input_part = root * (scaled - jnp.mean(scaled, -1, keepdims=True) - unit * inner)
-    grad_share = lax.dynamic_slice_in_dim(grad_flat, tensor * share, share, 0).astype(F32)
+    grad_share = shared_rows(cotangent).astype(F32)
     tokens_grad = (grad_share + input_part).astype(BF16)
     norm_sums = jnp.stack([jnp.sum(normed_grad * unit, 0), jnp.sum(normed_grad, 0)])
     order.mark(norm_sums)
     order.mark(tokens_grad)
-    tokens_grad = lax.all_gather(tokens_grad, "tensor", axis=0, tiled=True).reshape(tokens.shape)
-
-    second_sum.far[0], first_sum.far[1] = arrived(second_sum.far[0], first_sum.far[1])
+    small_sums = [norm_sums.reshape(1, -1), bias_sum] + [part[2] for part in fed_parts]
+    small_sums = jnp.concatenate(small_sums + [qkv_bias_sum], 1)
+    small_other = to_context(small_sums, 1)
+
+    second_sum.far[0], first_sum.far[1], small_other = arrived(
+        second_sum.far[0], first_sum.far[1], small_other
+    )
+    small_sums = small_sums + small_other
+    small_other = to_fsdp(small_sums)
     second_sum.over_fsdp(1, second_sum.far[0])
     second_sum.over_chips(0)
-    last_sum.send()
     first_sum.over_cores(1)
     last_sum.keep()
-    second_sum.far[1], second_sum.far[0] = arrived(second_sum.far[1], second_sum.far[0])
+    second_sum.far[1], second_sum.far[0], small_other = arrived(
+        second_sum.far[1], second_sum.far[0], small_other
+    )
+    small_sums = small_sums + small_other
+    for mask in masks_of(across):
+        small_sums = small_sums + to_context(small_sums, 2 * mask)
     last_sum.over_fsdp(1, second_sum.far[1])
     second_sum.over_chips(1)
     second_sum.over_cores(0)
+    norm_sums = order.mark(small_sums)[0, : 2 * width].reshape(2, width)
+    high = norm_sums.astype(BF16)
+    low = (norm_sums - high.astype(F32)).astype(BF16)
+    extra = jnp.concatenate([high, low, jnp.zeros((12, width), BF16)], 0)
+    gathered = jnp.concatenate([order(tokens_grad), extra], 0)
+    gathered = lax.all_gather(gathered, "tensor", axis=0, tiled=False)
+    tokens_grad = from_shares(gathered[:, :share])
+    norm_sums = jnp.sum(gathered[:, share : share + 4].astype(F32), 0)
+    norm_sums = norm_sums[:2] + norm_sums[2:]
     fc1_grad = order.mark(
         finish(place_s, [first_sum.pieces[0], second_sum.pieces[0]], block)
     )
@@ -1084,14 +1145,8 @@
     qkv_grad = order.mark(finish(place_s, [last_sum.pieces[1]], block, groups=3))
     last_sum.over_cores(0)
     out_grad = order.mark(finish(place_s, [last_sum.pieces[0]], block, turned=True))
-
     units_here = b_fc1.shape[0] * 2
-    small_sums = [norm_sums.reshape(1, -1), bias_sum] + [part[2] for part in fed_parts]
-    small_sums = jnp.concatenate(small_sums + [qkv_bias_sum], 1)
-    small_sums = sum_everywhere(after(small_sums, fc1_grad), False)[0]
-    norm_sums = small_sums[: 2 * width].reshape(2, width)
-    for mask in masks_of(tensor_size):
-        norm_sums = norm_sums + to_tensor(norm_sums, mask)
+    small_sums = small_sums[0]
     other_sums = small_sums[2 * width :]
 
     def shard_of(value):

time: 601 us -> 553 us (0.920)
  Pallas kernels: 285 us -> 266 us
  waiting for transfers between devices: 148 us -> 129 us
  starting transfers between devices: 63.9 us -> 45.1 us
  local copies, waits for them, and re-layouts: 50.7 us -> 57 us
    ppermute x5 -> x6, waiting for transfers between devices: 37.5 us -> 1.19 us  [to_tensor(): return lax.ppermute(value, 'tensor', [(i, i ^ mask) for i in range(size)])]
    ppermute x5 -> x6, starting transfers between devices: 28 us -> 8.9 us  [to_tensor(): return lax.ppermute(value, 'tensor', [(i, i ^ mask) for i in range(size)])]
    pallas_call x2, Pallas kernels: 56.5 us -> 41.3 us  [attend(): pl.pallas_call(functools.partial(attend_kernel, parts, bq, bk), out_shape...]
    all_gather x1, waiting for transfers between devices: 0.01 us -> 14.2 us  [per_device(): gathered = lax.all_gather(gathered, 'tensor', axis=0, tiled=False)]
    pallas_call x4, Pallas kernels: 29.9 us -> 21.8 us  [finish(): pl.pallas_call(functools.partial(finish_kernel, half, turned, groups), ou...]
    unnamed x136 -> x157, local copies, waits for them, and re-layouts: 29 us -> 21.8 us
  transfers between devices with their start and end apart: 64 -> 65, of which waited for: 36 -> 31; matrix products, arithmetic and copies ran while one was open for 10% -> 13% of each run, Pallas kernels for 47% -> 49%
where the time goes in v2:
time: 553 us; the launch traced here: 544 us
  Pallas kernels  266 us (48%)
  waiting for transfers between devices  129 us (23%)
  local copies, waits for them, and re-layouts  57 us (10%)
  starting transfers between devices  45.1 us (8%)
  other arithmetic  26.6 us (5%)
  between operations  15.3 us (3%)
    ppermute x40, waiting for transfers between devices, to_context(): return lax.ppermute(value, 'context', [(i, i ^ mask) for i in range(size)])  69.1 us
    pallas_call x6, Pallas kernels, outer(): pl.pallas_call(functools.partial(outer_kernel, steps, int(adds)), out_sha...  67.6 us
    pallas_call x2, Pallas kernels, feed(): pl.pallas_call(functools.partial(feed_kernel, len(first), len(second), le...  61.8 us
    pallas_call x2, Pallas kernels, attend(): pl.pallas_call(functools.partial(attend_kernel, parts, bq, bk), out_shape...  41.3 us
    ppermute x14, waiting for transfers between devices, to_fsdp(): return lax.ppermute(value, 'fsdp', [(0, 1), (1, 0)])  40.1 us
    ppermute x40, starting transfers between devices, to_context(): return lax.ppermute(value, 'context', [(i, i ^ mask) for i in range(size)])  21.9 us
    pallas_call x4, Pallas kernels, finish(): pl.pallas_call(functools.partial(finish_kernel, half, turned, groups), ou...  21.8 us
    unnamed x157, local copies, waits for them, and re-layouts  21.8 us
  transfers between devices with their start and end apart: 65, of which 31 were waited for; matrix products, arithmetic and copies ran while one was open for 13% of the time, Pallas kernels for 49%

profile of v2, /device:TPU:0, one launch (start us, length us, event | category | flops | bytes accessed | tf_op | source)
XLA Modules:
  0.0 543.9 jit_solution(4990231137399966408)
XLA Ops:
  7.2 2.1 constant_dynamic-slice_fusion.25
  9.3 3.0 collective-permute-start.1
  16.5 3.2 constant_dynamic-slice_fusion.27
  25.7 4.6 collective-permute-done
  36.1 10.5 %prepare.1 = (bf16[1024,2048]{1,0:T(8,128)(2,1)}, bf16[1024,2048]{1,0:T(8,128)(2,1)}, f32[1,2048]{1,0:T(1,128)}) custom-call(s32[1]{0:T(128)} %bitcast.3.me_ref, bf16[1024,2048]{1,0:T(8,128)(2,1)} %bitcast.88, bf16[1024,2048]{1,0:T(8,128)(2,1)} %bitcast.90, f32[1,2048]{1,0:T(1,128)} %bitcast.113, f32[1,2048]{1,0:T(1,128)} %bitcast.114), custom_call_target="tpu_custom_call" | custom-call | bytes 34000000 | tf_op jit(solution)/shard_map/prepare/pallas_call | solution.py:156
  46.6 4.0 collective-permute-done.3.refs_11_.refs_5_
  52.0 5.0 collective-permute-done.5.refs_19_
  57.0 3.4 collective-permute-done.2.refs_7_.refs_8_
  68.2 20.2 %project.1 = (bf16[1,4,512,128]{3,2,1,0:T(8,128)(2,1)}, bf16[1,4,512,128]{3,2,1,0:T(8,128)(2,1)}, bf16[2,4,512,128]{3,2,1,0:T(8,128)(2,1)}, bf16[1,4,512,128]{3,...) custom-call(s32[1]{0:T(128)} %bitcast.2.k_ref, s32[1]{0:T(128)} %bitcast.1.c_ref.me_ref, ...), custom_call_target="tpu_custom_call" | custom-call | bytes 64600000 | tf_op jit(solution)/shard_map/project/pallas_call | solution.py:249
  92.4 30.1 %feed.2 = (bf16[1024,1024]{1,0:T(8,128)(2,1)}, bf16[1024,1024]{1,0:T(8,128)(2,1)}, f32[1,1024]{1,0:T(1,128)}, bf16[1024,2048]{1,0:T(8,128)(2,1)}, bf16[1024,2048]{1,0:T(8,128)(2,1)}) custom-call(s32[1]{0:T(128)} %bitcast.2.k_ref, bf16[1024,2048]{1,0:T(8,128)(2,1)} %get-tuple-element.193.refs_0_.refs_1_.refs_2_.refs_3_, ...), custom_call_target="tpu_custom_call" | custom-call | bytes 105400000 | tf_op jit(solution)/shard_map/feed/pallas_call | solution.py:591
  125.9 2.1 collective-permute-done.16.refs_3_
  128.8 20.7 %attend.2 = (bf16[1,4,512,128]{3,2,1,0:T(8,128)(2,1)}, bf16[1,4,512,128]{3,2,1,0:T(8,128)(2,1)}, bf16[2,4,512,128]{3,2,1,0:T(8,128)(2,1)}) custom-call(s32[1]{0:T(128)} %bitcast.1.c_ref.me_ref, bf16[1,4,512,128]{3,2,1,0:T(8,128)(2,1)} %get-tuple-element.178.refs_0_, bf16[1,4,512,128]{3,2,1,0:T(8,128)(2,1)} %collective-permute-done.15.refs_1_, ...), custom_call_target="tpu_custom_call" | custom-call | bytes 95200000 | tf_op jit(solution)/shard_map/attend/pallas_call | solution.py:377
  149.7 2.5 collective-permute-done.23.refs_17_.refs_18_
  153.2 31.7 %feed.3 = (bf16[1024,1024]{1,0:T(8,128)(2,1)}, bf16[1024,1024]{1,0:T(8,128)(2,1)}, f32[1,1024]{1,0:T(1,128)}, bf16[1024,2048]{1,0:T(8,128)(2,1)}, bf16[1024,2048]{1,0:T(8,128)(2,1)}) custom-call(s32[1]{0:T(128)} %bitcast.2.k_ref, bf16[1024,2048]{1,0:T(8,128)(2,1)} %get-tuple-element.193.refs_0_.refs_1_.refs_2_.refs_3_, ...), custom_call_target="tpu_custom_call" | custom-call | bytes 105400000 | tf_op jit(solution)/shard_map/feed/pallas_call | solution.py:591
  185.1 2.2 fusion.25
  189.9 11.6 %outer.6 = bf16[2,512,2048]{2,1,0:T(8,128)(2,1)} custom-call(bf16[1024,2048]{1,0:T(8,128)(2,1)} %get-tuple-element.193.refs_0_.refs_1_.refs_2_.refs_3_, bf16[1024,2048]{1,0:T(8,128)(2,1)} %get-tuple-element.193.refs_0_.refs_1_.refs_2_.refs_3_, bf16[1024,2048]{1,0:T(8,128)(2,1)} %get-tuple-element.160.refs_1_.refs_2_.refs_3_.refs_0_, ...), custom_call_target="tpu_custom_call" | custom-call | bytes 37400000 | tf_op jit(solution)/shard_map/outer/pallas_call | solution.py:685
  203.2 20.7 %attend.3 = (bf16[1,4,512,128]{3,2,1,0:T(8,128)(2,1)}, bf16[1,4,512,128]{3,2,1,0:T(8,128)(2,1)}, bf16[2,4,512,128]{3,2,1,0:T(8,128)(2,1)}) custom-call(s32[1]{0:T(128)} %bitcast.1.c_ref.me_ref, bf16[1,4,512,128]{3,2,1,0:T(8,128)(2,1)} %get-tuple-element.201.refs_0_, bf16[1,4,512,128]{3,2,1,0:T(8,128)(2,1)} %copy-done.36, ...), custom_call_target="tpu_custom_call" | custom-call | bytes 95200000 | tf_op jit(solution)/shard_map/attend/pallas_call | solution.py:377
  224.4 3.1 collective-permute-done.17
  228.9 2.1 collective-permute-done.25.refs_3_
  232.1 4.2 unturn.2
  236.3 9.5 %norm_back.2.refs_8_ = bf16[4,2,128,2048]{3,2,1,0:T(8,128)(2,1)} custom-call(s32[1]{0:T(128)} %bitcast.2.k_ref, bf16[1024,1536]{1,0:T(8,128)(2,1)} %get-tuple-element.212.raw.refs_8_, bf16[1024,2048]{1,0:T(8,128)(2,1)} %get-tuple-element.213.back, bf16[3,1024,512]{2,1,0:T(8,128)(2,1)} %refs_3_.7, bf16[3,1024,512]{2,1,0:T(8,128)(2,1)} %refs_3_.7, ...), custom_call_target="tpu_custom_call" | custom-call | bytes 27200000 | tf_op jit(solution)/shard_map/norm_back/pallas_call | solution.py:482
  245.8 11.5 %outer.7 = (bf16[512,1024]{1,0:T(8,128)(2,1)}, bf16[512,1024]{1,0:T(8,128)(2,1)}, bf16[512,1024]{1,0:T(8,128)(2,1)}, bf16[512,1024]{1,0:T(8,128)(2,1)}) custom-call(bf16[1024,2048]{1,0:T(8,128)(2,1)} %get-tuple-element.193.refs_0_.refs_1_.refs_2_.refs_3_, bf16[1024,2048]{1,0:T(8,128)(2,1)} %get-tuple-element.193.refs_0_.refs_1_.refs_2_.refs_3_, ...), custom_call_target="tpu_custom_call" | custom-call | bytes 37400000 | tf_op jit(solution)/shard_map/outer/pallas_call | solution.py:685
  260.3 2.6 collective-permute-start.29
  264.2 4.2 unturn.3
  270.1 3.5 collective-permute-start.35
  274.0 9.2 %norm_back.3 = bf16[4,2,128,2048]{3,2,1,0:T(8,128)(2,1)} custom-call(s32[1]{0:T(128)} %bitcast.2.k_ref, bf16[1024,1536]{1,0:T(8,128)(2,1)} %get-tuple-element.225.raw.refs_5_, bf16[1024,2048]{1,0:T(8,128)(2,1)} %get-tuple-element.213.back, bf16[3,1024,512]{2,1,0:T(8,128)(2,1)} %refs_3_.7, ...), custom_call_target="tpu_custom_call", output_to_operand_aliasing={{}: (11, {})} | custom-call | bytes 27200000 | tf_op jit(solution)/shard_map/norm_back/pallas_call | solution.py:482
  286.2 1.9 collective-permute-start.27
  293.1 10.3 %outer.8 = bf16[2,512,2048]{2,1,0:T(8,128)(2,1)} custom-call(bf16[1024,2048]{1,0:T(8,128)(2,1)} %get-tuple-element.193.refs_0_.refs_1_.refs_2_.refs_3_, bf16[1024,2048]{1,0:T(8,128)(2,1)} %get-tuple-element.193.refs_0_.refs_1_.refs_2_.refs_3_, bf16[1024,2048]{1,0:T(8,128)(2,1)} %get-tuple-element.160.refs_1_.refs_2_.refs_3_.refs_0_, ...), custom_call_target="tpu_custom_call" | custom-call | bytes 37400000 | tf_op jit(solution)/shard_map/outer/pallas_call | solution.py:685
  303.6 8.4 %collective-permute-done.27 = bf16[512,1024]{1,0:T(8,128)(2,1)} collective-permute-done((bf16[512,1024]{1,0:T(8,128)(2,1)S(1)}, bf16[512,1024]{1,0:T(8,128)(2,1)}, u32[]{:S(2)}, u32[]{:S(2)}) %collective-permute-start.27) | collective-permute-done | bytes 1048608 | tf_op jit(solution)/shard_map/ppermute | solution.py:45
  318.4 3.5 fusion.30
  325.5 2.6 fusion.14
  328.2 11.8 %outer.9 = (bf16[512,1024]{1,0:T(8,128)(2,1)}, bf16[512,1024]{1,0:T(8,128)(2,1)}, bf16[512,1024]{1,0:T(8,128)(2,1)}, bf16[512,1024]{1,0:T(8,128)(2,1)}) custom-call(bf16[1024,2048]{1,0:T(8,128)(2,1)} %get-tuple-element.193.refs_0_.refs_1_.refs_2_.refs_3_, bf16[1024,2048]{1,0:T(8,128)(2,1)} %get-tuple-element.193.refs_0_.refs_1_.refs_2_.refs_3_, ...), custom_call_target="tpu_custom_call" | custom-call | bytes 37400000 | tf_op jit(solution)/shard_map/outer/pallas_call | solution.py:685
  340.0 10.5 %outer.10 = bf16[2,512,2048]{2,1,0:T(8,128)(2,1)} custom-call(bf16[1024,2048]{1,0:T(8,128)(2,1)} %get-tuple-element.160.refs_1_.refs_2_.refs_3_.refs_0_, bf16[1024,2048]{1,0:T(8,128)(2,1)} %get-tuple-element.160.refs_1_.refs_2_.refs_3_.refs_0_, bf16[1024,2048]{1,0:T(8,128)(2,1)} %get-tuple-element.193.refs_0_.refs_1_.refs_2_.refs_3_, ...), custom_call_target="tpu_custom_call" | custom-call | bytes 37400000 | tf_op jit(solution)/shard_map/outer/pallas_call | solution.py:685
  350.5 1.9 add_convert_fusion.3.left
  354.5 2.4 add_turned.6.refs_0_
  357.0 4.8 reduce-scatter.5.cloned.1.call-done
  371.5 1.9 fusion.5
  373.4 6.8 %collective-permute-done.41 = bf16[512,1024]{1,0:T(8,128)(2,1)} collective-permute-done((bf16[512,1024]{1,0:T(8,128)(2,1)}, bf16[512,1024]{1,0:T(8,128)(2,1)}, u32[]{:S(2)}, u32[]{:S(2)}) %collective-permute-start.41) | collective-permute-done | bytes 1048608 | tf_op jit(solution)/shard_map/ppermute | solution.py:45
  384.3 2.5 add_turned.7.refs_0_
  386.8 11.8 %outer.11 = (bf16[512,512]{1,0:T(8,128)(2,1)}, bf16[512,1536]{1,0:T(8,128)(2,1)}, bf16[512,512]{1,0:T(8,128)(2,1)}, bf16[512,1536]{1,0:T(8,128)(2,1)}) custom-call(bf16[1024,2048]{1,0:T(8,128)(2,1)} %get-tuple-element.160.refs_1_.refs_2_.refs_3_.refs_0_, bf16[1024,2048]{1,0:T(8,128)(2,1)} %get-tuple-element.160.refs_1_.refs_2_.refs_3_.refs_0_, ...), custom_call_target="tpu_custom_call" | custom-call | bytes 37400000 | tf_op jit(solution)/shard_map/outer/pallas_call | solution.py:685
  398.7 9.2 %collective-permute-done.46 = f32[1,9728]{1,0:T(1,128)S(1)} collective-permute-done((f32[1,9728]{1,0:T(1,128)S(1)}, f32[1,9728]{1,0:T(1,128)S(1)}, u32[]{:S(2)}, u32[]{:S(2)}) %collective-permute-start.46) | collective-permute-done | bytes 38944 | tf_op jit(solution)/shard_map/ppermute | solution.py:45
  409.7 2.2 collective-permute-done.48
  415.1 1.9 add_convert_fusion.1.left
  417.1 2.8 add_turned.8.refs_2_
  420.9 2.2 collective-permute-done.52.refs_3_
  423.0 6.3 %finish.4 = f32[1024,2048]{1,0:T(8,128)} custom-call(s32[1]{0:T(128)} %bitcast.2.k_ref, bf16[512,1024]{1,0:T(8,128)(2,1)} %add_turned.6.refs_0_, bf16[512,1024]{1,0:T(8,128)(2,1)} %collective-permute-done.51.refs_1_, bf16[512,1024]{1,0:T(8,128)(2,1)} %add_turned.8.refs_2_, bf16[512,1024]{1,0:T(8,128)(2,1)} %collective-permute-done.52.refs_3_), custom_call_target="tpu_custom_call" | custom-call | bytes 20400000 | tf_op jit(solution)/shard_map/finish/pallas_call | solution.py:761
  429.4 16.1 %collective-permute-done.50.right = bf16[512,1024]{1,0:T(8,128)(2,1)S(1)} collective-permute-done((bf16[512,1024]{1,0:T(8,128)(2,1)S(1)}, bf16[512,1024]{1,0:T(8,128)(2,1)S(1)}, u32[]{:S(2)}, u32[]{:S(2)}) %collective-permute-start.50) | collective-permute-done | bytes 1048608 | tf_op jit(solution)/shard_map/ppermute | solution.py:50
  445.5 2.6 collective-permute-done.49
  448.1 2.4 add_convert_fusion.left
  452.1 2.6 add_turned.9.refs_2_
  455.7 2.1 collective-permute-done.55.refs_3_
  457.8 6.4 %finish.5 = f32[2048,1024]{1,0:T(8,128)} custom-call(s32[1]{0:T(128)} %bitcast.2.k_ref, bf16[512,1024]{1,0:T(8,128)(2,1)} %add_turned.7.refs_0_, bf16[512,1024]{1,0:T(8,128)(2,1)} %collective-permute-done.54.refs_1_, bf16[512,1024]{1,0:T(8,128)(2,1)} %add_turned.9.refs_2_, bf16[512,1024]{1,0:T(8,128)(2,1)} %collective-permute-done.55.refs_3_), custom_call_target="tpu_custom_call" | custom-call | bytes 20400000 | tf_op jit(solution)/shard_map/finish/pallas_call | solution.py:761
  464.2 5.1 collective-permute-done.53
  469.5 15.1 %collective-permute-done.56.right = bf16[512,1536]{1,0:T(8,128)(2,1)} collective-permute-done((bf16[512,1536]{1,0:T(8,128)(2,1)S(1)}, bf16[512,1536]{1,0:T(8,128)(2,1)}, u32[]{:S(2)}, u32[]{:S(2)}) %collective-permute-start.56) | collective-permute-done | bytes 1572896 | tf_op jit(solution)/shard_map/ppermute | solution.py:50
  484.6 2.9 add_turned.10.refs_0_
  488.5 2.6 collective-permute-done.57.refs_1_
  492.2 5.3 finish.6
  497.6 4.3 collective-permute-done.58.right
  502.6 2.0 add_turned.11.refs_0_
  505.8 4.8 copy.35
  511.5 3.8 finish.7
  515.4 14.2 %all-gather.9.cloned.1.call-done = bf16[1088,2048]{1,0:T(8,128)(2,1)} async-done(((bf16[272,2048]{1,0:T(8,128)(2,1)}), bf16[1088,2048]{1,0:T(8,128)(2,1)}) %all-gather.9.cloned.1.call-update) | async-done | bytes 4456464 | tf_op jit(solution)/shard_map/all_gather | solution.py:1128
  529.6 2.5 slice.131
  533.1 2.3 copy.36
  (343 shorter events, 98.2 us)
Async XLA Ops:
  7.2 277.4 %all-gather.5.cloned.1.call-start = ((), (), s32[]{:S(2)}) async-start(), calls=%async_computation.2 | async-start | bytes 5242880 | tf_op jit(solution)/shard_map/all_gather | solution.py:883
  9.3 21.0 %collective-permute-start.1 = (bf16[3,256,512]{2,1,0:T(8,128)(2,1)}, bf16[3,256,512]{2,1,0:T(8,128)(2,1)S(1)}, u32[]{:S(2)}, u32[]{:S(2)}) collective-permute-start(bf16[3,256,512]{2,1,0:T(8,128)(2,1)} %constant_dynamic-slice_fusion.25), channel_id=1, source_target_pairs={{0,16},{16,0},{1,17},{17,1},{2,18},{18,2},{3,19},{19,3},{4,20},{20... | collective-permute-start | bytes 2359304 | tf_op jit(solution)/shard_map/ppermute | solution.py:45
  16.4 13.9 %collective-permute-start = (bf16[5888]{0:T(1024)(128)(2,1)S(1)}, bf16[5888]{0:T(1024)(128)(2,1)S(1)}, u32[]{:S(2)}, u32[]{:S(2)}) collective-permute-start(bf16[5888]{0:T(1024)(128)(2,1)S(1)} %constant_dynamic-update-slice_fusion.28), channel_id=1, source_target_pairs={{0,16},{16,0},{1,17},{17,1},{2,18},{18,2},{3,19},{19,3},{4,20},{20... | collective-permute-start | bytes 35336 | tf_op jit(solution)/shard_map/ppermute | solution.py:45
  30.3 16.2 %collective-permute-start.4 = (bf16[512,256]{1,0:T(8,128)(2,1)S(1)}, bf16[512,256]{1,0:T(8,128)(2,1)S(1)}, u32[]{:S(2)}, u32[]{:S(2)}) collective-permute-start(bf16[512,256]{1,0:T(8,128)(2,1)S(1)} %get-tuple-element.153), channel_id=1, source_target_pairs={{0,16},{16,0},{1,17},{17,1},{2,18},{18,2},{3,19},{19,3},{4,20},{20... | collective-permute-start | bytes 786440 | tf_op jit(solution)/shard_map/ppermute | solution.py:45
  32.2 28.2 %collective-permute-start.2 = (bf16[512,1024]{1,0:T(8,128)(2,1)}, bf16[512,1024]{1,0:T(8,128)(2,1)S(1)}, u32[]{:S(2)}, u32[]{:S(2)}) collective-permute-start(bf16[512,1024]{1,0:T(8,128)(2,1)} %get-tuple-element.152), channel_id=1, source_target_pairs={{0,16},{16,0},{1,17},{17,1},{2,18},{18,2},{3,19},{19,3},{4,20},{20... | collective-permute-start | bytes 3145736 | tf_op jit(solution)/shard_map/ppermute | solution.py:45
  32.4 18.2 %collective-permute-start.3 = (bf16[3,256,512]{2,1,0:T(8,128)(2,1)S(1)}, bf16[3,256,512]{2,1,0:T(8,128)(2,1)S(1)}, u32[]{:S(2)}, u32[]{:S(2)}) collective-permute-start(bf16[3,256,512]{2,1,0:T(8,128)(2,1)S(1)} %collective-permute-done.1.refs_10_.refs_4_), channel_id=1, source_target_pairs={{0,8},{4,12},{8,0},{12,4},{1,9},{5,13},{9,1},{13,5},{2,10},{6,14},... | collective-permute-start | bytes 2359304 | tf_op jit(solution)/shard_map/ppermute | solution.py:50
  50.6 6.4 %collective-permute-start.5 = (bf16[512,256]{1,0:T(8,128)(2,1)S(1)}, bf16[512,256]{1,0:T(8,128)(2,1)S(1)}, u32[]{:S(2)}, u32[]{:S(2)}) collective-permute-start(bf16[512,256]{1,0:T(8,128)(2,1)S(1)} %collective-permute-done.4.refs_18_), channel_id=1, source_target_pairs={{0,8},{4,12},{8,0},{12,4},{1,9},{5,13},{9,1},{13,5},{2,10},{6,14},... | collective-permute-start | bytes 786440 | tf_op jit(solution)/shard_map/ppermute | solution.py:50
  61.6 261.4 %reduce-scatter.3.cloned.1.call-start = ((), (), s32[]{:S(2)}) async-start(), calls=%async_computation.3 | async-start | bytes 5242880 | tf_op jit(solution)/shard_map/reduce_scatter | solution.py:960
  61.7 26.8 %collective-permute-start.11 = (bf16[1024,512]{1,0:T(8,128)(2,1)}, bf16[1024,512]{1,0:T(8,128)(2,1)}, u32[]{:S(2)}, u32[]{:S(2)}) collective-permute-start(bf16[1024,512]{1,0:T(8,128)(2,1)} %get-tuple-element.171), channel_id=1, source_target_pairs={{0,16},{16,0},{1,17},{17,1},{2,18},{18,2},{3,19},{19,3},{4,20},{20... | collective-permute-start | bytes 3145736 | tf_op jit(solution)/shard_map/ppermute | solution.py:45
  63.2 3.8 collective-permute-start.6
  63.2 4.2 collective-permute-start.7
  63.7 3.0 collective-permute-start.8
  63.8 3.2 collective-permute-start.9
  66.7 24.3 %collective-permute-start.13 = (bf16[512,1024]{1,0:T(8,128)(2,1)}, bf16[512,1024]{1,0:T(8,128)(2,1)}, u32[]{:S(2)}, u32[]{:S(2)}) collective-permute-start(bf16[512,1024]{1,0:T(8,128)(2,1)} %copy-done.15), channel_id=1, source_target_pairs={{0,4},{4,0},{8,12},{12,8},{1,5},{5,1},{9,13},{13,9},{2,6},{6,2},{1... | collective-permute-start | bytes 3145736 | tf_op jit(solution)/shard_map/ppermute | solution.py:50
  88.5 2.9 collective-permute-start.14
  88.7 33.8 %collective-permute-start.12 = (bf16[512,1024]{1,0:T(8,128)(2,1)}, bf16[512,1024]{1,0:T(8,128)(2,1)S(1)}, u32[]{:S(2)}, u32[]{:S(2)}) collective-permute-start(bf16[512,1024]{1,0:T(8,128)(2,1)} %get-tuple-element.173), channel_id=1, source_target_pairs={{0,16},{16,0},{1,17},{17,1},{2,18},{18,2},{3,19},{19,3},{4,20},{20... | collective-permute-start | bytes 3145736 | tf_op jit(solution)/shard_map/ppermute | solution.py:45
  89.1 33.5 %collective-permute-start.10 = (bf16[2,4,512,128]{3,2,1,0:T(8,128)(2,1)}, bf16[2,4,512,128]{3,2,1,0:T(8,128)(2,1)S(1)}, u32[]{:S(2)}, u32[]{:S(2)}) collective-permute-start(bf16[2,4,512,128]{3,2,1,0:T(8,128)(2,1)} %get-tuple-element.168), channel_id=1, source_target_pairs={{0,8},{4,12},{8,0},{12,4},{1,9},{5,13},{9,1},{13,5},{2,10},{6,14},... | collective-permute-start | bytes 3145736 | tf_op jit(solution)/shard_map/ppermute | solution.py:50
  122.5 27.0 %collective-permute-start.18 = (bf16[2,4,512,128]{3,2,1,0:T(8,128)(2,1)}, bf16[2,4,512,128]{3,2,1,0:T(8,128)(2,1)}, u32[]{:S(2)}, u32[]{:S(2)}) collective-permute-start(bf16[2,4,512,128]{3,2,1,0:T(8,128)(2,1)} %get-tuple-element.187), channel_id=1, source_target_pairs={{0,8},{4,12},{8,0},{12,4},{1,9},{5,13},{9,1},{13,5},{2,10},{6,14},... | collective-permute-start | bytes 3145736 | tf_op jit(solution)/shard_map/ppermute | solution.py:50
  124.1 25.4 %collective-permute-start.21 = (bf16[1024,512]{1,0:T(8,128)(2,1)}, bf16[1024,512]{1,0:T(8,128)(2,1)S(1)}, u32[]{:S(2)}, u32[]{:S(2)}) collective-permute-start(bf16[1024,512]{1,0:T(8,128)(2,1)} %get-tuple-element.191), channel_id=1, source_target_pairs={{0,16},{16,0},{1,17},{17,1},{2,18},{18,2},{3,19},{19,3},{4,20},{20... | collective-permute-start | bytes 3145736 | tf_op jit(solution)/shard_map/ppermute | solution.py:45
  125.4 2.6 collective-permute-start.16
  125.4 3.2 collective-permute-start.15
  125.9 23.8 %collective-permute-start.22 = (bf16[512,1024]{1,0:T(8,128)(2,1)S(1)}, bf16[512,1024]{1,0:T(8,128)(2,1)S(1)}, u32[]{:S(2)}, u32[]{:S(2)}) collective-permute-start(bf16[512,1024]{1,0:T(8,128)(2,1)S(1)} %collective-permute-done.12.refs_7_.refs_8_), channel_id=1, source_target_pairs={{0,4},{4,0},{8,12},{12,8},{1,5},{5,1},{9,13},{13,9},{2,6},{6,2},{1... | collective-permute-start | bytes 3145736 | tf_op jit(solution)/shard_map/ppermute | solution.py:50
  149.5 2.7 collective-permute-start.23
  185.0 176.8 %reduce-scatter.5.cloned.1.call-start = ((), (), s32[]{:S(2)}) async-start(), calls=%async_computation.5 | async-start | bytes 5242880 | tf_op jit(solution)/shard_map/reduce_scatter | solution.py:1050
  187.4 2.5 collective-permute-start.19
  201.5 44.2 %collective-permute-start.26 = (bf16[2,512,2048]{2,1,0:T(8,128)(2,1)}, bf16[2,512,2048]{2,1,0:T(8,128)(2,1)}, u32[]{:S(2)}, u32[]{:S(2)}) collective-permute-start(bf16[2,512,2048]{2,1,0:T(8,128)(2,1)} %outer.6), channel_id=1, source_target_pairs={{0,4},{4,0},{8,12},{12,8},{1,5},{5,1},{9,13},{13,9},{2,6},{6,2},{1... | collective-permute-start | bytes 12582920 | tf_op jit(solution)/shard_map/ppermute | solution.py:50
  201.8 25.8 %collective-permute-start.17 = (bf16[2,4,512,128]{3,2,1,0:T(8,128)(2,1)S(1)}, bf16[2,4,512,128]{3,2,1,0:T(8,128)(2,1)S(1)}, u32[]{:S(2)}, u32[]{:S(2)}) collective-permute-start(bf16[2,4,512,128]{3,2,1,0:T(8,128)(2,1)S(1)} %copy-done.57), channel_id=1, source_target_pairs={{0,8},{4,12},{8,0},{12,4},{1,9},{5,13},{9,1},{13,5},{2,10},{6,14},... | collective-permute-start | bytes 3145736 | tf_op jit(solution)/shard_map/ppermute | solution.py:50
  223.9 33.4 %collective-permute-start.31 = (bf16[2,4,512,128]{3,2,1,0:T(8,128)(2,1)}, bf16[2,4,512,128]{3,2,1,0:T(8,128)(2,1)S(1)}, u32[]{:S(2)}, u32[]{:S(2)}) collective-permute-start(bf16[2,4,512,128]{3,2,1,0:T(8,128)(2,1)} %get-tuple-element.218), channel_id=1, source_target_pairs={{0,8},{4,12},{8,0},{12,4},{1,9},{5,13},{9,1},{13,5},{2,10},{6,14},... | collective-permute-start | bytes 3145736 | tf_op jit(solution)/shard_map/ppermute | solution.py:50
  228.4 2.6 collective-permute-start.25
  228.4 2.9 collective-permute-start.24
  258.2 5.0 collective-permute-start.33
  258.4 4.9 collective-permute-start.32
  258.8 14.9 %collective-permute-start.28 = (bf16[128,512]{1,0:T(8,128)(2,1)S(1)}, bf16[128,512]{1,0:T(8,128)(2,1)S(1)}, u32[]{:S(2)}, u32[]{:S(2)}) collective-permute-start(bf16[128,512]{1,0:T(8,128)(2,1)S(1)} %get-tuple-element.330), channel_id=1, source_target_pairs={{0,1},{1,0},{2,3},{3,2},{4,5},{5,4},{6,7},{7,6},{8,9},{9,8},{10,11... | collective-permute-start | bytes 393224 | tf_op jit(solution)/shard_map/ppermute | solution.py:55
  260.3 22.9 %collective-permute-start.29 = (bf16[128,512]{1,0:T(8,128)(2,1)S(1)}, bf16[128,512]{1,0:T(8,128)(2,1)S(1)}, u32[]{:S(2)}, u32[]{:S(2)}) collective-permute-start(bf16[128,512]{1,0:T(8,128)(2,1)S(1)} %get-tuple-element.329), channel_id=1, source_target_pairs={{0,2},{1,3},{2,0},{3,1},{4,6},{5,7},{6,4},{7,5},{8,10},{9,11},{10,... | collective-permute-start | bytes 393224 | tf_op jit(solution)/shard_map/ppermute | solution.py:55
  262.9 20.4 %collective-permute-start.30 = (bf16[128,512]{1,0:T(8,128)(2,1)S(1)}, bf16[128,512]{1,0:T(8,128)(2,1)S(1)}, u32[]{:S(2)}, u32[]{:S(2)}) collective-permute-start(bf16[128,512]{1,0:T(8,128)(2,1)S(1)} %get-tuple-element.328), channel_id=1, source_target_pairs={{0,3},{1,2},{2,1},{3,0},{4,7},{5,6},{6,5},{7,4},{8,11},{9,10},{10,... | collective-permute-start | bytes 393224 | tf_op jit(solution)/shard_map/ppermute | solution.py:55
  269.5 13.7 %collective-permute-start.34 = (bf16[128,512]{1,0:T(8,128)(2,1)S(1)}, bf16[128,512]{1,0:T(8,128)(2,1)S(1)}, u32[]{:S(2)}, u32[]{:S(2)}) collective-permute-start(bf16[128,512]{1,0:T(8,128)(2,1)S(1)} %get-tuple-element.325), channel_id=1, source_target_pairs={{0,1},{1,0},{2,3},{3,2},{4,5},{5,4},{6,7},{7,6},{8,9},{9,8},{10,11... | collective-permute-start | bytes 393224 | tf_op jit(solution)/shard_map/ppermute | solution.py:55
  270.1 14.3 %collective-permute-start.35 = (bf16[128,512]{1,0:T(8,128)(2,1)S(1)}, bf16[128,512]{1,0:T(8,128)(2,1)S(1)}, u32[]{:S(2)}, u32[]{:S(2)}) collective-permute-start(bf16[128,512]{1,0:T(8,128)(2,1)S(1)} %get-tuple-element.324), channel_id=1, source_target_pairs={{0,2},{1,3},{2,0},{3,1},{4,6},{5,7},{6,4},{7,5},{8,10},{9,11},{10,... | collective-permute-start | bytes 393224 | tf_op jit(solution)/shard_map/ppermute | solution.py:55
  273.6 10.8 %collective-permute-start.36 = (bf16[128,512]{1,0:T(8,128)(2,1)S(1)}, bf16[128,512]{1,0:T(8,128)(2,1)}, u32[]{:S(2)}, u32[]{:S(2)}) collective-permute-start(bf16[128,512]{1,0:T(8,128)(2,1)S(1)} %get-tuple-element.323), channel_id=1, source_target_pairs={{0,3},{1,2},{2,1},{3,0},{4,7},{5,6},{6,5},{7,4},{8,11},{9,10},{10,... | collective-permute-start | bytes 393224 | tf_op jit(solution)/shard_map/ppermute | solution.py:55
  284.5 221.4 %all-gather.7.cloned.1.call-start = ((), (), s32[]{:S(2)}) async-start(), calls=%async_computation.4 | async-start | bytes 5242880 | tf_op jit(solution)/shard_map/all_gather | solution.py:1081
  284.5 33.9 %collective-permute-start.37 = (bf16[2048,1024]{1,0:T(8,128)(2,1)}, bf16[2048,1024]{1,0:T(8,128)(2,1)}, u32[]{:S(2)}, u32[]{:S(2)}) collective-permute-start(bf16[2048,1024]{1,0:T(8,128)(2,1)} %all-gather.5.cloned.1.call-done), channel_id=1, source_target_pairs={{0,4},{4,0},{8,12},{12,8},{1,5},{5,1},{9,13},{13,9},{2,6},{6,2},{1... | collective-permute-start | bytes 12582920 | tf_op jit(solution)/shard_map/ppermute | solution.py:50
  286.2 25.7 %collective-permute-start.27 = (bf16[512,1024]{1,0:T(8,128)(2,1)S(1)}, bf16[512,1024]{1,0:T(8,128)(2,1)}, u32[]{:S(2)}, u32[]{:S(2)}) collective-permute-start(bf16[512,1024]{1,0:T(8,128)(2,1)S(1)} %copy-done.56), channel_id=1, source_target_pairs={{0,16},{16,0},{1,17},{17,1},{2,18},{18,2},{3,19},{19,3},{4,20},{20... | collective-permute-start | bytes 3145736 | tf_op jit(solution)/shard_map/ppermute | solution.py:45
  303.5 24.8 %collective-permute-start.40 = (bf16[2,512,2048]{2,1,0:T(8,128)(2,1)}, bf16[2,512,2048]{2,1,0:T(8,128)(2,1)}, u32[]{:S(2)}, u32[]{:S(2)}) collective-permute-start(bf16[2,512,2048]{2,1,0:T(8,128)(2,1)} %outer.8), channel_id=1, source_target_pairs={{0,4},{4,0},{8,12},{12,8},{1,5},{5,1},{9,13},{13,9},{2,6},{6,2},{1... | collective-permute-start | bytes 12582920 | tf_op jit(solution)/shard_map/ppermute | solution.py:50
  313.7 36.8 %collective-permute-start.39 = (bf16[512,1024]{1,0:T(8,128)(2,1)S(1)}, bf16[512,1024]{1,0:T(8,128)(2,1)}, u32[]{:S(2)}, u32[]{:S(2)}) collective-permute-start(bf16[512,1024]{1,0:T(8,128)(2,1)S(1)} %add_convert_fusion.4.left), channel_id=1, source_target_pairs={{0,8},{4,12},{8,0},{12,4},{1,9},{5,13},{9,1},{13,5},{2,10},{6,14},... | collective-permute-start | bytes 3145736 | tf_op jit(solution)/shard_map/ppermute | solution.py:50
  315.5 35.0 %collective-permute-start.38 = (bf16[512,1024]{1,0:T(8,128)(2,1)}, bf16[512,1024]{1,0:T(8,128)(2,1)}, u32[]{:S(2)}, u32[]{:S(2)}) collective-permute-start(bf16[512,1024]{1,0:T(8,128)(2,1)} %get-tuple-element.248), channel_id=1, source_target_pairs={{0,16},{16,0},{1,17},{17,1},{2,18},{18,2},{3,19},{19,3},{4,20},{20... | collective-permute-start | bytes 3145736 | tf_op jit(solution)/shard_map/ppermute | solution.py:45
  328.2 201.4 %all-gather.9.cloned.1.call-start = ((), (), s32[]{:S(2)}) async-start(), calls=%async_computation.6 | async-start | bytes 5570560 | tf_op jit(solution)/shard_map/all_gather | solution.py:1128
  352.5 27.7 %collective-permute-start.42 = (bf16[512,1024]{1,0:T(8,128)(2,1)S(1)}, bf16[512,1024]{1,0:T(8,128)(2,1)}, u32[]{:S(2)}, u32[]{:S(2)}) collective-permute-start(bf16[512,1024]{1,0:T(8,128)(2,1)S(1)} %add_convert_fusion.3.left), channel_id=1, source_target_pairs={{0,8},{4,12},{8,0},{12,4},{1,9},{5,13},{9,1},{13,5},{2,10},{6,14},... | collective-permute-start | bytes 3145736 | tf_op jit(solution)/shard_map/ppermute | solution.py:50
  354.3 32.5 %collective-permute-start.47 = (bf16[2,512,2048]{2,1,0:T(8,128)(2,1)}, bf16[2,512,2048]{2,1,0:T(8,128)(2,1)}, u32[]{:S(2)}, u32[]{:S(2)}) collective-permute-start(bf16[2,512,2048]{2,1,0:T(8,128)(2,1)} %outer.10), channel_id=1, source_target_pairs={{0,4},{4,0},{8,12},{12,8},{1,5},{5,1},{9,13},{13,9},{2,6},{6,2},{1... | collective-permute-start | bytes 12582920 | tf_op jit(solution)/shard_map/ppermute | solution.py:50
  354.3 25.9 %collective-permute-start.41 = (bf16[512,1024]{1,0:T(8,128)(2,1)}, bf16[512,1024]{1,0:T(8,128)(2,1)}, u32[]{:S(2)}, u32[]{:S(2)}) collective-permute-start(bf16[512,1024]{1,0:T(8,128)(2,1)} %get-tuple-element.260), channel_id=1, source_target_pairs={{0,16},{16,0},{1,17},{17,1},{2,18},{18,2},{3,19},{19,3},{4,20},{20... | collective-permute-start | bytes 3145736 | tf_op jit(solution)/shard_map/ppermute | solution.py:45
  371.4 8.9 %collective-permute-start.43 = (f32[1,9728]{1,0:T(1,128)S(1)}, f32[1,9728]{1,0:T(1,128)S(1)}, u32[]{:S(2)}, u32[]{:S(2)}) collective-permute-start(f32[1,9728]{1,0:T(1,128)S(1)} %constant_dynamic-update-slice_fusion.17), channel_id=1, source_target_pairs={{0,4},{4,0},{8,12},{12,8},{1,5},{5,1},{9,13},{13,9},{2,6},{6,2},{1... | collective-permute-start | bytes 116744 | tf_op jit(solution)/shard_map/ppermute | solution.py:50
  381.9 26.0 %collective-permute-start.45 = (bf16[512,1024]{1,0:T(8,128)(2,1)S(1)}, bf16[512,1024]{1,0:T(8,128)(2,1)}, u32[]{:S(2)}, u32[]{:S(2)}) collective-permute-start(bf16[512,1024]{1,0:T(8,128)(2,1)S(1)} %add_convert_fusion.2.left), channel_id=1, source_target_pairs={{0,8},{4,12},{8,0},{12,4},{1,9},{5,13},{9,1},{13,5},{2,10},{6,14},... | collective-permute-start | bytes 3145736 | tf_op jit(solution)/shard_map/ppermute | solution.py:50
  382.2 25.7 %collective-permute-start.44 = (bf16[512,1024]{1,0:T(8,128)(2,1)}, bf16[512,1024]{1,0:T(8,128)(2,1)}, u32[]{:S(2)}, u32[]{:S(2)}) collective-permute-start(bf16[512,1024]{1,0:T(8,128)(2,1)} %get-tuple-element.264), channel_id=1, source_target_pairs={{0,16},{16,0},{1,17},{17,1},{2,18},{18,2},{3,19},{19,3},{4,20},{20... | collective-permute-start | bytes 3145736 | tf_op jit(solution)/shard_map/ppermute | solution.py:45
  383.9 23.9 %collective-permute-start.46 = (f32[1,9728]{1,0:T(1,128)S(1)}, f32[1,9728]{1,0:T(1,128)S(1)}, u32[]{:S(2)}, u32[]{:S(2)}) collective-permute-start(f32[1,9728]{1,0:T(1,128)S(1)} %add.258), channel_id=1, source_target_pairs={{0,16},{16,0},{1,17},{17,1},{2,18},{18,2},{3,19},{19,3},{4,20},{20... | collective-permute-start | bytes 116744 | tf_op jit(solution)/shard_map/ppermute | solution.py:45
  407.9 4.0 collective-permute-start.48
  413.4 34.7 %collective-permute-start.49 = (bf16[512,1536]{1,0:T(8,128)(2,1)}, bf16[512,1536]{1,0:T(8,128)(2,1)}, u32[]{:S(2)}, u32[]{:S(2)}) collective-permute-start(bf16[512,1536]{1,0:T(8,128)(2,1)} %get-tuple-element.275), channel_id=1, source_target_pairs={{0,16},{16,0},{1,17},{17,1},{2,18},{18,2},{3,19},{19,3},{4,20},{20... | collective-permute-start | bytes 4718600 | tf_op jit(solution)/shard_map/ppermute | solution.py:45
  415.1 5.8 %collective-permute-start.51 = (bf16[512,1024]{1,0:T(8,128)(2,1)S(1)}, bf16[512,1024]{1,0:T(8,128)(2,1)}, u32[]{:S(2)}, u32[]{:S(2)}) collective-permute-start(bf16[512,1024]{1,0:T(8,128)(2,1)S(1)} %copy-done.13), channel_id=1, source_target_pairs={{0,4},{4,0},{8,12},{12,8},{1,5},{5,1},{9,13},{13,9},{2,6},{6,2},{1... | collective-permute-start | bytes 3145736 | tf_op jit(solution)/shard_map/ppermute | solution.py:50
  419.9 3.1 collective-permute-start.52
  420.4 25.1 %collective-permute-start.50 = (bf16[512,1024]{1,0:T(8,128)(2,1)S(1)}, bf16[512,1024]{1,0:T(8,128)(2,1)S(1)}, u32[]{:S(2)}, u32[]{:S(2)}) collective-permute-start(bf16[512,1024]{1,0:T(8,128)(2,1)S(1)} %add_convert_fusion.1.left), channel_id=1, source_target_pairs={{0,8},{4,12},{8,0},{12,4},{1,9},{5,13},{9,1},{13,5},{2,10},{6,14},... | collective-permute-start | bytes 3145736 | tf_op jit(solution)/shard_map/ppermute | solution.py:50
  450.5 34.1 %collective-permute-start.56 = (bf16[512,1536]{1,0:T(8,128)(2,1)S(1)}, bf16[512,1536]{1,0:T(8,128)(2,1)}, u32[]{:S(2)}, u32[]{:S(2)}) collective-permute-start(bf16[512,1536]{1,0:T(8,128)(2,1)S(1)} %add_convert_fusion.left), channel_id=1, source_target_pairs={{0,8},{4,12},{8,0},{12,4},{1,9},{5,13},{9,1},{13,5},{2,10},{6,14},... | collective-permute-start | bytes 4718600 | tf_op jit(solution)/shard_map/ppermute | solution.py:50
  452.1 3.6 collective-permute-start.54
  454.7 3.1 collective-permute-start.55
  455.2 14.1 %collective-permute-start.53 = (bf16[512,512]{1,0:T(8,128)(2,1)}, bf16[512,512]{1,0:T(8,128)(2,1)S(1)}, u32[]{:S(2)}, u32[]{:S(2)}) collective-permute-start(bf16[512,512]{1,0:T(8,128)(2,1)} %get-tuple-element.283), channel_id=1, source_target_pairs={{0,16},{16,0},{1,17},{17,1},{2,18},{18,2},{3,19},{19,3},{4,20},{20... | collective-permute-start | bytes 1572872 | tf_op jit(solution)/shard_map/ppermute | solution.py:45
  487.5 3.6 collective-permute-start.57
  487.5 14.3 %collective-permute-start.58 = (bf16[512,512]{1,0:T(8,128)(2,1)S(1)}, bf16[512,512]{1,0:T(8,128)(2,1)S(1)}, u32[]{:S(2)}, u32[]{:S(2)}) collective-permute-start(bf16[512,512]{1,0:T(8,128)(2,1)S(1)} %add_convert_fusion.5.left), channel_id=1, source_target_pairs={{0,8},{4,12},{8,0},{12,4},{1,9},{5,13},{9,1},{13,5},{2,10},{6,14},... | collective-permute-start | bytes 1572872 | tf_op jit(solution)/shard_map/ppermute | solution.py:50
  504.6 6.1 %collective-permute-start.59 = (bf16[512,512]{1,0:T(8,128)(2,1)}, bf16[512,512]{1,0:T(8,128)(2,1)S(1)}, u32[]{:S(2)}, u32[]{:S(2)}) collective-permute-start(bf16[512,512]{1,0:T(8,128)(2,1)} %add_turned.11.refs_0_), channel_id=1, source_target_pairs={{0,4},{4,0},{8,12},{12,8},{1,5},{5,1},{9,13},{13,9},{2,6},{6,2},{1... | collective-permute-start | bytes 1572872 | tf_op jit(solution)/shard_map/ppermute | solution.py:50
  (61 other events, 460.9 us)
Sparse Core Ops, SparseCore 0:
  61.8 81.9 all-gather.4
  185.1 77.0 reduce-scatter.2
  284.6 77.1 reduce-scatter.4
  363.2 81.2 all-gather.6
  445.9 83.6 all-gather.8

commit v3 on v2

--- a/solution.py
+++ b/solution.py
@@ -97,8 +97,11 @@
     def __init__(self, order, pairs, block):
         self.order, self.pairs, self.block = order, pairs, block
 
+    def compute(self):
+        (self.sent,) = outer(self.order, self.pairs, 1, None)
+
     def send(self):
-        (self.sent,) = outer(self.order, self.pairs, 1, None)
+        self.compute()
         self.sent = to_context(self.sent, 1)
 
     def keep(self):
@@ -854,30 +857,34 @@
     second_mine = [
         lax.dynamic_slice(w_fc2, (i * units, core * half), (units, half)) for i in range(halves)
     ]
+    def spread(pieces):
+        for mask in masks_of(across):
+            pieces = pieces + [to_context(piece, 2 * mask) for piece in pieces]
+        return pieces
+
+    def to_both(pieces):
+        return pieces + [to_context(piece, 1) for piece in pieces]
+
     rest_qkv = [to_fsdp(qkv_at(0))]
     ready = rest_qkv[0]
     rest_out = [to_fsdp(after(out_at(0), ready))]
-    first_near = [to_fsdp(after(first_mine[0], ready))]
+    first_block = lax.dynamic_slice(w_fc1, (place * block, 0), (block, units))
+    second_block = lax.dynamic_slice(w_fc2, (0, place * block), (units, block))
+    first_near = [[to_fsdp(after(first_block, ready))]]
+    second_near = [[to_fsdp(after(second_block, ready))]]
     order.mark(bias_sum)
-    for mask in masks_of(across):
-        rest_qkv = rest_qkv + [to_context(piece, 2 * mask) for piece in rest_qkv]
-    mine = first_mine[1:] + second_mine
+    rest_qkv = spread(rest_qkv)
+    mine = first_mine[1:] + second_mine[1:]
     waited = order.wait(*rest_qkv, *rest_out, *mine)
     rest_qkv, rest_out = list(waited[:across]), list(waited[across : -len(mine)])
-    first_mine[1:], second_mine = waited[-len(mine) : -halves], waited[-halves:]
-    for mask in masks_of(across):
-        rest_out = rest_out + [to_context(piece, 2 * mask) for piece in rest_out]
-    rest_qkv = rest_qkv + [to_context(piece, 1) for piece in rest_qkv]
-    waited = order.wait(first_near[0], *rest_out)
-    first_near[0], rest_out = waited[0], list(waited[1:])
-    rest_out = rest_out + [to_context(piece, 1) for piece in rest_out]
-    second_near = [to_fsdp(after(second_mine[0], first_near[0]))]
-
-    def first_from(i, *done):
-        return to_fsdp(after(first_mine[i], *done))
-
-    def second_from(i, *done):
-        return to_fsdp(after(second_mine[i], *done))
+    first_mine[1:], second_mine[1:] = waited[-len(mine) : 1 - halves], waited[1 - halves :]
+    rest_out = spread(rest_out)
+    rest_qkv = to_both(rest_qkv)
+    waited = order.wait(first_near[0][0], second_near[0][0], *rest_out)
+    rest_out = to_both(list(waited[2:]))
+    first_near[0], second_near[0] = spread([waited[0]]), spread([waited[1]])
+    for i in range(1, halves):
+        first_near.append(to_fsdp(after(first_mine[i], waited[1])))
 
     near = jnp.concatenate([out_at(p) for p in range(across)] + rest_out[:across], 1)
     near = lax.all_gather(near, "tensor", axis=0, tiled=True)
@@ -926,8 +933,7 @@
     fed_parts = []
     back = []
 
-    def feed_part(i, sums):
-        first, second = first_near[i], second_near[i]
+    def feed_part(i, first, second, sums):
         hidden, pre_grad, pre_sum, *sums = feed(
             place_s,
             block,
@@ -935,9 +941,9 @@
             grad,
             fc1_bias,
             w_fc1,
-            [first, to_context(first, 1)],
+            first,
             w_fc2,
-            [second, to_context(second, 1)],
+            second,
             i,
             tuple(sums),
             *((seqs, tensor_size) if i == halves - 1 else (1, 1)),
@@ -945,43 +951,40 @@
         fed_parts.append((hidden, pre_grad, order.mark(pre_sum)))
         return sums
 
-    rows_here = list(here)
-    for i in range(max(halves, len(pieces) if direct else 1)):
-        if i < halves:
-            (second_near[i],) = order.wait(second_near[i])
-            if i + 1 < halves:
-                first_near.append(first_from(i + 1, second_near[i]))
-            sums = feed_part(i, sums)
-            if i + 1 < halves:
-                (first_near[i + 1],) = order.wait(first_near[i + 1])
-                second_near.append(second_from(i + 1, first_near[i + 1]))
-        if i == halves - 1:
-            fed, fed_back = sums
-            fed_share = lax.psum_scatter(fed, "tensor", scatter_dimension=0, tiled=True)
-            fc_sums = [
-                Reduction(order, ((normed, part[1]), (grad, part[0])), block)
-                for part in fed_parts
-            ]
-            if direct and 0 < i < len(rows_here):
-                rows_here[i] = list(order.wait(*rows_here[i]))
-            fc_sums[0].send()
-        if i < len(here):
-            if direct and i == 0:
-                rows_here = [pass_on(*here[0])]
-                for own, beside, across_pair in pieces[1:]:
-                    across_pair = after(order(across_pair), here[-1][2])
-                    here.append(send_across(own, beside, across_pair))
-            row = rows_here[i]
-            result = attend(context_s, [order(row[0])] + row[1:], direct)
-            order.mark(result[0])
-            if direct:
-                back.append(send_across(*result))
-                if i + 1 < len(here):
-                    rows_here.append(pass_on(*here[i + 1]))
-            else:
-                back.append(
-                    [result[0]] + [to_context(result[m], m) for m in range(1, size)]
-                )
+    def group(part):
+        return Reduction(order, ((normed, part[1]), (grad, part[0])), block)
+
+    def attend_next(row):
+        result = attend(context_s, [order(row[0])] + list(row[1:]), direct)
+        order.mark(result[0])
+        if direct:
+            back.append(send_across(*result))
+        else:
+            back.append([result[0]] + [to_context(result[m], m) for m in range(1, size)])
+
+    waited = order.wait(*first_near[0], *second_near[0], *first_near[1:])
+    first, second = list(waited[:across]), list(waited[across : 2 * across])
+    first_near[1:] = waited[2 * across :]
+    for i in range(1, halves):
+        second_near.append(to_fsdp(after(second_mine[i], first_near[i])))
+    sums = feed_part(0, to_both(first), to_both(second), sums)
+    if direct:
+        row = pass_on(*here[0])
+        for own, beside, across_pair in pieces[1:]:
+            here.append(send_across(own, beside, order(across_pair)))
+    else:
+        row = here[0]
+    for i in range(1, halves):
+        first, second = order.wait(first_near[i], second_near[i])
+        sums = feed_part(i, to_both([first]), to_both([second]), sums)
+    first_sum = group(fed_parts[0])
+    second_sum = group(fed_parts[1])
+    fed, fed_back = sums
+    next_rows = [pass_on(*later) for later in here[1:]]
+    fed_share = lax.psum_scatter(order(fed), "tensor", scatter_dimension=0, tiled=True)
+    attend_next(row)
+    for row in next_rows:
+        attend_next(row)
     if not direct:
         stacked = jnp.stack(back[0])
         sources = lax.iota(jnp.int32, size) ^ context
@@ -1026,9 +1029,9 @@
     def arrived(*values):
         return order.wait(*values)
 
-    first_sum, second_sum = fc_sums
     if direct:
         back[0] = pass_on(*back[0])
+    first_sum.send()
     unturned = []
     norm_terms = ()
     heads_from = []
@@ -1038,9 +1041,6 @@
         qkv_bias_sum = qkv_bias_sum + part_sum
         heads_from.append(heads_of(s, unturned[0]))
         norm_terms = [add_heads(s, unturned[1], norm_terms)]
-        if s == 0:
-            first_sum.keep()
-            first_sum.over_fsdp(0)
         if direct and s + 1 < seqs:
             back[s + 1] = pass_on(*back[s + 1])
     merged, raw_grad = unturned
@@ -1048,7 +1048,10 @@
     arrivals = arrived(*[piece for pieces_here in heads_from for piece in pieces_here[1:]])
     norm_share = order(norm_terms[0]).reshape(rows, width)
     norm_share = lax.psum_scatter(norm_share, "tensor", scatter_dimension=0, tiled=True)
+    first_sum.keep()
+    first_sum.over_fsdp(0)
     second_sum.send()
+    last_sum.send()
     (first_sum.far[0],) = arrived(first_sum.far[0])
     first_sum.over_fsdp(1, first_sum.far[0])
     first_sum.over_chips(0)
@@ -1080,11 +1083,11 @@
     order.mark(block_out)
     block_out = from_shares(lax.all_gather(block_out, "tensor", axis=0, tiled=True))
     second_sum.keep()
-    last_sum.send()
     first_sum.far[1], first_sum.far[0] = arrived(first_sum.far[1], first_sum.far[0])
     second_sum.over_fsdp(0, first_sum.far[1])
     first_sum.over_chips(1)
     first_sum.over_cores(0)
+    last_sum.keep()
 
     normed_grad = in_order(order(norm_share))
     centered = inputs - jnp.mean(inputs, -1, keepdims=True)
@@ -1101,25 +1104,21 @@
     small_sums = [norm_sums.reshape(1, -1), bias_sum] + [part[2] for part in fed_parts]
     small_sums = jnp.concatenate(small_sums + [qkv_bias_sum], 1)
     small_other = to_context(small_sums, 1)
-
-    second_sum.far[0], first_sum.far[1], small_other = arrived(
-        second_sum.far[0], first_sum.far[1], small_other
-    )
-    small_sums = small_sums + small_other
-    small_other = to_fsdp(small_sums)
+    second_sum.far[0], first_sum.far[1] = arrived(second_sum.far[0], first_sum.far[1])
     second_sum.over_fsdp(1, second_sum.far[0])
     second_sum.over_chips(0)
     first_sum.over_cores(1)
-    last_sum.keep()
     second_sum.far[1], second_sum.far[0], small_other = arrived(
         second_sum.far[1], second_sum.far[0], small_other
     )
     small_sums = small_sums + small_other
-    for mask in masks_of(across):
-        small_sums = small_sums + to_context(small_sums, 2 * mask)
+    small_other = to_fsdp(small_sums)
     last_sum.over_fsdp(1, second_sum.far[1])
     second_sum.over_chips(1)
     second_sum.over_cores(0)
+    small_sums = small_sums + order.wait(small_other)[0]
+    for mask in masks_of(across):
+        small_sums = small_sums + to_context(small_sums, 2 * mask)
     norm_sums = order.mark(small_sums)[0, : 2 * width].reshape(2, width)
     high = norm_sums.astype(BF16)
     low = (norm_sums - high.astype(F32)).astype(BF16)

time: 553 us -> 541 us (0.978)
  waiting for transfers between devices: 129 us -> 112 us
    ppermute x14, waiting for transfers between devices: 40.1 us -> 25.9 us  [to_fsdp(): return lax.ppermute(value, 'fsdp', [(0, 1), (1, 0)])]
    ppermute x40 -> x44, waiting for transfers between devices: 69.1 us -> 77.7 us  [to_context(): return lax.ppermute(value, 'context', [(i, i ^ mask) for i in range(size)])]
    all_gather x1, waiting for transfers between devices: 14.2 us -> 8.01 us  [per_device(): gathered = lax.all_gather(gathered, 'tensor', axis=0, tiled=False)]
    unnamed x157 -> x167, local copies, waits for them, and re-layouts: 21.8 us -> 24.3 us
    ppermute x40 -> x44, starting transfers between devices: 21.9 us -> 21.4 us  [to_context(): return lax.ppermute(value, 'context', [(i, i ^ mask) for i in range(size)])]
  transfers between devices with their start and end apart: 65 -> 69, of which waited for: 31 -> 27; matrix products, arithmetic and copies ran while one was open for 13% -> 13% of each run, Pallas kernels for 49% -> 50%
where the time goes in v3:
time: 541 us; the launch traced here: 532 us
  Pallas kernels  264 us (49%)
  waiting for transfers between devices  112 us (21%)
  local copies, waits for them, and re-layouts  61 us (11%)
  starting transfers between devices  48.1 us (9%)
  other arithmetic  27.4 us (5%)
  between operations  15.3 us (3%)
    ppermute x44, waiting for transfers between devices, to_context(): return lax.ppermute(value, 'context', [(i, i ^ mask) for i in range(size)])  77.7 us
    pallas_call x6, Pallas kernels, outer(): pl.pallas_call(functools.partial(outer_kernel, steps, int(adds)), out_sha...  66.3 us
    pallas_call x2, Pallas kernels, feed(): pl.pallas_call(functools.partial(feed_kernel, len(first), len(second), le...  61.9 us
    pallas_call x2, Pallas kernels, attend(): pl.pallas_call(functools.partial(attend_kernel, parts, bq, bk), out_shape...  41.7 us
    ppermute x14, waiting for transfers between devices, to_fsdp(): return lax.ppermute(value, 'fsdp', [(0, 1), (1, 0)])  25.9 us
    unnamed x167, local copies, waits for them, and re-layouts  24.3 us
    pallas_call x4, Pallas kernels, finish(): pl.pallas_call(functools.partial(finish_kernel, half, turned, groups), ou...  21.9 us
    ppermute x44, starting transfers between devices, to_context(): return lax.ppermute(value, 'context', [(i, i ^ mask) for i in range(size)])  21.4 us
  transfers between devices with their start and end apart: 69, of which 27 were waited for; matrix products, arithmetic and copies ran while one was open for 13% of the time, Pallas kernels for 50%

profile of v3, /device:TPU:0, one launch (start us, length us, event | category | flops | bytes accessed | tf_op | source)
XLA Modules:
  0.0 532.2 jit_solution(3982646750040677528)
XLA Ops:
  8.4 3.0 collective-permute-start.1
  15.6 1.9 constant_dynamic-slice_fusion.26
  17.5 1.9 constant_dynamic-slice_fusion.24
  19.4 2.4 constant_dynamic-slice_fusion.27
  21.7 2.3 constant_dynamic-slice_fusion.28
  29.3 1.8 collective-permute-start.5
  36.6 10.5 %prepare.1 = (bf16[1024,2048]{1,0:T(8,128)(2,1)}, bf16[1024,2048]{1,0:T(8,128)(2,1)}, f32[1,2048]{1,0:T(1,128)}) custom-call(s32[1]{0:T(128)} %bitcast.3.me_ref, bf16[1024,2048]{1,0:T(8,128)(2,1)} %bitcast.88, bf16[1024,2048]{1,0:T(8,128)(2,1)} %bitcast.90, f32[1,2048]{1,0:T(1,128)} %bitcast.113, f32[1,2048]{1,0:T(1,128)} %bitcast.114), custom_call_target="tpu_custom_call" | custom-call | bytes 34000000 | tf_op jit(solution)/shard_map/prepare/pallas_call | solution.py:159
  47.0 3.7 collective-permute-done.4.refs_11_.refs_5_
  52.2 7.1 %collective-permute-done.3.refs_15_ = bf16[1024,256]{1,0:T(8,128)(2,1)S(1)} collective-permute-done((bf16[1024,256]{1,0:T(8,128)(2,1)}, bf16[1024,256]{1,0:T(8,128)(2,1)S(1)}, u32[]{:S(2)}, u32[]{:S(2)}) %collective-permute-start.3) | collective-permute-done | bytes 524320 | tf_op jit(solution)/shard_map/ppermute | solution.py:45
  63.2 2.2 collective-permute-done.10.refs_21_
  70.4 19.5 %project.1 = (bf16[1,4,512,128]{3,2,1,0:T(8,128)(2,1)}, bf16[1,4,512,128]{3,2,1,0:T(8,128)(2,1)}, bf16[2,4,512,128]{3,2,1,0:T(8,128)(2,1)}, bf16[1,4,512,128]{3,...) custom-call(s32[1]{0:T(128)} %bitcast.2.k_ref, s32[1]{0:T(128)} %bitcast.1.c_ref.me_ref, ...), custom_call_target="tpu_custom_call" | custom-call | bytes 64600000 | tf_op jit(solution)/shard_map/project/pallas_call | solution.py:252
  97.4 29.6 %feed.2 = (bf16[1024,1024]{1,0:T(8,128)(2,1)}, bf16[1024,1024]{1,0:T(8,128)(2,1)}, f32[1,1024]{1,0:T(1,128)}, bf16[1024,2048]{1,0:T(8,128)(2,1)}, bf16[1024,2048]{1,0:T(8,128)(2,1)}) custom-call(s32[1]{0:T(128)} %bitcast.2.k_ref, bf16[1024,2048]{1,0:T(8,128)(2,1)} %get-tuple-element.186.refs_0_.refs_1_.refs_2_.refs_3_, ...), custom_call_target="tpu_custom_call" | custom-call | bytes 105400000 | tf_op jit(solution)/shard_map/feed/pallas_call | solution.py:594
  128.5 2.7 collective-permute-done.21.refs_9_.refs_10_
  133.1 32.4 %feed.3 = (bf16[1024,1024]{1,0:T(8,128)(2,1)}, bf16[1024,1024]{1,0:T(8,128)(2,1)}, f32[1,1024]{1,0:T(1,128)}, bf16[1024,2048]{1,0:T(8,128)(2,1)}, bf16[1024,2048]{1,0:T(8,128)(2,1)}) custom-call(s32[1]{0:T(128)} %bitcast.2.k_ref, bf16[1024,2048]{1,0:T(8,128)(2,1)} %get-tuple-element.186.refs_0_.refs_1_.refs_2_.refs_3_, ...), custom_call_target="tpu_custom_call" | custom-call | bytes 105400000 | tf_op jit(solution)/shard_map/feed/pallas_call | solution.py:594
  170.5 20.8 %attend.2 = (bf16[1,4,512,128]{3,2,1,0:T(8,128)(2,1)}, bf16[1,4,512,128]{3,2,1,0:T(8,128)(2,1)}, bf16[2,4,512,128]{3,2,1,0:T(8,128)(2,1)}) custom-call(s32[1]{0:T(128)} %bitcast.1.c_ref.me_ref, bf16[1,4,512,128]{3,2,1,0:T(8,128)(2,1)} %get-tuple-element.192.refs_0_, bf16[1,4,512,128]{3,2,1,0:T(8,128)(2,1)} %copy-done.39, ...), custom_call_target="tpu_custom_call" | custom-call | bytes 95200000 | tf_op jit(solution)/shard_map/attend/pallas_call | solution.py:380
  191.4 2.1 fusion.25
  196.3 20.9 %attend.3 = (bf16[1,4,512,128]{3,2,1,0:T(8,128)(2,1)}, bf16[1,4,512,128]{3,2,1,0:T(8,128)(2,1)}, bf16[2,4,512,128]{3,2,1,0:T(8,128)(2,1)}) custom-call(s32[1]{0:T(128)} %bitcast.1.c_ref.me_ref, bf16[1,4,512,128]{3,2,1,0:T(8,128)(2,1)} %get-tuple-element.199.refs_0_, bf16[1,4,512,128]{3,2,1,0:T(8,128)(2,1)} %copy-done.38, ...), custom_call_target="tpu_custom_call" | custom-call | bytes 95200000 | tf_op jit(solution)/shard_map/attend/pallas_call | solution.py:380
  217.2 1.9 collective-permute-start.33
  220.5 10.4 %outer.6 = bf16[2,512,2048]{2,1,0:T(8,128)(2,1)} custom-call(bf16[1024,2048]{1,0:T(8,128)(2,1)} %get-tuple-element.186.refs_0_.refs_1_.refs_2_.refs_3_, bf16[1024,2048]{1,0:T(8,128)(2,1)} %get-tuple-element.186.refs_0_.refs_1_.refs_2_.refs_3_, bf16[1024,2048]{1,0:T(8,128)(2,1)} %get-tuple-element.161.refs_1_.refs_2_.refs_3_.refs_0_, ...), custom_call_target="tpu_custom_call" | custom-call | bytes 37400000 | tf_op jit(solution)/shard_map/outer/pallas_call | solution.py:688
  232.0 4.2 unturn.2
  236.1 9.5 %norm_back.2.refs_8_ = bf16[4,2,128,2048]{3,2,1,0:T(8,128)(2,1)} custom-call(s32[1]{0:T(128)} %bitcast.2.k_ref, bf16[1024,1536]{1,0:T(8,128)(2,1)} %get-tuple-element.212.raw.refs_8_, bf16[1024,2048]{1,0:T(8,128)(2,1)} %get-tuple-element.213.back, bf16[3,1024,512]{2,1,0:T(8,128)(2,1)} %refs_3_.7, bf16[3,1024,512]{2,1,0:T(8,128)(2,1)} %refs_3_.7, ...), custom_call_target="tpu_custom_call" | custom-call | bytes 27200000 | tf_op jit(solution)/shard_map/norm_back/pallas_call | solution.py:485
  248.6 2.5 collective-permute-start.31
  252.7 4.2 unturn.3
  258.3 3.4 collective-permute-start.37
  261.7 2.2 collective-permute-start.38
  263.9 9.2 %norm_back.3 = bf16[4,2,128,2048]{3,2,1,0:T(8,128)(2,1)} custom-call(s32[1]{0:T(128)} %bitcast.2.k_ref, bf16[1024,1536]{1,0:T(8,128)(2,1)} %get-tuple-element.220.raw.refs_5_, bf16[1024,2048]{1,0:T(8,128)(2,1)} %get-tuple-element.213.back, bf16[3,1024,512]{2,1,0:T(8,128)(2,1)} %refs_3_.7, ...), custom_call_target="tpu_custom_call", output_to_operand_aliasing={{}: (11, {})} | custom-call | bytes 27200000 | tf_op jit(solution)/shard_map/norm_back/pallas_call | solution.py:485
  274.9 11.6 %outer.7 = (bf16[512,1024]{1,0:T(8,128)(2,1)}, bf16[512,1024]{1,0:T(8,128)(2,1)}, bf16[512,1024]{1,0:T(8,128)(2,1)}, bf16[512,1024]{1,0:T(8,128)(2,1)}) custom-call(bf16[1024,2048]{1,0:T(8,128)(2,1)} %get-tuple-element.186.refs_0_.refs_1_.refs_2_.refs_3_, bf16[1024,2048]{1,0:T(8,128)(2,1)} %get-tuple-element.186.refs_0_.refs_1_.refs_2_.refs_3_, ...), custom_call_target="tpu_custom_call" | custom-call | bytes 37400000 | tf_op jit(solution)/shard_map/outer/pallas_call | solution.py:688
  292.9 10.4 %outer.8 = bf16[2,512,2048]{2,1,0:T(8,128)(2,1)} custom-call(bf16[1024,2048]{1,0:T(8,128)(2,1)} %get-tuple-element.186.refs_0_.refs_1_.refs_2_.refs_3_, bf16[1024,2048]{1,0:T(8,128)(2,1)} %get-tuple-element.186.refs_0_.refs_1_.refs_2_.refs_3_, bf16[1024,2048]{1,0:T(8,128)(2,1)} %get-tuple-element.161.refs_1_.refs_2_.refs_3_.refs_0_, ...), custom_call_target="tpu_custom_call" | custom-call | bytes 37400000 | tf_op jit(solution)/shard_map/outer/pallas_call | solution.py:688
  303.4 10.6 %outer.9 = bf16[2,512,2048]{2,1,0:T(8,128)(2,1)} custom-call(bf16[1024,2048]{1,0:T(8,128)(2,1)} %get-tuple-element.161.refs_1_.refs_2_.refs_3_.refs_0_, bf16[1024,2048]{1,0:T(8,128)(2,1)} %get-tuple-element.161.refs_1_.refs_2_.refs_3_.refs_0_, bf16[1024,2048]{1,0:T(8,128)(2,1)} %get-tuple-element.186.refs_0_.refs_1_.refs_2_.refs_3_, ...), custom_call_target="tpu_custom_call" | custom-call | bytes 37400000 | tf_op jit(solution)/shard_map/outer/pallas_call | solution.py:688
  314.3 1.8 add_convert_fusion.4.left
  319.7 3.5 fusion.30
  324.3 1.9 maximum_add_fusion
  326.8 2.6 fusion.14
  329.5 11.7 %outer.10 = (bf16[512,1024]{1,0:T(8,128)(2,1)}, bf16[512,1024]{1,0:T(8,128)(2,1)}, bf16[512,1024]{1,0:T(8,128)(2,1)}, bf16[512,1024]{1,0:T(8,128)(2,1)}) custom-call(bf16[1024,2048]{1,0:T(8,128)(2,1)} %get-tuple-element.186.refs_0_.refs_1_.refs_2_.refs_3_, bf16[1024,2048]{1,0:T(8,128)(2,1)} %get-tuple-element.186.refs_0_.refs_1_.refs_2_.refs_3_, ...), custom_call_target="tpu_custom_call" | custom-call | bytes 37400000 | tf_op jit(solution)/shard_map/outer/pallas_call | solution.py:688
  342.2 1.9 add_convert_fusion.3.left
  345.5 2.5 add_turned.6.refs_0_
  348.8 11.6 %outer.11 = (bf16[512,512]{1,0:T(8,128)(2,1)}, bf16[512,1536]{1,0:T(8,128)(2,1)}, bf16[512,512]{1,0:T(8,128)(2,1)}, bf16[512,1536]{1,0:T(8,128)(2,1)}) custom-call(bf16[1024,2048]{1,0:T(8,128)(2,1)} %get-tuple-element.161.refs_1_.refs_2_.refs_3_.refs_0_, bf16[1024,2048]{1,0:T(8,128)(2,1)} %get-tuple-element.161.refs_1_.refs_2_.refs_3_.refs_0_, ...), custom_call_target="tpu_custom_call" | custom-call | bytes 37400000 | tf_op jit(solution)/shard_map/outer/pallas_call | solution.py:688
  366.4 1.9 fusion.5
  368.4 3.8 collective-permute-done.46
  376.3 2.4 add_turned.7.refs_0_
  378.7 18.1 %collective-permute-done.49.right = bf16[512,1024]{1,0:T(8,128)(2,1)S(1)} collective-permute-done((bf16[512,1024]{1,0:T(8,128)(2,1)S(1)}, bf16[512,1024]{1,0:T(8,128)(2,1)S(1)}, u32[]{:S(2)}, u32[]{:S(2)}) %collective-permute-start.49) | collective-permute-done | bytes 1048608 | tf_op jit(solution)/shard_map/ppermute | solution.py:50
  397.8 1.9 collective-permute-start.51
  401.4 2.8 add_turned.8.refs_2_
  405.6 2.7 collective-permute-done.52
  408.4 2.6 maximum_maximum_fusion
  415.7 6.3 %finish.4 = f32[1024,2048]{1,0:T(8,128)} custom-call(s32[1]{0:T(128)} %bitcast.2.k_ref, bf16[512,1024]{1,0:T(8,128)(2,1)} %add_turned.6.refs_0_, bf16[512,1024]{1,0:T(8,128)(2,1)} %copy-done.26, bf16[512,1024]{1,0:T(8,128)(2,1)} %add_turned.8.refs_2_, bf16[512,1024]{1,0:T(8,128)(2,1)} %collective-permute-done.56.refs_3_), custom_call_target="tpu_custom_call" | custom-call | bytes 20400000 | tf_op jit(solution)/shard_map/finish/pallas_call | solution.py:764
  422.0 15.0 %collective-permute-done.54.right = bf16[512,1024]{1,0:T(8,128)(2,1)} collective-permute-done((bf16[512,1024]{1,0:T(8,128)(2,1)S(1)}, bf16[512,1024]{1,0:T(8,128)(2,1)}, u32[]{:S(2)}, u32[]{:S(2)}) %collective-permute-start.54) | collective-permute-done | bytes 1048608 | tf_op jit(solution)/shard_map/ppermute | solution.py:50
  437.1 7.2 %collective-permute-done.53 = bf16[512,1536]{1,0:T(8,128)(2,1)} collective-permute-done((bf16[512,1536]{1,0:T(8,128)(2,1)}, bf16[512,1536]{1,0:T(8,128)(2,1)}, u32[]{:S(2)}, u32[]{:S(2)}) %collective-permute-start.53) | collective-permute-done | bytes 1572896 | tf_op jit(solution)/shard_map/ppermute | solution.py:45
  444.3 2.4 add_convert_fusion.left
  447.6 2.5 add_turned.9.refs_2_
  451.0 2.1 collective-permute-done.59.refs_3_
  453.2 6.5 %finish.5 = f32[2048,1024]{1,0:T(8,128)} custom-call(s32[1]{0:T(128)} %bitcast.2.k_ref, bf16[512,1024]{1,0:T(8,128)(2,1)} %add_turned.7.refs_0_, bf16[512,1024]{1,0:T(8,128)(2,1)} %collective-permute-done.58.refs_1_, bf16[512,1024]{1,0:T(8,128)(2,1)} %add_turned.9.refs_2_, bf16[512,1024]{1,0:T(8,128)(2,1)} %collective-permute-done.59.refs_3_), custom_call_target="tpu_custom_call" | custom-call | bytes 20400000 | tf_op jit(solution)/shard_map/finish/pallas_call | solution.py:764
  459.6 5.0 collective-permute-done.57
  464.8 14.4 %collective-permute-done.60.right = bf16[512,1536]{1,0:T(8,128)(2,1)} collective-permute-done((bf16[512,1536]{1,0:T(8,128)(2,1)S(1)}, bf16[512,1536]{1,0:T(8,128)(2,1)}, u32[]{:S(2)}, u32[]{:S(2)}) %collective-permute-start.60) | collective-permute-done | bytes 1572896 | tf_op jit(solution)/shard_map/ppermute | solution.py:50
  479.2 2.9 add_turned.10.refs_0_
  482.6 3.1 collective-permute-done.61.refs_1_
  486.8 5.3 finish.6
  492.2 4.3 collective-permute-done.62.right
  497.2 2.0 add_turned.11.refs_0_
  500.4 4.8 copy.35
  506.0 3.8 finish.7
  509.9 8.0 %all-gather.9.cloned.1.call-done = bf16[1088,2048]{1,0:T(8,128)(2,1)} async-done(((bf16[272,2048]{1,0:T(8,128)(2,1)}), bf16[1088,2048]{1,0:T(8,128)(2,1)}) %all-gather.9.cloned.1.call-update) | async-done | bytes 4456464 | tf_op jit(solution)/shard_map/all_gather | solution.py:1127
  517.9 2.5 slice.131
  521.3 2.3 copy.36
  (363 shorter events, 98.1 us)
Async XLA Ops:
  7.2 266.1 %all-gather.5.cloned.1.call-start = ((), (), s32[]{:S(2)}) async-start(), calls=%async_computation.2 | async-start | bytes 5242880 | tf_op jit(solution)/shard_map/all_gather | solution.py:890
  8.4 20.9 %collective-permute-start.1 = (bf16[3,256,512]{2,1,0:T(8,128)(2,1)S(1)}, bf16[3,256,512]{2,1,0:T(8,128)(2,1)S(1)}, u32[]{:S(2)}, u32[]{:S(2)}) collective-permute-start(bf16[3,256,512]{2,1,0:T(8,128)(2,1)S(1)} %constant_dynamic-slice_fusion.25), channel_id=1, source_target_pairs={{0,16},{16,0},{1,17},{17,1},{2,18},{18,2},{3,19},{19,3},{4,20},{20... | collective-permute-start | bytes 2359304 | tf_op jit(solution)/shard_map/ppermute | solution.py:45
  15.6 13.7 %collective-permute-start = (bf16[5888]{0:T(1024)(128)(2,1)S(1)}, bf16[5888]{0:T(1024)(128)(2,1)S(1)}, u32[]{:S(2)}, u32[]{:S(2)}) collective-permute-start(bf16[5888]{0:T(1024)(128)(2,1)S(1)} %constant_dynamic-update-slice_fusion.28), channel_id=1, source_target_pairs={{0,16},{16,0},{1,17},{17,1},{2,18},{18,2},{3,19},{19,3},{4,20},{20... | collective-permute-start | bytes 35336 | tf_op jit(solution)/shard_map/ppermute | solution.py:45
  29.3 17.7 %collective-permute-start.5 = (bf16[512,256]{1,0:T(8,128)(2,1)S(1)}, bf16[512,256]{1,0:T(8,128)(2,1)S(1)}, u32[]{:S(2)}, u32[]{:S(2)}) collective-permute-start(bf16[512,256]{1,0:T(8,128)(2,1)S(1)} %get-tuple-element.154), channel_id=1, source_target_pairs={{0,16},{16,0},{1,17},{17,1},{2,18},{18,2},{3,19},{19,3},{4,20},{20... | collective-permute-start | bytes 786440 | tf_op jit(solution)/shard_map/ppermute | solution.py:45
  31.1 21.1 %collective-permute-start.2 = (bf16[256,1024]{1,0:T(8,128)(2,1)}, bf16[256,1024]{1,0:T(8,128)(2,1)}, u32[]{:S(2)}, u32[]{:S(2)}) collective-permute-start(bf16[256,1024]{1,0:T(8,128)(2,1)} %constant_dynamic-slice_fusion.26), channel_id=1, source_target_pairs={{0,16},{16,0},{1,17},{17,1},{2,18},{18,2},{3,19},{19,3},{4,20},{20... | collective-permute-start | bytes 1572872 | tf_op jit(solution)/shard_map/ppermute | solution.py:45
  31.4 27.9 %collective-permute-start.3 = (bf16[1024,256]{1,0:T(8,128)(2,1)}, bf16[1024,256]{1,0:T(8,128)(2,1)S(1)}, u32[]{:S(2)}, u32[]{:S(2)}) collective-permute-start(bf16[1024,256]{1,0:T(8,128)(2,1)} %constant_dynamic-slice_fusion.24), channel_id=1, source_target_pairs={{0,16},{16,0},{1,17},{17,1},{2,18},{18,2},{3,19},{19,3},{4,20},{20... | collective-permute-start | bytes 1572872 | tf_op jit(solution)/shard_map/ppermute | solution.py:45
  33.2 17.6 %collective-permute-start.4 = (bf16[3,256,512]{2,1,0:T(8,128)(2,1)S(1)}, bf16[3,256,512]{2,1,0:T(8,128)(2,1)S(1)}, u32[]{:S(2)}, u32[]{:S(2)}) collective-permute-start(bf16[3,256,512]{2,1,0:T(8,128)(2,1)S(1)} %collective-permute-done.1.refs_10_.refs_4_), channel_id=1, source_target_pairs={{0,8},{4,12},{8,0},{12,4},{1,9},{5,13},{9,1},{13,5},{2,10},{6,14},... | collective-permute-start | bytes 2359304 | tf_op jit(solution)/shard_map/ppermute | solution.py:50
  50.8 8.6 %collective-permute-start.6 = (bf16[512,256]{1,0:T(8,128)(2,1)S(1)}, bf16[512,256]{1,0:T(8,128)(2,1)S(1)}, u32[]{:S(2)}, u32[]{:S(2)}) collective-permute-start(bf16[512,256]{1,0:T(8,128)(2,1)S(1)} %collective-permute-done.5.refs_18_), channel_id=1, source_target_pairs={{0,8},{4,12},{8,0},{12,4},{1,9},{5,13},{9,1},{13,5},{2,10},{6,14},... | collective-permute-start | bytes 786440 | tf_op jit(solution)/shard_map/ppermute | solution.py:50
  60.6 263.7 %reduce-scatter.3.cloned.1.call-start = ((), (), s32[]{:S(2)}) async-start(), calls=%async_computation.3 | async-start | bytes 5242880 | tf_op jit(solution)/shard_map/reduce_scatter | solution.py:984
  60.7 30.3 %collective-permute-start.14 = (bf16[512,1024]{1,0:T(8,128)(2,1)}, bf16[512,1024]{1,0:T(8,128)(2,1)}, u32[]{:S(2)}, u32[]{:S(2)}) collective-permute-start(bf16[512,1024]{1,0:T(8,128)(2,1)} %constant_dynamic-slice_fusion.28), channel_id=1, source_target_pairs={{0,16},{16,0},{1,17},{17,1},{2,18},{18,2},{3,19},{19,3},{4,20},{20... | collective-permute-start | bytes 3145736 | tf_op jit(solution)/shard_map/ppermute | solution.py:45
  62.2 7.0 %collective-permute-start.7 = (bf16[3,256,512]{2,1,0:T(8,128)(2,1)S(1)}, bf16[3,256,512]{2,1,0:T(8,128)(2,1)S(1)}, u32[]{:S(2)}, u32[]{:S(2)}) collective-permute-start(bf16[3,256,512]{2,1,0:T(8,128)(2,1)S(1)} %collective-permute-done.1.refs_10_.refs_4_), channel_id=1, source_target_pairs={{0,4},{4,0},{8,12},{12,8},{1,5},{5,1},{9,13},{13,9},{2,6},{6,2},{1... | collective-permute-start | bytes 2359304 | tf_op jit(solution)/shard_map/ppermute | solution.py:50
  62.2 7.0 %collective-permute-start.8 = (bf16[3,256,512]{2,1,0:T(8,128)(2,1)S(1)}, bf16[3,256,512]{2,1,0:T(8,128)(2,1)S(1)}, u32[]{:S(2)}, u32[]{:S(2)}) collective-permute-start(bf16[3,256,512]{2,1,0:T(8,128)(2,1)S(1)} %collective-permute-done.4.refs_11_.refs_5_), channel_id=1, source_target_pairs={{0,4},{4,0},{8,12},{12,8},{1,5},{5,1},{9,13},{13,9},{2,6},{6,2},{1... | collective-permute-start | bytes 2359304 | tf_op jit(solution)/shard_map/ppermute | solution.py:50
  62.7 2.7 collective-permute-start.10
  62.8 4.2 collective-permute-start.9
  65.4 24.4 %collective-permute-start.12 = (bf16[256,1024]{1,0:T(8,128)(2,1)}, bf16[256,1024]{1,0:T(8,128)(2,1)}, u32[]{:S(2)}, u32[]{:S(2)}) collective-permute-start(bf16[256,1024]{1,0:T(8,128)(2,1)} %collective-permute-done.2.refs_7_), channel_id=1, source_target_pairs={{0,8},{4,12},{8,0},{12,4},{1,9},{5,13},{9,1},{13,5},{2,10},{6,14},... | collective-permute-start | bytes 1572872 | tf_op jit(solution)/shard_map/ppermute | solution.py:50
  67.6 23.3 %collective-permute-start.13 = (bf16[1024,256]{1,0:T(8,128)(2,1)}, bf16[1024,256]{1,0:T(8,128)(2,1)}, u32[]{:S(2)}, u32[]{:S(2)}) collective-permute-start(bf16[1024,256]{1,0:T(8,128)(2,1)} %copy-done.30), channel_id=1, source_target_pairs={{0,8},{4,12},{8,0},{12,4},{1,9},{5,13},{9,1},{13,5},{2,10},{6,14},... | collective-permute-start | bytes 1572872 | tf_op jit(solution)/shard_map/ppermute | solution.py:50
  90.9 36.0 %collective-permute-start.11 = (bf16[2,4,512,128]{3,2,1,0:T(8,128)(2,1)}, bf16[2,4,512,128]{3,2,1,0:T(8,128)(2,1)S(1)}, u32[]{:S(2)}, u32[]{:S(2)}) collective-permute-start(bf16[2,4,512,128]{3,2,1,0:T(8,128)(2,1)} %get-tuple-element.170), channel_id=1, source_target_pairs={{0,8},{4,12},{8,0},{12,4},{1,9},{5,13},{9,1},{13,5},{2,10},{6,14},... | collective-permute-start | bytes 3145736 | tf_op jit(solution)/shard_map/ppermute | solution.py:50
  92.4 35.5 %collective-permute-start.20 = (bf16[1024,512]{1,0:T(8,128)(2,1)}, bf16[1024,512]{1,0:T(8,128)(2,1)S(1)}, u32[]{:S(2)}, u32[]{:S(2)}) collective-permute-start(bf16[1024,512]{1,0:T(8,128)(2,1)} %constant_dynamic-slice_fusion.27), channel_id=1, source_target_pairs={{0,16},{16,0},{1,17},{17,1},{2,18},{18,2},{3,19},{19,3},{4,20},{20... | collective-permute-start | bytes 3145736 | tf_op jit(solution)/shard_map/ppermute | solution.py:45
  92.9 3.6 collective-permute-start.17
  93.5 3.2 collective-permute-start.18
  128.0 3.2 collective-permute-start.21
  128.1 4.0 collective-permute-start.22
  128.5 37.0 %collective-permute-start.19 = (bf16[2,4,512,128]{3,2,1,0:T(8,128)(2,1)}, bf16[2,4,512,128]{3,2,1,0:T(8,128)(2,1)}, u32[]{:S(2)}, u32[]{:S(2)}) collective-permute-start(bf16[2,4,512,128]{3,2,1,0:T(8,128)(2,1)} %get-tuple-element.181), channel_id=1, source_target_pairs={{0,8},{4,12},{8,0},{12,4},{1,9},{5,13},{9,1},{13,5},{2,10},{6,14},... | collective-permute-start | bytes 3145736 | tf_op jit(solution)/shard_map/ppermute | solution.py:50
  165.5 194.9 %reduce-scatter.5.cloned.1.call-start = ((), (), s32[]{:S(2)}) async-start(), calls=%async_computation.5 | async-start | bytes 5242880 | tf_op jit(solution)/shard_map/reduce_scatter | solution.py:1050
  191.3 27.8 %collective-permute-start.25 = (bf16[2,4,512,128]{3,2,1,0:T(8,128)(2,1)}, bf16[2,4,512,128]{3,2,1,0:T(8,128)(2,1)S(1)}, u32[]{:S(2)}, u32[]{:S(2)}) collective-permute-start(bf16[2,4,512,128]{3,2,1,0:T(8,128)(2,1)} %get-tuple-element.197), channel_id=1, source_target_pairs={{0,8},{4,12},{8,0},{12,4},{1,9},{5,13},{9,1},{13,5},{2,10},{6,14},... | collective-permute-start | bytes 3145736 | tf_op jit(solution)/shard_map/ppermute | solution.py:50
  191.3 2.7 collective-permute-start.26
  217.2 28.5 %collective-permute-start.33 = (bf16[2,4,512,128]{3,2,1,0:T(8,128)(2,1)}, bf16[2,4,512,128]{3,2,1,0:T(8,128)(2,1)S(1)}, u32[]{:S(2)}, u32[]{:S(2)}) collective-permute-start(bf16[2,4,512,128]{3,2,1,0:T(8,128)(2,1)} %get-tuple-element.210), channel_id=1, source_target_pairs={{0,8},{4,12},{8,0},{12,4},{1,9},{5,13},{9,1},{13,5},{2,10},{6,14},... | collective-permute-start | bytes 3145736 | tf_op jit(solution)/shard_map/ppermute | solution.py:50
  219.1 11.9 %collective-permute-start.28 = (bf16[1,4,512,128]{3,2,1,0:T(8,128)(2,1)S(1)}, bf16[1,4,512,128]{3,2,1,0:T(8,128)(2,1)S(1)}, u32[]{:S(2)}, u32[]{:S(2)}) collective-permute-start(bf16[1,4,512,128]{3,2,1,0:T(8,128)(2,1)S(1)} %copy-done.64), channel_id=1, source_target_pairs={{0,4},{4,0},{8,12},{12,8},{1,5},{5,1},{9,13},{13,9},{2,6},{6,2},{1... | collective-permute-start | bytes 1572872 | tf_op jit(solution)/shard_map/ppermute | solution.py:50
  220.1 10.9 %collective-permute-start.29 = (bf16[1,4,512,128]{3,2,1,0:T(8,128)(2,1)S(1)}, bf16[1,4,512,128]{3,2,1,0:T(8,128)(2,1)S(1)}, u32[]{:S(2)}, u32[]{:S(2)}) collective-permute-start(bf16[1,4,512,128]{3,2,1,0:T(8,128)(2,1)S(1)} %get-tuple-element.328), channel_id=1, source_target_pairs={{0,4},{4,0},{8,12},{12,8},{1,5},{5,1},{9,13},{13,9},{2,6},{6,2},{1... | collective-permute-start | bytes 1572872 | tf_op jit(solution)/shard_map/ppermute | solution.py:50
  230.9 44.0 %collective-permute-start.39 = (bf16[2,512,2048]{2,1,0:T(8,128)(2,1)}, bf16[2,512,2048]{2,1,0:T(8,128)(2,1)}, u32[]{:S(2)}, u32[]{:S(2)}) collective-permute-start(bf16[2,512,2048]{2,1,0:T(8,128)(2,1)} %outer.6), channel_id=1, source_target_pairs={{0,4},{4,0},{8,12},{12,8},{1,5},{5,1},{9,13},{13,9},{2,6},{6,2},{1... | collective-permute-start | bytes 12582920 | tf_op jit(solution)/shard_map/ppermute | solution.py:50
  246.5 4.6 collective-permute-start.35
  246.9 5.0 collective-permute-start.34
  247.1 11.2 %collective-permute-start.30 = (bf16[128,512]{1,0:T(8,128)(2,1)S(1)}, bf16[128,512]{1,0:T(8,128)(2,1)S(1)}, u32[]{:S(2)}, u32[]{:S(2)}) collective-permute-start(bf16[128,512]{1,0:T(8,128)(2,1)S(1)} %get-tuple-element.326), channel_id=1, source_target_pairs={{0,1},{1,0},{2,3},{3,2},{4,5},{5,4},{6,7},{7,6},{8,9},{9,8},{10,11... | collective-permute-start | bytes 393224 | tf_op jit(solution)/shard_map/ppermute | solution.py:55
  248.6 13.2 %collective-permute-start.31 = (bf16[128,512]{1,0:T(8,128)(2,1)S(1)}, bf16[128,512]{1,0:T(8,128)(2,1)S(1)}, u32[]{:S(2)}, u32[]{:S(2)}) collective-permute-start(bf16[128,512]{1,0:T(8,128)(2,1)S(1)} %get-tuple-element.325), channel_id=1, source_target_pairs={{0,2},{1,3},{2,0},{3,1},{4,6},{5,7},{6,4},{7,5},{8,10},{9,11},{10,... | collective-permute-start | bytes 393224 | tf_op jit(solution)/shard_map/ppermute | solution.py:55
  251.1 22.0 %collective-permute-start.32 = (bf16[128,512]{1,0:T(8,128)(2,1)S(1)}, bf16[128,512]{1,0:T(8,128)(2,1)S(1)}, u32[]{:S(2)}, u32[]{:S(2)}) collective-permute-start(bf16[128,512]{1,0:T(8,128)(2,1)S(1)} %get-tuple-element.324), channel_id=1, source_target_pairs={{0,3},{1,2},{2,1},{3,0},{4,7},{5,6},{6,5},{7,4},{8,11},{9,10},{10,... | collective-permute-start | bytes 393224 | tf_op jit(solution)/shard_map/ppermute | solution.py:55
  258.1 15.1 %collective-permute-start.36 = (bf16[128,512]{1,0:T(8,128)(2,1)S(1)}, bf16[128,512]{1,0:T(8,128)(2,1)S(1)}, u32[]{:S(2)}, u32[]{:S(2)}) collective-permute-start(bf16[128,512]{1,0:T(8,128)(2,1)S(1)} %get-tuple-element.321), channel_id=1, source_target_pairs={{0,1},{1,0},{2,3},{3,2},{4,5},{5,4},{6,7},{7,6},{8,9},{9,8},{10,11... | collective-permute-start | bytes 393224 | tf_op jit(solution)/shard_map/ppermute | solution.py:55
  258.3 14.9 %collective-permute-start.37 = (bf16[128,512]{1,0:T(8,128)(2,1)S(1)}, bf16[128,512]{1,0:T(8,128)(2,1)S(1)}, u32[]{:S(2)}, u32[]{:S(2)}) collective-permute-start(bf16[128,512]{1,0:T(8,128)(2,1)S(1)} %get-tuple-element.320), channel_id=1, source_target_pairs={{0,2},{1,3},{2,0},{3,1},{4,6},{5,7},{6,4},{7,5},{8,10},{9,11},{10,... | collective-permute-start | bytes 393224 | tf_op jit(solution)/shard_map/ppermute | solution.py:55
  261.7 11.4 %collective-permute-start.38 = (bf16[128,512]{1,0:T(8,128)(2,1)S(1)}, bf16[128,512]{1,0:T(8,128)(2,1)}, u32[]{:S(2)}, u32[]{:S(2)}) collective-permute-start(bf16[128,512]{1,0:T(8,128)(2,1)S(1)} %get-tuple-element.319), channel_id=1, source_target_pairs={{0,3},{1,2},{2,1},{3,0},{4,7},{5,6},{6,5},{7,4},{8,11},{9,10},{10,... | collective-permute-start | bytes 393224 | tf_op jit(solution)/shard_map/ppermute | solution.py:55
  273.2 227.2 %all-gather.7.cloned.1.call-start = ((), (), s32[]{:S(2)}) async-start(), calls=%async_computation.4 | async-start | bytes 5242880 | tf_op jit(solution)/shard_map/all_gather | solution.py:1084
  273.3 46.4 %collective-permute-start.41 = (bf16[2048,1024]{1,0:T(8,128)(2,1)}, bf16[2048,1024]{1,0:T(8,128)(2,1)}, u32[]{:S(2)}, u32[]{:S(2)}) collective-permute-start(bf16[2048,1024]{1,0:T(8,128)(2,1)} %all-gather.5.cloned.1.call-done), channel_id=1, source_target_pairs={{0,4},{4,0},{8,12},{12,8},{1,5},{5,1},{9,13},{13,9},{2,6},{6,2},{1... | collective-permute-start | bytes 12582920 | tf_op jit(solution)/shard_map/ppermute | solution.py:50
  286.5 27.8 %collective-permute-start.40 = (bf16[512,1024]{1,0:T(8,128)(2,1)}, bf16[512,1024]{1,0:T(8,128)(2,1)}, u32[]{:S(2)}, u32[]{:S(2)}) collective-permute-start(bf16[512,1024]{1,0:T(8,128)(2,1)} %get-tuple-element.224), channel_id=1, source_target_pairs={{0,16},{16,0},{1,17},{17,1},{2,18},{18,2},{3,19},{19,3},{4,20},{20... | collective-permute-start | bytes 3145736 | tf_op jit(solution)/shard_map/ppermute | solution.py:45
  303.3 26.2 %collective-permute-start.44 = (bf16[2,512,2048]{2,1,0:T(8,128)(2,1)}, bf16[2,512,2048]{2,1,0:T(8,128)(2,1)}, u32[]{:S(2)}, u32[]{:S(2)}) collective-permute-start(bf16[2,512,2048]{2,1,0:T(8,128)(2,1)} %outer.8), channel_id=1, source_target_pairs={{0,4},{4,0},{8,12},{12,8},{1,5},{5,1},{9,13},{13,9},{2,6},{6,2},{1... | collective-permute-start | bytes 12582920 | tf_op jit(solution)/shard_map/ppermute | solution.py:50
  314.0 34.8 %collective-permute-start.45 = (bf16[2,512,2048]{2,1,0:T(8,128)(2,1)}, bf16[2,512,2048]{2,1,0:T(8,128)(2,1)}, u32[]{:S(2)}, u32[]{:S(2)}) collective-permute-start(bf16[2,512,2048]{2,1,0:T(8,128)(2,1)} %outer.9), channel_id=1, source_target_pairs={{0,4},{4,0},{8,12},{12,8},{1,5},{5,1},{9,13},{13,9},{2,6},{6,2},{1... | collective-permute-start | bytes 12582920 | tf_op jit(solution)/shard_map/ppermute | solution.py:50
  316.1 26.1 %collective-permute-start.43 = (bf16[512,1024]{1,0:T(8,128)(2,1)S(1)}, bf16[512,1024]{1,0:T(8,128)(2,1)}, u32[]{:S(2)}, u32[]{:S(2)}) collective-permute-start(bf16[512,1024]{1,0:T(8,128)(2,1)S(1)} %add_convert_fusion.4.left), channel_id=1, source_target_pairs={{0,8},{4,12},{8,0},{12,4},{1,9},{5,13},{9,1},{13,5},{2,10},{6,14},... | collective-permute-start | bytes 3145736 | tf_op jit(solution)/shard_map/ppermute | solution.py:50
  316.9 25.2 %collective-permute-start.42 = (bf16[512,1024]{1,0:T(8,128)(2,1)}, bf16[512,1024]{1,0:T(8,128)(2,1)}, u32[]{:S(2)}, u32[]{:S(2)}) collective-permute-start(bf16[512,1024]{1,0:T(8,128)(2,1)} %get-tuple-element.249), channel_id=1, source_target_pairs={{0,16},{16,0},{1,17},{17,1},{2,18},{18,2},{3,19},{19,3},{4,20},{20... | collective-permute-start | bytes 3145736 | tf_op jit(solution)/shard_map/ppermute | solution.py:45
  329.5 188.4 %all-gather.9.cloned.1.call-start = ((), (), s32[]{:S(2)}) async-start(), calls=%async_computation.6 | async-start | bytes 5570560 | tf_op jit(solution)/shard_map/all_gather | solution.py:1127
  344.1 28.0 %collective-permute-start.47 = (bf16[512,1024]{1,0:T(8,128)(2,1)S(1)}, bf16[512,1024]{1,0:T(8,128)(2,1)}, u32[]{:S(2)}, u32[]{:S(2)}) collective-permute-start(bf16[512,1024]{1,0:T(8,128)(2,1)S(1)} %add_convert_fusion.3.left), channel_id=1, source_target_pairs={{0,8},{4,12},{8,0},{12,4},{1,9},{5,13},{9,1},{13,5},{2,10},{6,14},... | collective-permute-start | bytes 3145736 | tf_op jit(solution)/shard_map/ppermute | solution.py:50
  348.0 24.2 %collective-permute-start.46 = (bf16[512,1024]{1,0:T(8,128)(2,1)}, bf16[512,1024]{1,0:T(8,128)(2,1)}, u32[]{:S(2)}, u32[]{:S(2)}) collective-permute-start(bf16[512,1024]{1,0:T(8,128)(2,1)} %get-tuple-element.263), channel_id=1, source_target_pairs={{0,16},{16,0},{1,17},{17,1},{2,18},{18,2},{3,19},{19,3},{4,20},{20... | collective-permute-start | bytes 3145736 | tf_op jit(solution)/shard_map/ppermute | solution.py:45
  373.8 23.0 %collective-permute-start.49 = (bf16[512,1024]{1,0:T(8,128)(2,1)S(1)}, bf16[512,1024]{1,0:T(8,128)(2,1)S(1)}, u32[]{:S(2)}, u32[]{:S(2)}) collective-permute-start(bf16[512,1024]{1,0:T(8,128)(2,1)S(1)} %add_convert_fusion.2.left), channel_id=1, source_target_pairs={{0,8},{4,12},{8,0},{12,4},{1,9},{5,13},{9,1},{13,5},{2,10},{6,14},... | collective-permute-start | bytes 3145736 | tf_op jit(solution)/shard_map/ppermute | solution.py:50
  374.6 23.2 %collective-permute-start.48 = (bf16[512,1024]{1,0:T(8,128)(2,1)}, bf16[512,1024]{1,0:T(8,128)(2,1)}, u32[]{:S(2)}, u32[]{:S(2)}) collective-permute-start(bf16[512,1024]{1,0:T(8,128)(2,1)} %get-tuple-element.265), channel_id=1, source_target_pairs={{0,16},{16,0},{1,17},{17,1},{2,18},{18,2},{3,19},{19,3},{4,20},{20... | collective-permute-start | bytes 3145736 | tf_op jit(solution)/shard_map/ppermute | solution.py:45
  376.2 2.5 collective-permute-start.50
  397.8 6.4 %collective-permute-start.51 = (f32[1,9728]{1,0:T(1,128)S(1)}, f32[1,9728]{1,0:T(1,128)S(1)}, u32[]{:S(2)}, u32[]{:S(2)}) collective-permute-start(f32[1,9728]{1,0:T(1,128)S(1)} %add.259), channel_id=1, source_target_pairs={{0,16},{16,0},{1,17},{17,1},{2,18},{18,2},{3,19},{19,3},{4,20},{20... | collective-permute-start | bytes 116744 | tf_op jit(solution)/shard_map/ppermute | solution.py:45
  404.3 4.0 collective-permute-start.52
  411.0 33.3 %collective-permute-start.53 = (bf16[512,1536]{1,0:T(8,128)(2,1)}, bf16[512,1536]{1,0:T(8,128)(2,1)}, u32[]{:S(2)}, u32[]{:S(2)}) collective-permute-start(bf16[512,1536]{1,0:T(8,128)(2,1)} %get-tuple-element.279), channel_id=1, source_target_pairs={{0,16},{16,0},{1,17},{17,1},{2,18},{18,2},{3,19},{19,3},{4,20},{20... | collective-permute-start | bytes 4718600 | tf_op jit(solution)/shard_map/ppermute | solution.py:45
  411.3 3.4 collective-permute-start.55
  411.3 4.4 collective-permute-start.56
  411.8 25.2 %collective-permute-start.54 = (bf16[512,1024]{1,0:T(8,128)(2,1)S(1)}, bf16[512,1024]{1,0:T(8,128)(2,1)}, u32[]{:S(2)}, u32[]{:S(2)}) collective-permute-start(bf16[512,1024]{1,0:T(8,128)(2,1)S(1)} %add_convert_fusion.1.left), channel_id=1, source_target_pairs={{0,8},{4,12},{8,0},{12,4},{1,9},{5,13},{9,1},{13,5},{2,10},{6,14},... | collective-permute-start | bytes 3145736 | tf_op jit(solution)/shard_map/ppermute | solution.py:50
  446.7 32.5 %collective-permute-start.60 = (bf16[512,1536]{1,0:T(8,128)(2,1)S(1)}, bf16[512,1536]{1,0:T(8,128)(2,1)}, u32[]{:S(2)}, u32[]{:S(2)}) collective-permute-start(bf16[512,1536]{1,0:T(8,128)(2,1)S(1)} %add_convert_fusion.left), channel_id=1, source_target_pairs={{0,8},{4,12},{8,0},{12,4},{1,9},{5,13},{9,1},{13,5},{2,10},{6,14},... | collective-permute-start | bytes 4718600 | tf_op jit(solution)/shard_map/ppermute | solution.py:50
  447.6 3.5 collective-permute-start.58
  450.0 3.1 collective-permute-start.59
  450.5 14.1 %collective-permute-start.57 = (bf16[512,512]{1,0:T(8,128)(2,1)}, bf16[512,512]{1,0:T(8,128)(2,1)S(1)}, u32[]{:S(2)}, u32[]{:S(2)}) collective-permute-start(bf16[512,512]{1,0:T(8,128)(2,1)} %get-tuple-element.283), channel_id=1, source_target_pairs={{0,16},{16,0},{1,17},{17,1},{2,18},{18,2},{3,19},{19,3},{4,20},{20... | collective-permute-start | bytes 1572872 | tf_op jit(solution)/shard_map/ppermute | solution.py:45
  482.1 3.6 collective-permute-start.61
  482.1 14.3 %collective-permute-start.62 = (bf16[512,512]{1,0:T(8,128)(2,1)S(1)}, bf16[512,512]{1,0:T(8,128)(2,1)S(1)}, u32[]{:S(2)}, u32[]{:S(2)}) collective-permute-start(bf16[512,512]{1,0:T(8,128)(2,1)S(1)} %add_convert_fusion.5.left), channel_id=1, source_target_pairs={{0,8},{4,12},{8,0},{12,4},{1,9},{5,13},{9,1},{13,5},{2,10},{6,14},... | collective-permute-start | bytes 1572872 | tf_op jit(solution)/shard_map/ppermute | solution.py:50
  499.2 6.1 %collective-permute-start.63 = (bf16[512,512]{1,0:T(8,128)(2,1)}, bf16[512,512]{1,0:T(8,128)(2,1)S(1)}, u32[]{:S(2)}, u32[]{:S(2)}) collective-permute-start(bf16[512,512]{1,0:T(8,128)(2,1)} %add_turned.11.refs_0_), channel_id=1, source_target_pairs={{0,4},{4,0},{8,12},{12,8},{1,5},{5,1},{9,13},{13,9},{2,6},{6,2},{1... | collective-permute-start | bytes 1572872 | tf_op jit(solution)/shard_map/ppermute | solution.py:50
  (70 other events, 441.3 us)
Sparse Core Ops, SparseCore 0:
  60.7 81.9 all-gather.4
  165.7 77.0 reduce-scatter.2
  273.3 76.6 reduce-scatter.4
  351.5 81.2 all-gather.6
  434.2 83.6 all-gather.8

commit v4 on v3

--- a/solution.py
+++ b/solution.py
@@ -522,22 +522,27 @@
     hidden_out, pre_grad_out, sum_out, fed_out, back_out, fed, back = refs[ends[1] + onto :]
     tile = pl.program_id(0)
 
-    @pl.when(tile == 0)
-    def _():
-        if onto:
-            fed[...] = refs[ends[1]][...].astype(F32)
-            back[...] = refs[ends[1] + 1][...].astype(F32)
-        else:
-            fed[...] = jnp.zeros_like(fed)
-            back[...] = jnp.zeros_like(back)
-
     hidden, slope = gelu_pair(nn(normed[...], first) + bias[...])
     hidden_low = hidden.astype(BF16)
     pre_grad = (nt(grad[...], second) * slope).astype(BF16)
     hidden_out[...] = hidden_low
     pre_grad_out[...] = pre_grad
-    fed[...] += nn(hidden_low, second)
-    back[...] += nt(pre_grad, first)
+
+    @pl.when(tile == 0)
+    def _():
+        fed[...] = nn(hidden_low, second)
+        back[...] = nt(pre_grad, first)
+
+    @pl.when(tile > 0)
+    def _():
+        fed[...] += nn(hidden_low, second)
+        back[...] += nt(pre_grad, first)
+
+    if onto:
+        some = refs[ends[1]].shape[0]
+        at = pl.ds(pl.multiple_of(tile * some, some), some)
+        fed[at, :] += refs[ends[1]][...].astype(F32)
+        back[at, :] += refs[ends[1] + 1][...].astype(F32)
     sum_out[...] = jnp.sum(pre_grad.astype(F32), 0, keepdims=True)
 
     @pl.when(tile == pl.num_programs(0) - 1)
@@ -606,7 +611,7 @@
             in_specs=[whole, whole, pl.BlockSpec((1, tile), lambda t, k: (0, t + skip))]
             + first
             + second
-            + [whole] * len(sums),
+            + [pl.BlockSpec((rows // (units // tile), width), lambda t, k: (t, 0))] * len(sums),
             out_specs=[
                 unit_rows,
                 unit_rows,
@@ -976,6 +981,7 @@
         row = here[0]
     for i in range(1, halves):
         first, second = order.wait(first_near[i], second_near[i])
+        row = list(order.wait(*row))
         sums = feed_part(i, to_both([first]), to_both([second]), sums)
     first_sum = group(fed_parts[0])
     second_sum = group(fed_parts[1])
@@ -1031,7 +1037,8 @@
 
     if direct:
         back[0] = pass_on(*back[0])
-    first_sum.send()
+    first_sum.compute()
+    first_sum.sent = to_context(after(first_sum.sent, *back[0][1:]), 1)
     unturned = []
     norm_terms = ()
     heads_from = []

time: 541 us -> 538 us (level)
    unnamed x167 -> x165, local copies, waits for them, and re-layouts: 24.3 us -> 23.3 us
  transfers between devices with their start and end apart: 69 -> 69, of which waited for: 27 -> 25; matrix products, arithmetic and copies ran while one was open for 13% -> 13% of each run, Pallas kernels for 50% -> 50%
where the time goes in v4:
time: 538 us; the launch traced here: 529 us
  Pallas kernels  262 us (49%)
  waiting for transfers between devices  108 us (20%)
  local copies, waits for them, and re-layouts  61.3 us (11%)
  starting transfers between devices  50 us (9%)
  other arithmetic  27.5 us (5%)
  between operations  15.2 us (3%)
    ppermute x44, waiting for transfers between devices, to_context(): return lax.ppermute(value, 'context', [(i, i ^ mask) for i in range(size)])  73.3 us
    pallas_call x6, Pallas kernels, outer(): pl.pallas_call(functools.partial(outer_kernel, steps, int(adds)), out_sha...  66.3 us
    pallas_call x2, Pallas kernels, feed(): pl.pallas_call(functools.partial(feed_kernel, len(first), len(second), le...  60.1 us
    pallas_call x2, Pallas kernels, attend(): pl.pallas_call(functools.partial(attend_kernel, parts, bq, bk), out_shape...  41.7 us
    ppermute x14, waiting for transfers between devices, to_fsdp(): return lax.ppermute(value, 'fsdp', [(0, 1), (1, 0)])  25.5 us
    unnamed x165, local copies, waits for them, and re-layouts  23.3 us
    ppermute x44, starting transfers between devices, to_context(): return lax.ppermute(value, 'context', [(i, i ^ mask) for i in range(size)])  22.9 us
    pallas_call x4, Pallas kernels, finish(): pl.pallas_call(functools.partial(finish_kernel, half, turned, groups), ou...  21.9 us
  transfers between devices with their start and end apart: 69, of which 25 were waited for; matrix products, arithmetic and copies ran while one was open for 13% of the time, Pallas kernels for 50%

profile of v4, /device:TPU:0, one launch (start us, length us, event | category | flops | bytes accessed | tf_op | source)
XLA Modules:
  0.0 528.7 jit_solution(2176293390438399852)
XLA Ops:
  8.4 3.0 collective-permute-start.1
  15.6 1.9 constant_dynamic-slice_fusion.26
  17.5 1.9 constant_dynamic-slice_fusion.24
  19.4 2.4 constant_dynamic-slice_fusion.27
  21.7 2.3 constant_dynamic-slice_fusion.28
  29.3 1.8 collective-permute-start.5
  36.6 10.5 %prepare.1 = (bf16[1024,2048]{1,0:T(8,128)(2,1)}, bf16[1024,2048]{1,0:T(8,128)(2,1)}, f32[1,2048]{1,0:T(1,128)}) custom-call(s32[1]{0:T(128)} %bitcast.3.me_ref, bf16[1024,2048]{1,0:T(8,128)(2,1)} %bitcast.88, bf16[1024,2048]{1,0:T(8,128)(2,1)} %bitcast.90, f32[1,2048]{1,0:T(1,128)} %bitcast.113, f32[1,2048]{1,0:T(1,128)} %bitcast.114), custom_call_target="tpu_custom_call" | custom-call | bytes 34000000 | tf_op jit(solution)/shard_map/prepare/pallas_call | solution.py:159
  47.0 3.7 collective-permute-done.4.refs_11_.refs_5_
  52.2 7.1 %collective-permute-done.3.refs_15_ = bf16[1024,256]{1,0:T(8,128)(2,1)S(1)} collective-permute-done((bf16[1024,256]{1,0:T(8,128)(2,1)}, bf16[1024,256]{1,0:T(8,128)(2,1)S(1)}, u32[]{:S(2)}, u32[]{:S(2)}) %collective-permute-start.3) | collective-permute-done | bytes 524320 | tf_op jit(solution)/shard_map/ppermute | solution.py:45
  63.2 2.2 collective-permute-done.10.refs_21_
  70.4 19.5 %project.1 = (bf16[1,4,512,128]{3,2,1,0:T(8,128)(2,1)}, bf16[1,4,512,128]{3,2,1,0:T(8,128)(2,1)}, bf16[2,4,512,128]{3,2,1,0:T(8,128)(2,1)}, bf16[1,4,512,128]{3,...) custom-call(s32[1]{0:T(128)} %bitcast.2.k_ref, s32[1]{0:T(128)} %bitcast.1.c_ref.me_ref, ...), custom_call_target="tpu_custom_call" | custom-call | bytes 64600000 | tf_op jit(solution)/shard_map/project/pallas_call | solution.py:252
  97.4 28.5 %feed.2 = (bf16[1024,1024]{1,0:T(8,128)(2,1)}, bf16[1024,1024]{1,0:T(8,128)(2,1)}, f32[1,1024]{1,0:T(1,128)}, bf16[1024,2048]{1,0:T(8,128)(2,1)}, bf16[1024,2048]{1,0:T(8,128)(2,1)}) custom-call(s32[1]{0:T(128)} %bitcast.2.k_ref, bf16[1024,2048]{1,0:T(8,128)(2,1)} %get-tuple-element.194.refs_0_.refs_1_.refs_2_.refs_3_, ...), custom_call_target="tpu_custom_call" | custom-call | bytes 105400000 | tf_op jit(solution)/shard_map/feed/pallas_call | solution.py:599
  127.4 2.1 fusion.26
  134.4 31.6 %feed.3 = (bf16[1024,1024]{1,0:T(8,128)(2,1)}, bf16[1024,1024]{1,0:T(8,128)(2,1)}, f32[1,1024]{1,0:T(1,128)}, bf16[1024,2048]{1,0:T(8,128)(2,1)}, bf16[1024,2048]{1,0:T(8,128)(2,1)}) custom-call(s32[1]{0:T(128)} %bitcast.2.k_ref, bf16[1024,2048]{1,0:T(8,128)(2,1)} %get-tuple-element.194.refs_0_.refs_1_.refs_2_.refs_3_, ...), custom_call_target="tpu_custom_call" | custom-call | bytes 105400000 | tf_op jit(solution)/shard_map/feed/pallas_call | solution.py:599
  166.3 20.7 %attend.2 = (bf16[1,4,512,128]{3,2,1,0:T(8,128)(2,1)}, bf16[1,4,512,128]{3,2,1,0:T(8,128)(2,1)}, bf16[2,4,512,128]{3,2,1,0:T(8,128)(2,1)}) custom-call(s32[1]{0:T(128)} %bitcast.1.c_ref.me_ref, bf16[1,4,512,128]{3,2,1,0:T(8,128)(2,1)} %get-tuple-element.200.refs_0_, bf16[1,4,512,128]{3,2,1,0:T(8,128)(2,1)} %copy-done.37, ...), custom_call_target="tpu_custom_call" | custom-call | bytes 95200000 | tf_op jit(solution)/shard_map/attend/pallas_call | solution.py:380
  188.6 2.1 fusion.25
  193.5 21.0 %attend.3 = (bf16[1,4,512,128]{3,2,1,0:T(8,128)(2,1)}, bf16[1,4,512,128]{3,2,1,0:T(8,128)(2,1)}, bf16[2,4,512,128]{3,2,1,0:T(8,128)(2,1)}) custom-call(s32[1]{0:T(128)} %bitcast.1.c_ref.me_ref, bf16[1,4,512,128]{3,2,1,0:T(8,128)(2,1)} %get-tuple-element.208.refs_0_, bf16[1,4,512,128]{3,2,1,0:T(8,128)(2,1)} %copy-done.39, ...), custom_call_target="tpu_custom_call" | custom-call | bytes 95200000 | tf_op jit(solution)/shard_map/attend/pallas_call | solution.py:380
  216.2 10.4 %outer.6 = bf16[2,512,2048]{2,1,0:T(8,128)(2,1)} custom-call(bf16[1024,2048]{1,0:T(8,128)(2,1)} %get-tuple-element.194.refs_0_.refs_1_.refs_2_.refs_3_, bf16[1024,2048]{1,0:T(8,128)(2,1)} %get-tuple-element.194.refs_0_.refs_1_.refs_2_.refs_3_, bf16[1024,2048]{1,0:T(8,128)(2,1)} %get-tuple-element.166.refs_1_.refs_2_.refs_3_.refs_0_, ...), custom_call_target="tpu_custom_call" | custom-call | bytes 37400000 | tf_op jit(solution)/shard_map/outer/pallas_call | solution.py:693
  227.6 4.2 unturn.2
  231.8 9.5 %norm_back.2.refs_8_ = bf16[4,2,128,2048]{3,2,1,0:T(8,128)(2,1)} custom-call(s32[1]{0:T(128)} %bitcast.2.k_ref, bf16[1024,1536]{1,0:T(8,128)(2,1)} %get-tuple-element.221.raw.refs_8_, bf16[1024,2048]{1,0:T(8,128)(2,1)} %get-tuple-element.222.back, bf16[3,1024,512]{2,1,0:T(8,128)(2,1)} %refs_3_.7, bf16[3,1024,512]{2,1,0:T(8,128)(2,1)} %refs_3_.7, ...), custom_call_target="tpu_custom_call" | custom-call | bytes 27200000 | tf_op jit(solution)/shard_map/norm_back/pallas_call | solution.py:485
  244.4 2.5 collective-permute-start.31
  248.9 4.2 unturn.3
  254.4 3.2 collective-permute-start.37
  257.5 2.1 collective-permute-start.38
  259.6 9.2 %norm_back.3 = bf16[4,2,128,2048]{3,2,1,0:T(8,128)(2,1)} custom-call(s32[1]{0:T(128)} %bitcast.2.k_ref, bf16[1024,1536]{1,0:T(8,128)(2,1)} %get-tuple-element.229.raw.refs_5_, bf16[1024,2048]{1,0:T(8,128)(2,1)} %get-tuple-element.222.back, bf16[3,1024,512]{2,1,0:T(8,128)(2,1)} %refs_3_.7, ...), custom_call_target="tpu_custom_call", output_to_operand_aliasing={{}: (11, {})} | custom-call | bytes 27200000 | tf_op jit(solution)/shard_map/norm_back/pallas_call | solution.py:485
  270.6 11.7 %outer.7 = (bf16[512,1024]{1,0:T(8,128)(2,1)}, bf16[512,1024]{1,0:T(8,128)(2,1)}, bf16[512,1024]{1,0:T(8,128)(2,1)}, bf16[512,1024]{1,0:T(8,128)(2,1)}) custom-call(bf16[1024,2048]{1,0:T(8,128)(2,1)} %get-tuple-element.194.refs_0_.refs_1_.refs_2_.refs_3_, bf16[1024,2048]{1,0:T(8,128)(2,1)} %get-tuple-element.194.refs_0_.refs_1_.refs_2_.refs_3_, ...), custom_call_target="tpu_custom_call" | custom-call | bytes 37400000 | tf_op jit(solution)/shard_map/outer/pallas_call | solution.py:693
  288.8 10.4 %outer.8 = bf16[2,512,2048]{2,1,0:T(8,128)(2,1)} custom-call(bf16[1024,2048]{1,0:T(8,128)(2,1)} %get-tuple-element.194.refs_0_.refs_1_.refs_2_.refs_3_, bf16[1024,2048]{1,0:T(8,128)(2,1)} %get-tuple-element.194.refs_0_.refs_1_.refs_2_.refs_3_, bf16[1024,2048]{1,0:T(8,128)(2,1)} %get-tuple-element.166.refs_1_.refs_2_.refs_3_.refs_0_, ...), custom_call_target="tpu_custom_call" | custom-call | bytes 37400000 | tf_op jit(solution)/shard_map/outer/pallas_call | solution.py:693
  299.2 10.6 %outer.9 = bf16[2,512,2048]{2,1,0:T(8,128)(2,1)} custom-call(bf16[1024,2048]{1,0:T(8,128)(2,1)} %get-tuple-element.166.refs_1_.refs_2_.refs_3_.refs_0_, bf16[1024,2048]{1,0:T(8,128)(2,1)} %get-tuple-element.166.refs_1_.refs_2_.refs_3_.refs_0_, bf16[1024,2048]{1,0:T(8,128)(2,1)} %get-tuple-element.194.refs_0_.refs_1_.refs_2_.refs_3_, ...), custom_call_target="tpu_custom_call" | custom-call | bytes 37400000 | tf_op jit(solution)/shard_map/outer/pallas_call | solution.py:693
  310.2 1.8 add_convert_fusion.4.left
  316.6 3.5 fusion.30
  321.1 1.9 maximum_add_fusion
  323.7 2.6 fusion.14
  326.4 11.7 %outer.10 = (bf16[512,1024]{1,0:T(8,128)(2,1)}, bf16[512,1024]{1,0:T(8,128)(2,1)}, bf16[512,1024]{1,0:T(8,128)(2,1)}, bf16[512,1024]{1,0:T(8,128)(2,1)}) custom-call(bf16[1024,2048]{1,0:T(8,128)(2,1)} %get-tuple-element.194.refs_0_.refs_1_.refs_2_.refs_3_, bf16[1024,2048]{1,0:T(8,128)(2,1)} %get-tuple-element.194.refs_0_.refs_1_.refs_2_.refs_3_, ...), custom_call_target="tpu_custom_call" | custom-call | bytes 37400000 | tf_op jit(solution)/shard_map/outer/pallas_call | solution.py:693
  338.8 1.9 add_convert_fusion.3.left
  341.4 2.4 add_turned.6.refs_0_
  344.7 11.6 %outer.11 = (bf16[512,512]{1,0:T(8,128)(2,1)}, bf16[512,1536]{1,0:T(8,128)(2,1)}, bf16[512,512]{1,0:T(8,128)(2,1)}, bf16[512,1536]{1,0:T(8,128)(2,1)}) custom-call(bf16[1024,2048]{1,0:T(8,128)(2,1)} %get-tuple-element.166.refs_1_.refs_2_.refs_3_.refs_0_, bf16[1024,2048]{1,0:T(8,128)(2,1)} %get-tuple-element.166.refs_1_.refs_2_.refs_3_.refs_0_, ...), custom_call_target="tpu_custom_call" | custom-call | bytes 37400000 | tf_op jit(solution)/shard_map/outer/pallas_call | solution.py:693
  362.6 1.9 fusion.5
  364.6 3.5 collective-permute-done.46
  372.8 2.5 add_turned.7.refs_0_
  375.3 17.5 %collective-permute-done.49.right = bf16[512,1024]{1,0:T(8,128)(2,1)S(1)} collective-permute-done((bf16[512,1024]{1,0:T(8,128)(2,1)S(1)}, bf16[512,1024]{1,0:T(8,128)(2,1)S(1)}, u32[]{:S(2)}, u32[]{:S(2)}) %collective-permute-start.49) | collective-permute-done | bytes 1048608 | tf_op jit(solution)/shard_map/ppermute | solution.py:50
  394.5 1.8 collective-permute-start.51
  397.9 2.8 add_turned.8.refs_2_
  401.8 3.1 collective-permute-done.52
  405.0 2.5 maximum_maximum_fusion
  409.1 2.2 collective-permute-done.55.refs_1_
  412.3 6.3 %finish.4 = f32[1024,2048]{1,0:T(8,128)} custom-call(s32[1]{0:T(128)} %bitcast.2.k_ref, bf16[512,1024]{1,0:T(8,128)(2,1)} %add_turned.6.refs_0_, bf16[512,1024]{1,0:T(8,128)(2,1)} %copy-done.26, bf16[512,1024]{1,0:T(8,128)(2,1)} %add_turned.8.refs_2_, bf16[512,1024]{1,0:T(8,128)(2,1)} %collective-permute-done.56.refs_3_), custom_call_target="tpu_custom_call" | custom-call | bytes 20400000 | tf_op jit(solution)/shard_map/finish/pallas_call | solution.py:769
  418.6 15.0 %collective-permute-done.54.right = bf16[512,1024]{1,0:T(8,128)(2,1)} collective-permute-done((bf16[512,1024]{1,0:T(8,128)(2,1)S(1)}, bf16[512,1024]{1,0:T(8,128)(2,1)}, u32[]{:S(2)}, u32[]{:S(2)}) %collective-permute-start.54) | collective-permute-done | bytes 1048608 | tf_op jit(solution)/shard_map/ppermute | solution.py:50
  433.7 6.7 %collective-permute-done.53 = bf16[512,1536]{1,0:T(8,128)(2,1)} collective-permute-done((bf16[512,1536]{1,0:T(8,128)(2,1)}, bf16[512,1536]{1,0:T(8,128)(2,1)}, u32[]{:S(2)}, u32[]{:S(2)}) %collective-permute-start.53) | collective-permute-done | bytes 1572896 | tf_op jit(solution)/shard_map/ppermute | solution.py:45
  440.4 2.4 add_convert_fusion.left
  444.0 2.5 add_turned.9.refs_2_
  447.5 2.1 collective-permute-done.59.refs_3_
  449.6 6.5 %finish.5 = f32[2048,1024]{1,0:T(8,128)} custom-call(s32[1]{0:T(128)} %bitcast.2.k_ref, bf16[512,1024]{1,0:T(8,128)(2,1)} %add_turned.7.refs_0_, bf16[512,1024]{1,0:T(8,128)(2,1)} %collective-permute-done.58.refs_1_, bf16[512,1024]{1,0:T(8,128)(2,1)} %add_turned.9.refs_2_, bf16[512,1024]{1,0:T(8,128)(2,1)} %collective-permute-done.59.refs_3_), custom_call_target="tpu_custom_call" | custom-call | bytes 20400000 | tf_op jit(solution)/shard_map/finish/pallas_call | solution.py:769
  456.1 5.0 collective-permute-done.57
  461.2 13.5 %collective-permute-done.60.right = bf16[512,1536]{1,0:T(8,128)(2,1)} collective-permute-done((bf16[512,1536]{1,0:T(8,128)(2,1)S(1)}, bf16[512,1536]{1,0:T(8,128)(2,1)}, u32[]{:S(2)}, u32[]{:S(2)}) %collective-permute-start.60) | collective-permute-done | bytes 1572896 | tf_op jit(solution)/shard_map/ppermute | solution.py:50
  474.8 2.9 add_turned.10.refs_0_
  479.3 2.0 collective-permute-done.61.refs_1_
  482.5 5.3 %finish.6 = f32[3,1024,512]{2,1,0:T(8,128)} custom-call(s32[1]{0:T(128)} %bitcast.2.k_ref, bf16[512,1536]{1,0:T(8,128)(2,1)} %add_turned.10.refs_0_, bf16[512,1536]{1,0:T(8,128)(2,1)} %copy-done.19), custom_call_target="tpu_custom_call" | custom-call | bytes 20400000 | tf_op jit(solution)/shard_map/finish/pallas_call | solution.py:769
  487.8 4.3 collective-permute-done.62.right
  492.9 2.0 add_turned.11.refs_0_
  496.1 4.8 copy.35
  501.7 3.8 finish.7
  505.5 8.8 %all-gather.9.cloned.1.call-done = bf16[1088,2048]{1,0:T(8,128)(2,1)} async-done(((bf16[272,2048]{1,0:T(8,128)(2,1)}), bf16[1088,2048]{1,0:T(8,128)(2,1)}) %all-gather.9.cloned.1.call-update) | async-done | bytes 4456464 | tf_op jit(solution)/shard_map/all_gather | solution.py:1134
  514.4 2.5 slice.131
  517.8 2.3 copy.36
  (361 shorter events, 99.3 us)
Async XLA Ops:
  7.2 261.8 %all-gather.5.cloned.1.call-start = ((), (), s32[]{:S(2)}) async-start(), calls=%async_computation.2 | async-start | bytes 5242880 | tf_op jit(solution)/shard_map/all_gather | solution.py:895
  8.4 20.9 %collective-permute-start.1 = (bf16[3,256,512]{2,1,0:T(8,128)(2,1)S(1)}, bf16[3,256,512]{2,1,0:T(8,128)(2,1)S(1)}, u32[]{:S(2)}, u32[]{:S(2)}) collective-permute-start(bf16[3,256,512]{2,1,0:T(8,128)(2,1)S(1)} %constant_dynamic-slice_fusion.25), channel_id=1, source_target_pairs={{0,16},{16,0},{1,17},{17,1},{2,18},{18,2},{3,19},{19,3},{4,20},{20... | collective-permute-start | bytes 2359304 | tf_op jit(solution)/shard_map/ppermute | solution.py:45
  15.6 13.7 %collective-permute-start = (bf16[5888]{0:T(1024)(128)(2,1)S(1)}, bf16[5888]{0:T(1024)(128)(2,1)S(1)}, u32[]{:S(2)}, u32[]{:S(2)}) collective-permute-start(bf16[5888]{0:T(1024)(128)(2,1)S(1)} %constant_dynamic-update-slice_fusion.28), channel_id=1, source_target_pairs={{0,16},{16,0},{1,17},{17,1},{2,18},{18,2},{3,19},{19,3},{4,20},{20... | collective-permute-start | bytes 35336 | tf_op jit(solution)/shard_map/ppermute | solution.py:45
  29.3 17.7 %collective-permute-start.5 = (bf16[512,256]{1,0:T(8,128)(2,1)S(1)}, bf16[512,256]{1,0:T(8,128)(2,1)S(1)}, u32[]{:S(2)}, u32[]{:S(2)}) collective-permute-start(bf16[512,256]{1,0:T(8,128)(2,1)S(1)} %get-tuple-element.159), channel_id=1, source_target_pairs={{0,16},{16,0},{1,17},{17,1},{2,18},{18,2},{3,19},{19,3},{4,20},{20... | collective-permute-start | bytes 786440 | tf_op jit(solution)/shard_map/ppermute | solution.py:45
  31.1 21.1 %collective-permute-start.2 = (bf16[256,1024]{1,0:T(8,128)(2,1)}, bf16[256,1024]{1,0:T(8,128)(2,1)}, u32[]{:S(2)}, u32[]{:S(2)}) collective-permute-start(bf16[256,1024]{1,0:T(8,128)(2,1)} %constant_dynamic-slice_fusion.26), channel_id=1, source_target_pairs={{0,16},{16,0},{1,17},{17,1},{2,18},{18,2},{3,19},{19,3},{4,20},{20... | collective-permute-start | bytes 1572872 | tf_op jit(solution)/shard_map/ppermute | solution.py:45
  31.4 27.9 %collective-permute-start.3 = (bf16[1024,256]{1,0:T(8,128)(2,1)}, bf16[1024,256]{1,0:T(8,128)(2,1)S(1)}, u32[]{:S(2)}, u32[]{:S(2)}) collective-permute-start(bf16[1024,256]{1,0:T(8,128)(2,1)} %constant_dynamic-slice_fusion.24), channel_id=1, source_target_pairs={{0,16},{16,0},{1,17},{17,1},{2,18},{18,2},{3,19},{19,3},{4,20},{20... | collective-permute-start | bytes 1572872 | tf_op jit(solution)/shard_map/ppermute | solution.py:45
  33.2 17.6 %collective-permute-start.4 = (bf16[3,256,512]{2,1,0:T(8,128)(2,1)S(1)}, bf16[3,256,512]{2,1,0:T(8,128)(2,1)S(1)}, u32[]{:S(2)}, u32[]{:S(2)}) collective-permute-start(bf16[3,256,512]{2,1,0:T(8,128)(2,1)S(1)} %collective-permute-done.1.refs_10_.refs_4_), channel_id=1, source_target_pairs={{0,8},{4,12},{8,0},{12,4},{1,9},{5,13},{9,1},{13,5},{2,10},{6,14},... | collective-permute-start | bytes 2359304 | tf_op jit(solution)/shard_map/ppermute | solution.py:50
  50.8 8.6 %collective-permute-start.6 = (bf16[512,256]{1,0:T(8,128)(2,1)S(1)}, bf16[512,256]{1,0:T(8,128)(2,1)S(1)}, u32[]{:S(2)}, u32[]{:S(2)}) collective-permute-start(bf16[512,256]{1,0:T(8,128)(2,1)S(1)} %collective-permute-done.5.refs_18_), channel_id=1, source_target_pairs={{0,8},{4,12},{8,0},{12,4},{1,9},{5,13},{9,1},{13,5},{2,10},{6,14},... | collective-permute-start | bytes 786440 | tf_op jit(solution)/shard_map/ppermute | solution.py:50
  60.6 260.5 %reduce-scatter.3.cloned.1.call-start = ((), (), s32[]{:S(2)}) async-start(), calls=%async_computation.3 | async-start | bytes 5242880 | tf_op jit(solution)/shard_map/reduce_scatter | solution.py:990
  60.7 30.3 %collective-permute-start.14 = (bf16[512,1024]{1,0:T(8,128)(2,1)}, bf16[512,1024]{1,0:T(8,128)(2,1)}, u32[]{:S(2)}, u32[]{:S(2)}) collective-permute-start(bf16[512,1024]{1,0:T(8,128)(2,1)} %constant_dynamic-slice_fusion.28), channel_id=1, source_target_pairs={{0,16},{16,0},{1,17},{17,1},{2,18},{18,2},{3,19},{19,3},{4,20},{20... | collective-permute-start | bytes 3145736 | tf_op jit(solution)/shard_map/ppermute | solution.py:45
  62.2 7.0 %collective-permute-start.7 = (bf16[3,256,512]{2,1,0:T(8,128)(2,1)S(1)}, bf16[3,256,512]{2,1,0:T(8,128)(2,1)S(1)}, u32[]{:S(2)}, u32[]{:S(2)}) collective-permute-start(bf16[3,256,512]{2,1,0:T(8,128)(2,1)S(1)} %collective-permute-done.1.refs_10_.refs_4_), channel_id=1, source_target_pairs={{0,4},{4,0},{8,12},{12,8},{1,5},{5,1},{9,13},{13,9},{2,6},{6,2},{1... | collective-permute-start | bytes 2359304 | tf_op jit(solution)/shard_map/ppermute | solution.py:50
  62.2 7.0 %collective-permute-start.8 = (bf16[3,256,512]{2,1,0:T(8,128)(2,1)S(1)}, bf16[3,256,512]{2,1,0:T(8,128)(2,1)S(1)}, u32[]{:S(2)}, u32[]{:S(2)}) collective-permute-start(bf16[3,256,512]{2,1,0:T(8,128)(2,1)S(1)} %collective-permute-done.4.refs_11_.refs_5_), channel_id=1, source_target_pairs={{0,4},{4,0},{8,12},{12,8},{1,5},{5,1},{9,13},{13,9},{2,6},{6,2},{1... | collective-permute-start | bytes 2359304 | tf_op jit(solution)/shard_map/ppermute | solution.py:50
  62.7 2.7 collective-permute-start.10
  62.8 4.2 collective-permute-start.9
  65.4 24.5 %collective-permute-start.12 = (bf16[256,1024]{1,0:T(8,128)(2,1)}, bf16[256,1024]{1,0:T(8,128)(2,1)}, u32[]{:S(2)}, u32[]{:S(2)}) collective-permute-start(bf16[256,1024]{1,0:T(8,128)(2,1)} %collective-permute-done.2.refs_7_), channel_id=1, source_target_pairs={{0,8},{4,12},{8,0},{12,4},{1,9},{5,13},{9,1},{13,5},{2,10},{6,14},... | collective-permute-start | bytes 1572872 | tf_op jit(solution)/shard_map/ppermute | solution.py:50
  67.6 23.3 %collective-permute-start.13 = (bf16[1024,256]{1,0:T(8,128)(2,1)}, bf16[1024,256]{1,0:T(8,128)(2,1)}, u32[]{:S(2)}, u32[]{:S(2)}) collective-permute-start(bf16[1024,256]{1,0:T(8,128)(2,1)} %copy-done.29), channel_id=1, source_target_pairs={{0,8},{4,12},{8,0},{12,4},{1,9},{5,13},{9,1},{13,5},{2,10},{6,14},... | collective-permute-start | bytes 1572872 | tf_op jit(solution)/shard_map/ppermute | solution.py:50
  90.9 35.0 %collective-permute-start.11 = (bf16[2,4,512,128]{3,2,1,0:T(8,128)(2,1)}, bf16[2,4,512,128]{3,2,1,0:T(8,128)(2,1)S(1)}, u32[]{:S(2)}, u32[]{:S(2)}) collective-permute-start(bf16[2,4,512,128]{3,2,1,0:T(8,128)(2,1)} %get-tuple-element.175), channel_id=1, source_target_pairs={{0,8},{4,12},{8,0},{12,4},{1,9},{5,13},{9,1},{13,5},{2,10},{6,14},... | collective-permute-start | bytes 3145736 | tf_op jit(solution)/shard_map/ppermute | solution.py:50
  92.4 34.5 %collective-permute-start.21 = (bf16[1024,512]{1,0:T(8,128)(2,1)}, bf16[1024,512]{1,0:T(8,128)(2,1)S(1)}, u32[]{:S(2)}, u32[]{:S(2)}) collective-permute-start(bf16[1024,512]{1,0:T(8,128)(2,1)} %constant_dynamic-slice_fusion.27), channel_id=1, source_target_pairs={{0,16},{16,0},{1,17},{17,1},{2,18},{18,2},{3,19},{19,3},{4,20},{20... | collective-permute-start | bytes 3145736 | tf_op jit(solution)/shard_map/ppermute | solution.py:45
  92.9 3.6 collective-permute-start.17
  93.5 3.2 collective-permute-start.18
  126.9 5.7 %collective-permute-start.23 = (bf16[512,1024]{1,0:T(8,128)(2,1)}, bf16[512,1024]{1,0:T(8,128)(2,1)S(1)}, u32[]{:S(2)}, u32[]{:S(2)}) collective-permute-start(bf16[512,1024]{1,0:T(8,128)(2,1)} %collective-permute-done.14.refs_7_.refs_8_), channel_id=1, source_target_pairs={{0,4},{4,0},{8,12},{12,8},{1,5},{5,1},{9,13},{13,9},{2,6},{6,2},{1... | collective-permute-start | bytes 3145736 | tf_op jit(solution)/shard_map/ppermute | solution.py:50
  127.1 5.5 %collective-permute-start.24 = (bf16[1024,512]{1,0:T(8,128)(2,1)S(1)}, bf16[1024,512]{1,0:T(8,128)(2,1)S(1)}, u32[]{:S(2)}, u32[]{:S(2)}) collective-permute-start(bf16[1024,512]{1,0:T(8,128)(2,1)S(1)} %collective-permute-done.21.refs_15_.refs_16_), channel_id=1, source_target_pairs={{0,4},{4,0},{8,12},{12,8},{1,5},{5,1},{9,13},{13,9},{2,6},{6,2},{1... | collective-permute-start | bytes 3145736 | tf_op jit(solution)/shard_map/ppermute | solution.py:50
  127.4 38.6 %collective-permute-start.22 = (bf16[2,4,512,128]{3,2,1,0:T(8,128)(2,1)}, bf16[2,4,512,128]{3,2,1,0:T(8,128)(2,1)}, u32[]{:S(2)}, u32[]{:S(2)}) collective-permute-start(bf16[2,4,512,128]{3,2,1,0:T(8,128)(2,1)} %get-tuple-element.193), channel_id=1, source_target_pairs={{0,8},{4,12},{8,0},{12,4},{1,9},{5,13},{9,1},{13,5},{2,10},{6,14},... | collective-permute-start | bytes 3145736 | tf_op jit(solution)/shard_map/ppermute | solution.py:50
  129.7 2.9 collective-permute-start.19
  166.0 190.3 %reduce-scatter.5.cloned.1.call-start = ((), (), s32[]{:S(2)}) async-start(), calls=%async_computation.5 | async-start | bytes 5242880 | tf_op jit(solution)/shard_map/reduce_scatter | solution.py:1057
  186.9 27.9 %collective-permute-start.25 = (bf16[2,4,512,128]{3,2,1,0:T(8,128)(2,1)}, bf16[2,4,512,128]{3,2,1,0:T(8,128)(2,1)S(1)}, u32[]{:S(2)}, u32[]{:S(2)}) collective-permute-start(bf16[2,4,512,128]{3,2,1,0:T(8,128)(2,1)} %get-tuple-element.206), channel_id=1, source_target_pairs={{0,8},{4,12},{8,0},{12,4},{1,9},{5,13},{9,1},{13,5},{2,10},{6,14},... | collective-permute-start | bytes 3145736 | tf_op jit(solution)/shard_map/ppermute | solution.py:50
  188.6 2.6 collective-permute-start.26
  214.5 26.8 %collective-permute-start.33 = (bf16[2,4,512,128]{3,2,1,0:T(8,128)(2,1)}, bf16[2,4,512,128]{3,2,1,0:T(8,128)(2,1)S(1)}, u32[]{:S(2)}, u32[]{:S(2)}) collective-permute-start(bf16[2,4,512,128]{3,2,1,0:T(8,128)(2,1)} %get-tuple-element.219), channel_id=1, source_target_pairs={{0,8},{4,12},{8,0},{12,4},{1,9},{5,13},{9,1},{13,5},{2,10},{6,14},... | collective-permute-start | bytes 3145736 | tf_op jit(solution)/shard_map/ppermute | solution.py:50
  215.7 10.9 %collective-permute-start.28 = (bf16[1,4,512,128]{3,2,1,0:T(8,128)(2,1)S(1)}, bf16[1,4,512,128]{3,2,1,0:T(8,128)(2,1)S(1)}, u32[]{:S(2)}, u32[]{:S(2)}) collective-permute-start(bf16[1,4,512,128]{3,2,1,0:T(8,128)(2,1)S(1)} %copy-done.63), channel_id=1, source_target_pairs={{0,4},{4,0},{8,12},{12,8},{1,5},{5,1},{9,13},{13,9},{2,6},{6,2},{1... | collective-permute-start | bytes 1572872 | tf_op jit(solution)/shard_map/ppermute | solution.py:50
  215.9 10.8 %collective-permute-start.29 = (bf16[1,4,512,128]{3,2,1,0:T(8,128)(2,1)S(1)}, bf16[1,4,512,128]{3,2,1,0:T(8,128)(2,1)S(1)}, u32[]{:S(2)}, u32[]{:S(2)}) collective-permute-start(bf16[1,4,512,128]{3,2,1,0:T(8,128)(2,1)S(1)} %get-tuple-element.338), channel_id=1, source_target_pairs={{0,4},{4,0},{8,12},{12,8},{1,5},{5,1},{9,13},{13,9},{2,6},{6,2},{1... | collective-permute-start | bytes 1572872 | tf_op jit(solution)/shard_map/ppermute | solution.py:50
  226.7 43.9 %collective-permute-start.39 = (bf16[2,512,2048]{2,1,0:T(8,128)(2,1)}, bf16[2,512,2048]{2,1,0:T(8,128)(2,1)}, u32[]{:S(2)}, u32[]{:S(2)}) collective-permute-start(bf16[2,512,2048]{2,1,0:T(8,128)(2,1)} %outer.6), channel_id=1, source_target_pairs={{0,4},{4,0},{8,12},{12,8},{1,5},{5,1},{9,13},{13,9},{2,6},{6,2},{1... | collective-permute-start | bytes 12582920 | tf_op jit(solution)/shard_map/ppermute | solution.py:50
  242.2 4.7 collective-permute-start.35
  242.3 5.8 %collective-permute-start.34 = (bf16[1,4,512,128]{3,2,1,0:T(8,128)(2,1)}, bf16[1,4,512,128]{3,2,1,0:T(8,128)(2,1)S(1)}, u32[]{:S(2)}, u32[]{:S(2)}) collective-permute-start(bf16[1,4,512,128]{3,2,1,0:T(8,128)(2,1)} %get-tuple-element.226), channel_id=1, source_target_pairs={{0,4},{4,0},{8,12},{12,8},{1,5},{5,1},{9,13},{13,9},{2,6},{6,2},{1... | collective-permute-start | bytes 1572872 | tf_op jit(solution)/shard_map/ppermute | solution.py:50
  242.7 11.6 %collective-permute-start.30 = (bf16[128,512]{1,0:T(8,128)(2,1)S(1)}, bf16[128,512]{1,0:T(8,128)(2,1)S(1)}, u32[]{:S(2)}, u32[]{:S(2)}) collective-permute-start(bf16[128,512]{1,0:T(8,128)(2,1)S(1)} %get-tuple-element.336), channel_id=1, source_target_pairs={{0,1},{1,0},{2,3},{3,2},{4,5},{5,4},{6,7},{7,6},{8,9},{9,8},{10,11... | collective-permute-start | bytes 393224 | tf_op jit(solution)/shard_map/ppermute | solution.py:55
  244.4 13.2 %collective-permute-start.31 = (bf16[128,512]{1,0:T(8,128)(2,1)S(1)}, bf16[128,512]{1,0:T(8,128)(2,1)S(1)}, u32[]{:S(2)}, u32[]{:S(2)}) collective-permute-start(bf16[128,512]{1,0:T(8,128)(2,1)S(1)} %get-tuple-element.335), channel_id=1, source_target_pairs={{0,2},{1,3},{2,0},{3,1},{4,6},{5,7},{6,4},{7,5},{8,10},{9,11},{10,... | collective-permute-start | bytes 393224 | tf_op jit(solution)/shard_map/ppermute | solution.py:55
  246.9 21.9 %collective-permute-start.32 = (bf16[128,512]{1,0:T(8,128)(2,1)S(1)}, bf16[128,512]{1,0:T(8,128)(2,1)S(1)}, u32[]{:S(2)}, u32[]{:S(2)}) collective-permute-start(bf16[128,512]{1,0:T(8,128)(2,1)S(1)} %get-tuple-element.334), channel_id=1, source_target_pairs={{0,3},{1,2},{2,1},{3,0},{4,7},{5,6},{6,5},{7,4},{8,11},{9,10},{10,... | collective-permute-start | bytes 393224 | tf_op jit(solution)/shard_map/ppermute | solution.py:55
  254.3 14.6 %collective-permute-start.36 = (bf16[128,512]{1,0:T(8,128)(2,1)S(1)}, bf16[128,512]{1,0:T(8,128)(2,1)S(1)}, u32[]{:S(2)}, u32[]{:S(2)}) collective-permute-start(bf16[128,512]{1,0:T(8,128)(2,1)S(1)} %get-tuple-element.331), channel_id=1, source_target_pairs={{0,1},{1,0},{2,3},{3,2},{4,5},{5,4},{6,7},{7,6},{8,9},{9,8},{10,11... | collective-permute-start | bytes 393224 | tf_op jit(solution)/shard_map/ppermute | solution.py:55
  254.4 14.5 %collective-permute-start.37 = (bf16[128,512]{1,0:T(8,128)(2,1)S(1)}, bf16[128,512]{1,0:T(8,128)(2,1)S(1)}, u32[]{:S(2)}, u32[]{:S(2)}) collective-permute-start(bf16[128,512]{1,0:T(8,128)(2,1)S(1)} %get-tuple-element.330), channel_id=1, source_target_pairs={{0,2},{1,3},{2,0},{3,1},{4,6},{5,7},{6,4},{7,5},{8,10},{9,11},{10,... | collective-permute-start | bytes 393224 | tf_op jit(solution)/shard_map/ppermute | solution.py:55
  257.5 11.3 %collective-permute-start.38 = (bf16[128,512]{1,0:T(8,128)(2,1)S(1)}, bf16[128,512]{1,0:T(8,128)(2,1)}, u32[]{:S(2)}, u32[]{:S(2)}) collective-permute-start(bf16[128,512]{1,0:T(8,128)(2,1)S(1)} %get-tuple-element.329), channel_id=1, source_target_pairs={{0,3},{1,2},{2,1},{3,0},{4,7},{5,6},{6,5},{7,4},{8,11},{9,10},{10,... | collective-permute-start | bytes 393224 | tf_op jit(solution)/shard_map/ppermute | solution.py:55
  268.9 227.2 %all-gather.7.cloned.1.call-start = ((), (), s32[]{:S(2)}) async-start(), calls=%async_computation.4 | async-start | bytes 5242880 | tf_op jit(solution)/shard_map/all_gather | solution.py:1091
  269.0 47.6 %collective-permute-start.41 = (bf16[2048,1024]{1,0:T(8,128)(2,1)}, bf16[2048,1024]{1,0:T(8,128)(2,1)}, u32[]{:S(2)}, u32[]{:S(2)}) collective-permute-start(bf16[2048,1024]{1,0:T(8,128)(2,1)} %all-gather.5.cloned.1.call-done), channel_id=1, source_target_pairs={{0,4},{4,0},{8,12},{12,8},{1,5},{5,1},{9,13},{13,9},{2,6},{6,2},{1... | collective-permute-start | bytes 12582920 | tf_op jit(solution)/shard_map/ppermute | solution.py:50
  282.3 27.9 %collective-permute-start.40 = (bf16[512,1024]{1,0:T(8,128)(2,1)}, bf16[512,1024]{1,0:T(8,128)(2,1)}, u32[]{:S(2)}, u32[]{:S(2)}) collective-permute-start(bf16[512,1024]{1,0:T(8,128)(2,1)} %get-tuple-element.234), channel_id=1, source_target_pairs={{0,16},{16,0},{1,17},{17,1},{2,18},{18,2},{3,19},{19,3},{4,20},{20... | collective-permute-start | bytes 3145736 | tf_op jit(solution)/shard_map/ppermute | solution.py:45
  299.2 27.2 %collective-permute-start.44 = (bf16[2,512,2048]{2,1,0:T(8,128)(2,1)}, bf16[2,512,2048]{2,1,0:T(8,128)(2,1)}, u32[]{:S(2)}, u32[]{:S(2)}) collective-permute-start(bf16[2,512,2048]{2,1,0:T(8,128)(2,1)} %outer.8), channel_id=1, source_target_pairs={{0,4},{4,0},{8,12},{12,8},{1,5},{5,1},{9,13},{13,9},{2,6},{6,2},{1... | collective-permute-start | bytes 12582920 | tf_op jit(solution)/shard_map/ppermute | solution.py:50
  309.8 34.9 %collective-permute-start.45 = (bf16[2,512,2048]{2,1,0:T(8,128)(2,1)}, bf16[2,512,2048]{2,1,0:T(8,128)(2,1)}, u32[]{:S(2)}, u32[]{:S(2)}) collective-permute-start(bf16[2,512,2048]{2,1,0:T(8,128)(2,1)} %outer.9), channel_id=1, source_target_pairs={{0,4},{4,0},{8,12},{12,8},{1,5},{5,1},{9,13},{13,9},{2,6},{6,2},{1... | collective-permute-start | bytes 12582920 | tf_op jit(solution)/shard_map/ppermute | solution.py:50
  312.0 26.8 %collective-permute-start.43 = (bf16[512,1024]{1,0:T(8,128)(2,1)S(1)}, bf16[512,1024]{1,0:T(8,128)(2,1)}, u32[]{:S(2)}, u32[]{:S(2)}) collective-permute-start(bf16[512,1024]{1,0:T(8,128)(2,1)S(1)} %add_convert_fusion.4.left), channel_id=1, source_target_pairs={{0,8},{4,12},{8,0},{12,4},{1,9},{5,13},{9,1},{13,5},{2,10},{6,14},... | collective-permute-start | bytes 3145736 | tf_op jit(solution)/shard_map/ppermute | solution.py:50
  313.6 25.2 %collective-permute-start.42 = (bf16[512,1024]{1,0:T(8,128)(2,1)}, bf16[512,1024]{1,0:T(8,128)(2,1)}, u32[]{:S(2)}, u32[]{:S(2)}) collective-permute-start(bf16[512,1024]{1,0:T(8,128)(2,1)} %get-tuple-element.259), channel_id=1, source_target_pairs={{0,16},{16,0},{1,17},{17,1},{2,18},{18,2},{3,19},{19,3},{4,20},{20... | collective-permute-start | bytes 3145736 | tf_op jit(solution)/shard_map/ppermute | solution.py:45
  326.3 188.1 %all-gather.9.cloned.1.call-start = ((), (), s32[]{:S(2)}) async-start(), calls=%async_computation.6 | async-start | bytes 5570560 | tf_op jit(solution)/shard_map/all_gather | solution.py:1134
  340.8 27.3 %collective-permute-start.47 = (bf16[512,1024]{1,0:T(8,128)(2,1)S(1)}, bf16[512,1024]{1,0:T(8,128)(2,1)}, u32[]{:S(2)}, u32[]{:S(2)}) collective-permute-start(bf16[512,1024]{1,0:T(8,128)(2,1)S(1)} %add_convert_fusion.3.left), channel_id=1, source_target_pairs={{0,8},{4,12},{8,0},{12,4},{1,9},{5,13},{9,1},{13,5},{2,10},{6,14},... | collective-permute-start | bytes 3145736 | tf_op jit(solution)/shard_map/ppermute | solution.py:50
  343.8 24.3 %collective-permute-start.46 = (bf16[512,1024]{1,0:T(8,128)(2,1)}, bf16[512,1024]{1,0:T(8,128)(2,1)}, u32[]{:S(2)}, u32[]{:S(2)}) collective-permute-start(bf16[512,1024]{1,0:T(8,128)(2,1)} %get-tuple-element.273), channel_id=1, source_target_pairs={{0,16},{16,0},{1,17},{17,1},{2,18},{18,2},{3,19},{19,3},{4,20},{20... | collective-permute-start | bytes 3145736 | tf_op jit(solution)/shard_map/ppermute | solution.py:45
  369.7 23.1 %collective-permute-start.49 = (bf16[512,1024]{1,0:T(8,128)(2,1)S(1)}, bf16[512,1024]{1,0:T(8,128)(2,1)S(1)}, u32[]{:S(2)}, u32[]{:S(2)}) collective-permute-start(bf16[512,1024]{1,0:T(8,128)(2,1)S(1)} %add_convert_fusion.2.left), channel_id=1, source_target_pairs={{0,8},{4,12},{8,0},{12,4},{1,9},{5,13},{9,1},{13,5},{2,10},{6,14},... | collective-permute-start | bytes 3145736 | tf_op jit(solution)/shard_map/ppermute | solution.py:50
  371.2 23.2 %collective-permute-start.48 = (bf16[512,1024]{1,0:T(8,128)(2,1)}, bf16[512,1024]{1,0:T(8,128)(2,1)}, u32[]{:S(2)}, u32[]{:S(2)}) collective-permute-start(bf16[512,1024]{1,0:T(8,128)(2,1)} %get-tuple-element.275), channel_id=1, source_target_pairs={{0,16},{16,0},{1,17},{17,1},{2,18},{18,2},{3,19},{19,3},{4,20},{20... | collective-permute-start | bytes 3145736 | tf_op jit(solution)/shard_map/ppermute | solution.py:45
  394.5 6.3 %collective-permute-start.51 = (f32[1,9728]{1,0:T(1,128)S(1)}, f32[1,9728]{1,0:T(1,128)S(1)}, u32[]{:S(2)}, u32[]{:S(2)}) collective-permute-start(f32[1,9728]{1,0:T(1,128)S(1)} %add.259), channel_id=1, source_target_pairs={{0,16},{16,0},{1,17},{17,1},{2,18},{18,2},{3,19},{19,3},{4,20},{20... | collective-permute-start | bytes 116744 | tf_op jit(solution)/shard_map/ppermute | solution.py:45
  400.8 4.0 collective-permute-start.52
  407.5 32.8 %collective-permute-start.53 = (bf16[512,1536]{1,0:T(8,128)(2,1)}, bf16[512,1536]{1,0:T(8,128)(2,1)}, u32[]{:S(2)}, u32[]{:S(2)}) collective-permute-start(bf16[512,1536]{1,0:T(8,128)(2,1)} %get-tuple-element.289), channel_id=1, source_target_pairs={{0,16},{16,0},{1,17},{17,1},{2,18},{18,2},{3,19},{19,3},{4,20},{20... | collective-permute-start | bytes 4718600 | tf_op jit(solution)/shard_map/ppermute | solution.py:45
  407.9 3.4 collective-permute-start.55
  407.9 4.4 collective-permute-start.56
  408.4 25.2 %collective-permute-start.54 = (bf16[512,1024]{1,0:T(8,128)(2,1)S(1)}, bf16[512,1024]{1,0:T(8,128)(2,1)}, u32[]{:S(2)}, u32[]{:S(2)}) collective-permute-start(bf16[512,1024]{1,0:T(8,128)(2,1)S(1)} %add_convert_fusion.1.left), channel_id=1, source_target_pairs={{0,8},{4,12},{8,0},{12,4},{1,9},{5,13},{9,1},{13,5},{2,10},{6,14},... | collective-permute-start | bytes 3145736 | tf_op jit(solution)/shard_map/ppermute | solution.py:50
  442.8 32.0 %collective-permute-start.60 = (bf16[512,1536]{1,0:T(8,128)(2,1)S(1)}, bf16[512,1536]{1,0:T(8,128)(2,1)}, u32[]{:S(2)}, u32[]{:S(2)}) collective-permute-start(bf16[512,1536]{1,0:T(8,128)(2,1)S(1)} %add_convert_fusion.left), channel_id=1, source_target_pairs={{0,8},{4,12},{8,0},{12,4},{1,9},{5,13},{9,1},{13,5},{2,10},{6,14},... | collective-permute-start | bytes 4718600 | tf_op jit(solution)/shard_map/ppermute | solution.py:50
  444.0 3.5 collective-permute-start.58
  446.5 3.1 collective-permute-start.59
  447.0 14.1 %collective-permute-start.57 = (bf16[512,512]{1,0:T(8,128)(2,1)}, bf16[512,512]{1,0:T(8,128)(2,1)S(1)}, u32[]{:S(2)}, u32[]{:S(2)}) collective-permute-start(bf16[512,512]{1,0:T(8,128)(2,1)} %get-tuple-element.293), channel_id=1, source_target_pairs={{0,16},{16,0},{1,17},{17,1},{2,18},{18,2},{3,19},{19,3},{4,20},{20... | collective-permute-start | bytes 1572872 | tf_op jit(solution)/shard_map/ppermute | solution.py:45
  477.7 3.6 collective-permute-start.61
  477.7 14.3 %collective-permute-start.62 = (bf16[512,512]{1,0:T(8,128)(2,1)S(1)}, bf16[512,512]{1,0:T(8,128)(2,1)S(1)}, u32[]{:S(2)}, u32[]{:S(2)}) collective-permute-start(bf16[512,512]{1,0:T(8,128)(2,1)S(1)} %add_convert_fusion.5.left), channel_id=1, source_target_pairs={{0,8},{4,12},{8,0},{12,4},{1,9},{5,13},{9,1},{13,5},{2,10},{6,14},... | collective-permute-start | bytes 1572872 | tf_op jit(solution)/shard_map/ppermute | solution.py:50
  494.8 6.1 %collective-permute-start.63 = (bf16[512,512]{1,0:T(8,128)(2,1)}, bf16[512,512]{1,0:T(8,128)(2,1)S(1)}, u32[]{:S(2)}, u32[]{:S(2)}) collective-permute-start(bf16[512,512]{1,0:T(8,128)(2,1)} %add_turned.11.refs_0_), channel_id=1, source_target_pairs={{0,4},{4,0},{8,12},{12,8},{1,5},{5,1},{9,13},{13,9},{2,6},{6,2},{1... | collective-permute-start | bytes 1572872 | tf_op jit(solution)/shard_map/ppermute | solution.py:50
  (69 other events, 477.6 us)
Sparse Core Ops, SparseCore 0:
  60.7 81.9 all-gather.4
  166.2 78.1 reduce-scatter.2
  269.0 77.5 reduce-scatter.4
  348.0 81.2 all-gather.6
  430.7 83.6 all-gather.8
